TPU v7x, 32 devices: a whole 2x2x4 slice. The times are simulated.
32 devices in a mesh: dp: 4 (over z), mp: 8 (over y, x, core).
Axes of the slice: x: 2, y: 2, z: 4, core: 2. Of those that a mesh axis runs over, the one named last changes fastest.
Arguments:
- src_ids: int32 [32, 768], P('dp'), may hold values from 0 to 32127
- targets: int32 [32, 256], P('dp'), may hold values from 0 to 32127
- loss_pos: int32 [32, 128], P('dp'), may hold values from 0 to 255, as said below
- loss_mask: int32 [32, 128], P('dp'), may hold values from 0 to 1
- routes_src: int32 [32, 768], replicated, may hold values from 0 to 3, as said below
- routes_tgt: int32 [32, 256], replicated, may hold values from 0 to 3, as said below
- dense_w: float32 [12, 589824], P(None, 'mp'), may hold values from -1.1547005 to 1.1547005
- dense_m: float32 [12, 589824], P(None, 'mp'), may hold values from -0.0017089844 to 0.0017089844
- expert_w: float32 [2, 2, 4, 768, 3072], P(None, None, 'dp', None, 'mp'), may hold values from -0.6350853 to 0.6350853
- expert_m: float32 [2, 2, 4, 768, 3072], P(None, None, 'dp', None, 'mp'), may hold values from -0.0017089844 to 0.0017089844
- table_w: float32 [32128, 768], P('mp'), may hold values from -12 to 12
- table_m: float32 [32128, 768], P(('mp', 'dp')), may hold values from -0.00018310547 to 0.00018310547
- table_v: float32 [32128, 768], P(('mp', 'dp')), may hold values from 7.1941486e-10 to 2.8776594e-09
- gains_w: float32 [7, 768], replicated, may hold values from 0.25 to 2.25
- gains_m: float32 [7, 768], P(None, 'mp'), may hold values from -0.0009765625 to 0.0009765625
- gains_v: float32 [7, 768], P(None, 'mp'), may hold values from 1.7985371e-08 to 7.1941486e-08
- router_w: float32 [2, 768, 4], replicated, may hold values from -0.375 to 0.375
- router_m: float32 [2, 768, 4], P(None, 'mp'), may hold values from -0.0009765625 to 0.0009765625
- router_v: float32 [2, 768, 4], P(None, 'mp'), may hold values from 1.7985371e-08 to 7.1941486e-08
- bias_w: float32 [2, 32, 12], replicated, may hold values from -4 to 4
- bias_m: float32 [2, 32, 12], P(None, 'mp'), may hold values from -0.0009765625 to 0.0009765625
- bias_v: float32 [2, 32, 12], P(None, 'mp'), may hold values from 1.7985371e-08 to 7.1941486e-08
Outputs:
- loss: float32 [2], replicated
- grad_norm: float32 [], replicated
- dense_new: float32 [12, 589824], P(None, 'mp')
- dense_moment: float32 [12, 589824], P(None, 'mp')
- dense_low: bfloat16 [12, 589824], P(None, 'mp')
- expert_new: float32 [2, 2, 4, 768, 3072], P(None, None, 'dp', None, 'mp')
- expert_moment: float32 [2, 2, 4, 768, 3072], P(None, None, 'dp', None, 'mp')
- expert_low: bfloat16 [2, 2, 4, 768, 3072], P(None, None, 'dp', None, 'mp')
- table_new: float32 [32128, 768], P(('mp', 'dp'))
- table_clipped: float32 [32128, 768], P(('mp', 'dp'))
- table_second: float32 [32128, 768], P(('mp', 'dp'))
- gains_new: float32 [7, 768], P(None, 'mp')
- gains_first: float32 [7, 768], P(None, 'mp')
- gains_second: float32 [7, 768], P(None, 'mp')
- router_new: float32 [2, 768, 4], P(None, 'mp')
- router_first: float32 [2, 768, 4], P(None, 'mp')
- router_second: float32 [2, 768, 4], P(None, 'mp')
- bias_new: float32 [2, 32, 12], P(None, 'mp')
- bias_first: float32 [2, 32, 12], P(None, 'mp')
- bias_second: float32 [2, 32, 12], P(None, 'mp')
Inputs may be any that keep to these rules, and one draw needn't show every extreme that they name: `routes_src`: in each device's block of 768 rows no expert is named by more than 240 rows, and some expert by exactly 240. `routes_tgt`: in each device's block of 256 rows no expert is named by more than 80 rows, and some expert by exactly 80. `loss_pos`: the 128 positions of a sequence are distinct.
All inputs are finite; a program needn't handle non-finite values.
Results may differ from a plain program's by a relative error of at most 0.025.
Values may be sent and summed in bfloat16 or wider, within the bound.
A program may use at most 512 MiB of HBM per device.

v0:
```python
from functools import partial
import math

import jax
import jax.numpy as jnp
from jax import lax
from jax.sharding import PartitionSpec as P

D = 768
HEADS = 12
HD = 64
FF = 3072
NS_ITERS = 5
STEP = 10


eps_norm = 1e-06
eps_gram = 1e-07
eps_adam = 1e-08
neg_fill = -1000000000.0
coef_a = 3.4445
coef_b = -4.775
coef_c = 2.0315
beta_one = 0.9
beta_two = 0.95
rate_matrix = 0.2
decay_matrix = 0.01
aux_weight = 0.01
enc_edges = (12, 16, 23, 32, 46, 64, 91)
dec_edges = (19, 21, 24, 27, 31, 35, 40, 46, 52, 59, 67, 77, 87, 99, 113)
highest = lax.Precision.HIGHEST


def merged(part, axis, combine):
    gathered = jax.tree.map(lambda a: lax.all_gather(a, axis), part)

    def take(source):
        return jax.tree.map(lambda a: lax.dynamic_index_in_dim(a, source, 0, False), gathered)

    return lax.fori_loop(
        1, lax.axis_size(axis), lambda source, state: combine(state, take(source)), take(0)
    )


def normalize(rows, gain):
    inverse = lax.rsqrt(jnp.mean(rows * rows, axis=-1, keepdims=True) + eps_norm)
    return (rows * inverse * gain, inverse)


def normalize_back(rows, inverse, gain, grad):
    scaled = grad * gain
    d_rows = inverse * scaled - rows * inverse**3 * jnp.mean(scaled * rows, axis=-1, keepdims=True)
    return (d_rows, jnp.sum(grad * rows * inverse, axis=0))


def bucket_of(relative, causal):
    if causal:
        distance = jnp.maximum(-relative, 0)
        far = 16 + sum(((distance >= edge).astype(jnp.int32) for edge in dec_edges))
        return jnp.where(distance < 16, distance, far)
    distance = jnp.abs(relative)
    far = 8 + sum(((distance >= edge).astype(jnp.int32) for edge in enc_edges))
    return jnp.where(distance < 8, distance, far) + 16 * (relative > 0).astype(jnp.int32)


def offset_hot(length, count, causal):
    place = jnp.arange(2 * length, dtype=jnp.int32)
    offset = jnp.where(place < length, place, place - 2 * length)
    return (
        bucket_of(offset, causal)[:, None] == jnp.arange(count, dtype=jnp.int32)[None, :]
    ).astype(jnp.float32)


def offset_bias(table, length, causal):
    hot = offset_hot(length, table.shape[0], causal)
    per_offset = jnp.dot(hot, table, precision=highest)
    tiled = jnp.tile(per_offset.T, (1, length))
    skewed = tiled[:, : length * (2 * length - 1)].reshape(-1, length, 2 * length - 1)
    return (skewed[:, :, :length], hot)


def offset_sums(d_scores, hot):
    length = d_scores.shape[-1]
    summed = jnp.sum(d_scores, axis=0, dtype=jnp.float32)
    padded = jnp.pad(summed, ((0, 0), (0, 0), (0, length - 1))).reshape(summed.shape[0], -1)
    padded = jnp.pad(padded, ((0, 0), (0, length))).reshape(summed.shape[0], length, 2 * length)
    per_offset = jnp.sum(padded, axis=1)
    return jnp.dot(hot.T, per_offset.T, precision=highest)


def split_heads(rows, nseq):
    return rows.reshape(nseq, -1, HEADS, HD)


def attn_scores(queries, keys, table, causal):
    len_q, len_k = (queries.shape[1], keys.shape[1])
    scores = jnp.einsum(
        "sqhd,skhd->shqk", queries, keys, preferred_element_type=jnp.float32
    ) * HD ** (-0.5)
    hot = None
    if table is not None:
        bias, hot = offset_bias(table, len_q, causal)
        scores = scores + bias[None]
    if causal:
        allowed = lax.broadcasted_iota(jnp.int32, (len_q, len_k), 1) <= lax.broadcasted_iota(
            jnp.int32, (len_q, len_k), 0
        )
        scores = jnp.where(allowed, scores, neg_fill)
    return (scores, hot)


def attend(normed, context, weights, table, causal, nseq):
    queries = jnp.dot(normed, weights[0], preferred_element_type=jnp.float32).astype(jnp.bfloat16)
    keys = jnp.dot(context, weights[1], preferred_element_type=jnp.float32).astype(jnp.bfloat16)
    values = jnp.dot(context, weights[2], preferred_element_type=jnp.float32).astype(jnp.bfloat16)
    scores, unused = attn_scores(split_heads(queries, nseq), split_heads(keys, nseq), table, causal)
    top = jnp.max(scores, axis=-1, keepdims=True)
    expo = jnp.exp(scores - top)
    total = jnp.sum(expo, axis=-1, keepdims=True)
    probs = (expo / total).astype(jnp.bfloat16)
    mixed = jnp.einsum(
        "shqk,skhd->sqhd", probs, split_heads(values, nseq), preferred_element_type=jnp.float32
    )
    return (
        mixed.astype(jnp.bfloat16).reshape(-1, D),
        (queries, keys, values, top + jnp.log(total)),
    )


def attend_back(normed, context, weights, table, causal, nseq, kept, mixed, grad):
    queries, keys, values, logsum = kept
    grad_low = grad.astype(jnp.bfloat16)
    d_mixed = jnp.dot(grad_low, weights[3].T, preferred_element_type=jnp.float32).astype(
        jnp.bfloat16
    )
    scores, hot = attn_scores(split_heads(queries, nseq), split_heads(keys, nseq), table, causal)
    probs = jnp.exp(scores - logsum)
    d_probs = jnp.einsum(
        "sqhd,skhd->shqk",
        split_heads(d_mixed, nseq),
        split_heads(values, nseq),
        preferred_element_type=jnp.float32,
    )
    d_scores = (probs * (d_probs - jnp.sum(probs * d_probs, axis=-1, keepdims=True))).astype(
        jnp.bfloat16
    )
    scale = HD ** (-0.5)
    d_query = (
        (
            jnp.einsum(
                "shqk,skhd->sqhd",
                d_scores,
                split_heads(keys, nseq),
                preferred_element_type=jnp.float32,
            )
            * scale
        )
        .astype(jnp.bfloat16)
        .reshape(-1, D)
    )
    d_key = (
        (
            jnp.einsum(
                "shqk,sqhd->skhd",
                d_scores,
                split_heads(queries, nseq),
                preferred_element_type=jnp.float32,
            )
            * scale
        )
        .astype(jnp.bfloat16)
        .reshape(-1, D)
    )
    d_value = (
        jnp.einsum(
            "shqk,sqhd->skhd",
            probs.astype(jnp.bfloat16),
            split_heads(d_mixed, nseq),
            preferred_element_type=jnp.float32,
        )
        .astype(jnp.bfloat16)
        .reshape(-1, D)
    )
    d_weights = jnp.stack(
        [
            jnp.dot(normed.T, d_query, preferred_element_type=jnp.float32),
            jnp.dot(context.T, d_key, preferred_element_type=jnp.float32),
            jnp.dot(context.T, d_value, preferred_element_type=jnp.float32),
            jnp.dot(mixed.T, grad_low, preferred_element_type=jnp.float32),
        ]
    )
    d_normed = jnp.dot(d_query, weights[0].T, preferred_element_type=jnp.float32)
    d_context = jnp.dot(d_key, weights[1].T, preferred_element_type=jnp.float32) + jnp.dot(
        d_value, weights[2].T, preferred_element_type=jnp.float32
    )
    d_table = None
    if table is not None:
        d_table = offset_sums(d_scores, hot)
    return (d_weights, d_normed, d_context, d_table)


def swap_owners(buffer):
    return lax.all_to_all(buffer, "dp", split_axis=0, concat_axis=0, tiled=True)


def moe_forward(resid, gain, router, w_in, w_out, routes, cap):
    experts = router.shape[1]
    normed, inverse = normalize(resid, gain)
    normed_low = normed.astype(jnp.bfloat16)
    probs = jax.nn.softmax(
        jnp.dot(normed_low.astype(jnp.float32), router, precision=highest), axis=-1
    )
    hot = (routes[:, None] == jnp.arange(experts, dtype=jnp.int32)[None, :]).astype(jnp.int32)
    slots = jnp.sum(hot * jnp.cumsum(hot, axis=0), axis=1) - 1
    buffer = jnp.zeros((experts, cap, D), jnp.bfloat16).at[routes, slots].set(normed_low)
    arrived = swap_owners(buffer).reshape(-1, D)
    pre = jnp.dot(arrived, w_in, preferred_element_type=jnp.float32)
    hidden = jax.nn.gelu(pre, approximate=True).astype(jnp.bfloat16)
    result = jnp.einsum("nf,df->nd", hidden, w_out, preferred_element_type=jnp.float32).astype(
        jnp.bfloat16
    )
    returned = swap_owners(result.reshape(experts, cap, D))
    outputs = returned[routes, slots].astype(jnp.float32)
    gate = jnp.sum(probs * hot.astype(jnp.float32), axis=1)
    kept = (normed_low, inverse, probs, slots, hot, arrived, pre, hidden, outputs)
    return (resid + gate[:, None] * outputs, kept)


def moe_backward(resid, gain, router, w_in, w_out, routes, kept, grad, aux_scale, frac):
    normed_low, inverse, probs, slots, hot, arrived, pre, hidden, outputs = kept
    experts = router.shape[1]
    cap = arrived.shape[0] // experts
    hot_float = hot.astype(jnp.float32)
    gate = jnp.sum(probs * hot_float, axis=1)
    d_gate = jnp.sum(grad * outputs, axis=1)
    d_rows = (gate[:, None] * grad).astype(jnp.bfloat16)
    buffer = jnp.zeros((experts, cap, D), jnp.bfloat16).at[routes, slots].set(d_rows)
    d_arrived = swap_owners(buffer).reshape(-1, D)
    d_hidden = jnp.dot(d_arrived, w_out, preferred_element_type=jnp.float32)
    d_w_out = jnp.einsum("nd,nf->df", d_arrived, hidden, preferred_element_type=jnp.float32)
    unused, gelu_back = jax.vjp(partial(jax.nn.gelu, approximate=True), pre)
    d_pre = gelu_back(d_hidden)[0].astype(jnp.bfloat16)
    d_w_in = jnp.einsum("nd,nf->df", arrived, d_pre, preferred_element_type=jnp.float32)
    d_back = jnp.einsum("nf,df->nd", d_pre, w_in, preferred_element_type=jnp.float32).astype(
        jnp.bfloat16
    )
    returned = swap_owners(d_back.reshape(experts, cap, D))
    d_normed = returned[routes, slots].astype(jnp.float32)
    d_probs = hot_float * d_gate[:, None] + aux_scale * frac[None, :]
    d_logits = probs * (d_probs - jnp.sum(probs * d_probs, axis=-1, keepdims=True))
    d_router = jnp.dot(normed_low.astype(jnp.float32).T, d_logits, precision=highest)
    d_normed = d_normed + jnp.dot(d_logits, router.T, precision=highest)
    d_resid, d_gain = normalize_back(resid, inverse, gain, d_normed)
    return (grad + d_resid, d_gain, d_router, d_w_in, d_w_out)


def layer_forward(resid, memory, weights, gains, table, router, w_in, w_out, routes, cap, nseq):
    kept = []
    for index in range(1 if memory is None else 2):
        normed, inverse = normalize(resid, gains[index])
        normed = normed.astype(jnp.bfloat16)
        context = memory if index == 1 else normed
        weight_part = weights[4 * index : 4 * index + 4]
        mixed, saved = attend(
            normed,
            context,
            weight_part,
            None if index == 1 else table,
            memory is not None and index == 0,
            nseq,
        )
        kept.append((resid, inverse, normed, mixed, saved))
        resid = resid + jnp.dot(mixed, weight_part[3], preferred_element_type=jnp.float32)
    moe_input = resid
    resid, moe_kept = moe_forward(resid, gains[-1], router, w_in, w_out, routes, cap)
    return (resid, (kept, moe_input, moe_kept))


def layer_backward(
    memory,
    weights,
    gains,
    table,
    router,
    w_in,
    w_out,
    routes,
    nseq,
    saved_all,
    grad,
    aux_scale,
    frac,
):
    kept, moe_input, moe_kept = saved_all
    grad, gain_moe, d_router, d_w_in, d_w_out = moe_backward(
        moe_input, gains[-1], router, w_in, w_out, routes, moe_kept, grad, aux_scale, frac
    )
    d_weights = []
    d_gains = [gain_moe]
    d_table = None
    d_memory = None
    for index in reversed(range(len(kept))):
        resid, inverse, normed, mixed, saved = kept[index]
        context = memory if index == 1 else normed
        weight_part = weights[4 * index : 4 * index + 4]
        part_grads, d_normed, d_context, table_grad = attend_back(
            normed,
            context,
            weight_part,
            None if index == 1 else table,
            memory is not None and index == 0,
            nseq,
            saved,
            mixed,
            grad,
        )
        if index == 1:
            d_memory = d_context
        else:
            d_normed = d_normed + d_context
            d_table = table_grad
        d_resid, d_gain = normalize_back(resid, inverse, gains[index], d_normed)
        grad = grad + d_resid
        d_weights.insert(0, part_grads)
        d_gains.insert(0, d_gain)
    return (
        grad,
        jnp.concatenate(d_weights, axis=0),
        d_gains,
        d_table,
        d_router,
        d_w_in,
        d_w_out,
        d_memory,
    )


def merge_stats(first, second):
    top = jnp.maximum(first[0], second[0])
    total = first[1] * jnp.exp(first[0] - top) + second[1] * jnp.exp(second[0] - top)
    return (top, total, first[2] + second[2])


def route_share(routes, experts):
    flat_routes = routes.reshape(-1)
    hot = (flat_routes[:, None] == jnp.arange(experts, dtype=jnp.int32)[None, :]).astype(
        jnp.float32
    )
    return jnp.sum(hot, axis=0) / flat_routes.shape[0]


def ns_step(product, current):
    once = jnp.einsum("mde,mec->mdc", product, current, preferred_element_type=jnp.float32).astype(
        jnp.bfloat16
    )
    twice = jnp.einsum("mde,mec->mdc", product, once, preferred_element_type=jnp.float32)
    return (
        coef_a * current.astype(jnp.float32) + coef_b * once.astype(jnp.float32) + coef_c * twice
    ).astype(jnp.bfloat16)


def gram_of(dense_part, expert_part):
    local = jnp.concatenate(
        [
            jnp.einsum("mdc,mec->mde", dense_part, dense_part, preferred_element_type=jnp.float32),
            jnp.einsum(
                "mdc,mec->mde", expert_part, expert_part, preferred_element_type=jnp.float32
            ),
        ],
        axis=0,
    )
    summed = lax.psum_scatter(local.astype(jnp.bfloat16), "mp", scatter_dimension=1, tiled=True)
    return lax.all_gather(summed, "mp", axis=1, tiled=True)


def orthogonalize(dense_mom, expert_mom):
    expert_shape = expert_mom.shape
    expert_flat = expert_mom.reshape(-1, D, expert_shape[-1])
    count_dense = dense_mom.shape[0]
    start = gram_of(dense_mom.astype(jnp.bfloat16), expert_flat.astype(jnp.bfloat16))
    start_float = start.astype(jnp.float32)
    scale = jnp.trace(start_float, axis1=1, axis2=2) + eps_gram
    root = lax.rsqrt(scale)[:, None, None]
    dense_part = (dense_mom * root[:count_dense]).astype(jnp.bfloat16)
    expert_part = (expert_flat * root[count_dense:]).astype(jnp.bfloat16)
    product = (start_float / scale[:, None, None]).astype(jnp.bfloat16)
    for turn in range(NS_ITERS):
        if turn:
            product = gram_of(dense_part, expert_part)
        dense_part = ns_step(product[:count_dense], dense_part)
        expert_part = ns_step(product[count_dense:], expert_part)
    return (dense_part, expert_part.reshape(expert_shape))


def adam(weight, first, second, grad, rate, decay):
    first = beta_one * first + (1 - beta_one) * grad
    second = beta_two * second + (1 - beta_two) * grad * grad
    update = first / (1 - beta_one**STEP) / (jnp.sqrt(second / (1 - beta_two**STEP)) + eps_adam)
    return (weight - rate * (update + decay * weight), first, second)


def as_columns(stored):
    return jnp.transpose(stored.reshape(stored.shape[0], -1, D), (0, 2, 1))


def as_stored(columns):
    return jnp.transpose(columns, (0, 2, 1)).reshape(columns.shape[0], -1)


def on_device(
    src_ids,
    targets,
    loss_pos,
    loss_mask,
    routes_src,
    routes_tgt,
    dense_w,
    dense_m,
    expert_w,
    expert_m,
    table_w,
    table_m,
    table_v,
    gains_w,
    gains_m,
    gains_v,
    router_w,
    router_m,
    router_v,
    bias_w,
    bias_m,
    bias_v,
):
    groups = lax.axis_size("mp")
    column = lax.axis_index("mp")
    experts = lax.axis_size("dp")
    seq_dev = src_ids.shape[0] // groups
    src_len = src_ids.shape[1]
    tgt_len = targets.shape[1]
    npos = loss_pos.shape[1]
    vocab_dev = table_w.shape[0]
    first_seq = (lax.axis_index("dp") * groups + column) * seq_dev
    src_rows = seq_dev * src_len
    rows_dev = src_rows + seq_dev * tgt_len
    dense_cols = as_columns(dense_w)
    dense_old = as_columns(dense_m)
    dense_low, expert_low = (
        lax.all_gather(dense_cols.astype(jnp.bfloat16), "mp", axis=2, tiled=True),
        lax.all_gather(expert_w.astype(jnp.bfloat16), "mp", axis=4, tiled=True),
    )
    table_low = table_w.astype(jnp.bfloat16)
    whole = lax.all_gather(table_low, "mp", axis=0, tiled=True)
    dec_ids = jnp.concatenate(
        [jnp.zeros((targets.shape[0], 1), jnp.int32), targets[:, :-1]], axis=1
    )
    all_ids = jnp.concatenate([src_ids, dec_ids], axis=1).reshape(-1)
    local_ids = all_ids - column * vocab_dev
    inside = (local_ids >= 0) & (local_ids < vocab_dev)
    clipped = jnp.clip(local_ids, 0, vocab_dev - 1)
    own_ids = lax.dynamic_slice_in_dim(all_ids, column * rows_dev, rows_dev)
    embedded = jnp.take(whole, own_ids, axis=0).astype(jnp.float32)
    own_src = lax.dynamic_slice_in_dim(routes_src, first_seq, seq_dev, 0).reshape(-1)
    own_tgt = lax.dynamic_slice_in_dim(routes_tgt, first_seq, seq_dev, 0).reshape(-1)
    cap_src = (5 * src_rows + 4 * experts - 1) // (4 * experts)
    cap_tgt = (5 * seq_dev * tgt_len + 4 * experts - 1) // (4 * experts)
    total_src = routes_src.shape[0] * routes_src.shape[1]
    total_tgt = routes_tgt.shape[0] * routes_tgt.shape[1]
    frac_src = route_share(routes_src, experts)
    frac_tgt = route_share(routes_tgt, experts)
    enc_out, enc_saved = layer_forward(
        embedded[:src_rows],
        None,
        dense_low[0:4],
        gains_w[0:2],
        bias_w[0],
        router_w[0],
        expert_low[0, 0, 0],
        expert_low[0, 1, 0],
        own_src,
        cap_src,
        seq_dev,
    )
    memory_float, memory_inv = normalize(enc_out, gains_w[2])
    memory = memory_float.astype(jnp.bfloat16)
    dec_result, dec_saved = layer_forward(
        embedded[src_rows:],
        memory,
        dense_low[4:12],
        gains_w[3:6],
        bias_w[1],
        router_w[1],
        expert_low[1, 0, 0],
        expert_low[1, 1, 0],
        own_tgt,
        cap_tgt,
        seq_dev,
    )
    final_float, final_inv = normalize(dec_result, gains_w[6])
    final_low = final_float.astype(jnp.bfloat16)
    head_scale = D ** (-0.5)
    own_pos = lax.dynamic_slice_in_dim(loss_pos, column * seq_dev, seq_dev, 0)
    flat_pos = (jnp.arange(seq_dev, dtype=jnp.int32)[:, None] * tgt_len + own_pos).reshape(-1)
    chosen = jnp.take(final_low, flat_pos, axis=0)
    gathered = lax.all_gather(chosen, "mp", axis=0, tiled=True)
    logits = jnp.dot(gathered, table_low.T, preferred_element_type=jnp.float32) * head_scale
    wanted = jnp.take_along_axis(targets, loss_pos, axis=1).reshape(-1) - column * vocab_dev
    hits = jnp.arange(vocab_dev, dtype=jnp.int32)[None, :] == wanted[:, None]
    top = jnp.max(logits, axis=1)
    top, expsum, picked = merged(
        (
            top,
            jnp.sum(jnp.exp(logits - top[:, None]), axis=1),
            jnp.sum(jnp.where(hits, logits, 0.0), axis=1),
        ),
        "mp",
        merge_stats,
    )
    logsum = top + jnp.log(expsum)
    mask_rows = loss_mask.reshape(-1).astype(jnp.float32)
    own_span = seq_dev * npos
    own_loss = jnp.sum(
        lax.dynamic_slice_in_dim(mask_rows * (logsum - picked), column * own_span, own_span)
    )
    own_count = jnp.sum(lax.dynamic_slice_in_dim(mask_rows, column * own_span, own_span))
    d_logits = (
        mask_rows[:, None] * (jnp.exp(logits - logsum[:, None]) - hits.astype(jnp.float32))
    ).astype(jnp.bfloat16)
    table_grad = jnp.dot(d_logits.T, gathered, preferred_element_type=jnp.float32) * head_scale
    d_chosen = lax.psum_scatter(
        (jnp.dot(d_logits, table_low, preferred_element_type=jnp.float32) * head_scale).astype(
            jnp.bfloat16
        ),
        "mp",
        scatter_dimension=0,
        tiled=True,
    ).astype(jnp.float32)
    d_final = jnp.zeros(final_float.shape, jnp.float32).at[flat_pos].add(d_chosen)
    d_dec, gain_final = normalize_back(dec_result, final_inv, gains_w[6], d_final)
    d_dec, dec_dense, dec_gains, dec_table, dec_router, dec_in, dec_outw, d_memory = layer_backward(
        memory,
        dense_low[4:12],
        gains_w[3:6],
        bias_w[1],
        router_w[1],
        expert_low[1, 0, 0],
        expert_low[1, 1, 0],
        own_tgt,
        seq_dev,
        dec_saved,
        d_dec,
        aux_weight * experts / total_tgt,
        frac_tgt,
    )
    d_enc, gain_memory = normalize_back(enc_out, memory_inv, gains_w[2], d_memory)
    d_enc, enc_dense, enc_gains, enc_table, enc_router, enc_in, enc_outw, unused = layer_backward(
        None,
        dense_low[0:4],
        gains_w[0:2],
        bias_w[0],
        router_w[0],
        expert_low[0, 0, 0],
        expert_low[0, 1, 0],
        own_src,
        seq_dev,
        enc_saved,
        d_enc,
        aux_weight * experts / total_src,
        frac_src,
    )
    d_embedded = jnp.concatenate([d_enc, d_dec], axis=0).astype(jnp.bfloat16)
    arrived = lax.all_gather(d_embedded, "mp", axis=0, tiled=True)
    table_grad = table_grad.at[clipped].add(
        jnp.where(inside[:, None], arrived.astype(jnp.float32), 0.0)
    )
    dense_grad = jnp.concatenate([enc_dense, dec_dense], axis=0)
    expert_grad = jnp.stack([jnp.stack([enc_in, enc_outw]), jnp.stack([dec_in, dec_outw])])[
        :, :, None
    ]
    gains_grad = jnp.stack(enc_gains + [gain_memory] + dec_gains + [gain_final])
    router_grad = jnp.stack([enc_router, dec_router])
    bias_grad = jnp.stack([enc_table, dec_table])
    dense_share, expert_share, gains_share, router_share, bias_share = (
        lax.psum_scatter(
            dense_grad.astype(jnp.bfloat16), "mp", scatter_dimension=2, tiled=True
        ).astype(jnp.float32),
        lax.psum_scatter(
            expert_grad.astype(jnp.bfloat16), "mp", scatter_dimension=4, tiled=True
        ).astype(jnp.float32),
        lax.psum_scatter(
            gains_grad.astype(jnp.bfloat16), "mp", scatter_dimension=1, tiled=True
        ).astype(jnp.float32),
        lax.psum_scatter(
            router_grad.astype(jnp.bfloat16), "mp", scatter_dimension=1, tiled=True
        ).astype(jnp.float32),
        lax.psum_scatter(
            bias_grad.astype(jnp.bfloat16), "mp", scatter_dimension=1, tiled=True
        ).astype(jnp.float32),
    )
    others = (gains_share, router_share, bias_share, table_grad)
    summed = (
        lax.psum(others[0].astype(jnp.bfloat16), "dp").astype(jnp.float32),
        lax.psum(others[1].astype(jnp.bfloat16), "dp").astype(jnp.float32),
        lax.psum(others[2].astype(jnp.bfloat16), "dp").astype(jnp.float32),
        lax.psum(others[3].astype(jnp.bfloat16), "dp").astype(jnp.float32),
    )
    gains_share, router_share, bias_share, table_grad = (summed[0], summed[1], summed[2], summed[3])
    first_row = (lax.axis_index("dp") == 0).astype(jnp.float32)
    count_dense = dense_share.shape[0]
    per_dev = -(-count_dense // experts)
    filler = jnp.zeros((per_dev * experts - count_dense,) + dense_share.shape[1:], jnp.float32)
    dense_piece = lax.psum_scatter(
        jnp.concatenate([dense_share, filler], axis=0).astype(jnp.bfloat16),
        "dp",
        scatter_dimension=0,
        tiled=True,
    ).astype(jnp.float32)
    old_piece = lax.dynamic_slice_in_dim(
        jnp.concatenate([dense_old, filler], axis=0), lax.axis_index("dp") * per_dev, per_dev, 0
    )
    dense_squares = jnp.sum(dense_piece * dense_piece)
    replicated = sum(
        (jnp.sum(part * part) for part in (gains_share, router_share, bias_share, table_grad))
    )
    squares = first_row * replicated + dense_squares + jnp.sum(expert_share * expert_share)
    load_src = jnp.sum(enc_saved[2][2], axis=0)
    load_tgt = jnp.sum(dec_saved[2][2], axis=0)
    squares, loss_sum, count, load_src, load_tgt = lax.psum(
        (squares, own_loss, own_count, load_src, load_tgt), ("dp", "mp")
    )
    grad_norm = jnp.sqrt(squares)
    clip = 1.0 / jnp.maximum(grad_norm, 1.0)
    aux = (
        aux_weight
        * experts
        * (jnp.sum(frac_src * load_src) / total_src + jnp.sum(frac_tgt * load_tgt) / total_tgt)
    )
    loss = jnp.stack([loss_sum + aux, count])
    piece_moment = 0.5 * old_piece + clip * dense_piece
    expert_moment = 0.5 * expert_m + clip * expert_share
    piece_orth, expert_orth = orthogonalize(piece_moment, expert_moment)
    both = lax.all_gather(
        jnp.stack([piece_moment, piece_orth.astype(jnp.float32)]).astype(jnp.bfloat16),
        "dp",
        axis=1,
        tiled=True,
    ).astype(jnp.float32)
    dense_moment = both[0][:count_dense]
    dense_orth = both[1][:count_dense]
    keep_rate = 1 - rate_matrix * decay_matrix
    dense_new = dense_cols * keep_rate - rate_matrix * 0.2 * math.sqrt(D) * dense_orth
    expert_new = expert_w * keep_rate - rate_matrix * 0.2 * math.sqrt(
        max(D, FF)
    ) * expert_orth.astype(jnp.float32)
    table_piece = table_m.shape[0]
    table_start = lax.axis_index("dp") * table_piece
    table_clipped = clip * lax.dynamic_slice_in_dim(table_grad, table_start, table_piece, 0)
    table_new, table_first, table_second = adam(
        lax.dynamic_slice_in_dim(table_w, table_start, table_piece, 0),
        table_m,
        table_v,
        table_clipped,
        1.5,
        0.01,
    )
    gain_cols = gains_share.shape[1]
    gains_new, gains_first, gains_second = adam(
        lax.dynamic_slice_in_dim(gains_w, column * gain_cols, gain_cols, 1),
        gains_m,
        gains_v,
        clip * gains_share,
        0.5,
        0.0,
    )
    router_rows = router_share.shape[1]
    router_new, router_first, router_second = adam(
        lax.dynamic_slice_in_dim(router_w, column * router_rows, router_rows, 1),
        router_m,
        router_v,
        clip * router_share,
        0.02,
        0.01,
    )
    bias_rows = bias_share.shape[1]
    bias_new, bias_first, bias_second = adam(
        lax.dynamic_slice_in_dim(bias_w, column * bias_rows, bias_rows, 1),
        bias_m,
        bias_v,
        clip * bias_share,
        0.5,
        0.0,
    )
    dense_flat = as_stored(dense_new)
    return (
        loss,
        grad_norm,
        dense_flat,
        as_stored(dense_moment),
        dense_flat.astype(jnp.bfloat16),
        expert_new,
        expert_moment,
        expert_new.astype(jnp.bfloat16),
        table_new,
        table_clipped,
        table_second,
        gains_new,
        gains_first,
        gains_second,
        router_new,
        router_first,
        router_second,
        bias_new,
        bias_first,
        bias_second,
    )


def solution(mesh):
    in_specs = (
        P("dp", None),
        P("dp", None),
        P("dp", None),
        P("dp", None),
        P(),
        P(),
        P(None, "mp"),
        P(None, "mp"),
        P(None, None, "dp", None, "mp"),
        P(None, None, "dp", None, "mp"),
        P("mp", None),
        P(("mp", "dp"), None),
        P(("mp", "dp"), None),
        P(),
        P(None, "mp"),
        P(None, "mp"),
        P(),
        P(None, "mp", None),
        P(None, "mp", None),
        P(),
        P(None, "mp", None),
        P(None, "mp", None),
    )
    out_specs = (
        P(),
        P(),
        P(None, "mp"),
        P(None, "mp"),
        P(None, "mp"),
        P(None, None, "dp", None, "mp"),
        P(None, None, "dp", None, "mp"),
        P(None, None, "dp", None, "mp"),
        P(("mp", "dp"), None),
        P(("mp", "dp"), None),
        P(("mp", "dp"), None),
        P(None, "mp"),
        P(None, "mp"),
        P(None, "mp"),
        P(None, "mp", None),
        P(None, "mp", None),
        P(None, "mp", None),
        P(None, "mp", None),
        P(None, "mp", None),
        P(None, "mp", None),
    )
    return jax.shard_map(
        on_device, mesh=mesh, in_specs=in_specs, out_specs=out_specs, check_vma=False
    )
```

profile of v0, /device:TPU:2, one launch (start us, length us, event | category | flops | bytes accessed | tf_op | source)
XLA Modules:
  0.0 5136.1 jit_solution(12619227847209231323)
XLA Ops:
  94.9 63.4 %copy.296 = f32[2,8,768,1536]{3,1,2,0:T(8,128)} copy(f32[2,8,768,1536]{3,2,1,0:T(8,128)} %bitcast.186) | data formatting | bytes 150994944
  209.3 1086.0 %while.22 = (u32[]{:T(128)}, f32[1,12,1178880]{2,1,0:T(8,128)}, f32[14146560]{0:T(1024)}, u32[]{}, f32[]{:T(128)}, /*index=5*/u32[]{}, u32[]{}, u32[]{}) while((u32[]{:T(128)}, f32[1,12,1178880]{2,1,0:T(8,128)}, f32[14146560]{0:T(1024)}, u32[]{}, f32[]{:T(128)}, /*index=5*/u32[]{}, u32[]{}, u32[]{}) %tuple.137), condition=%wide.cond, body=%wide.body.sunk | while | flops 9 | bytes 18862272
  1295.3 88.5 %reshape.1014 = f32[12,768,1535]{2,1,0:T(8,128)} reshape(f32[14146560]{0:T(1024)} %get-tuple-element.305) | data formatting | bytes 113172480 | tf_op jit(solution)/shard_map/reshape | solution.py:78
  1548.3 106.9 %scatter_fusion = bf16[4,240,768]{2,1,0:T(8,128)(2,1)} fusion(bf16[4,240,768]{2,1,0:T(8,128)(2,1)} %broadcast.879.clone, s32[768]{0:T(1024)S(1)} %get-tuple-element.328, bf16[768,768]{1,0:T(8,128)(2,1)} %multiply_convert_fusion.12), kind=kCustom, calls=%fused_computation.7 | custom fusion | bytes 3545088 | tf_op jit(solution)/shard_map/scatter | solution.py:215
  2096.8 107.8 %scatter_fusion.3 = bf16[4,240,768]{2,1,0:T(8,128)(2,1)} fusion(bf16[4,240,768]{2,1,0:T(8,128)(2,1)} %broadcast.879, s32[768]{0:T(1024)S(1)} %copy-done.6, bf16[768,768]{1,0:T(8,128)(2,1)S(1)} %get-tuple-element.390), kind=kCustom, calls=%fused_computation.11 | custom fusion | bytes 3545088 | tf_op jit(solution)/shard_map/scatter | solution.py:237
  2828.9 1091.0 %while.23 = (u32[]{:T(128)}, bf16[14146560]{0:T(1024)(128)(2,1)}, bf16[1,12,1178880]{2,1,0:T(8,128)(2,1)}, u32[]{}, u32[]{}, /*index=5*/u32[]{}, u32[]{}, u32[]{}) while((u32[]{:T(128)}, bf16[14146560]{0:T(1024)(128)(2,1)}, bf16[1,12,1178880]{2,1,0:T(8,128)(2,1)}, u32[]{}, u32[]{}, /*index=5*/u32[]{}, u32[]{}, u32[]{}) %tuple.143), condition=%wide.cond.1, body=%wide.body.1.sunk | while | flops 9 | bytes 14146737
  2835.6 84.3 %dynamic-update-slice.29 = bf16[1,12,1178880]{2,1,0:T(8,128)(2,1)} dynamic-update-slice(bf16[1,12,1178880]{2,1,0:T(8,128)(2,1)} %get-tuple-element.619, bf16[1,1,1178880]{2,1,0:T(2,128)(2,1)} %reshape.1194, u32[]{:T(128)S(6)} %multiply.153, u32[]{:T(128)S(6)} %multiply.155, u32[]{} %constant.890..sunk) | dynamic-update-slice | bytes 4715524
  2926.7 84.1 %dynamic-update-slice.29 = bf16[1,12,1178880]{2,1,0:T(8,128)(2,1)} dynamic-update-slice(bf16[1,12,1178880]{2,1,0:T(8,128)(2,1)} %get-tuple-element.619, bf16[1,1,1178880]{2,1,0:T(2,128)(2,1)} %reshape.1194, u32[]{:T(128)S(6)} %multiply.153, u32[]{:T(128)S(6)} %multiply.155, u32[]{} %constant.890..sunk) | dynamic-update-slice | bytes 4715524
  3017.5 84.1 %dynamic-update-slice.29 = bf16[1,12,1178880]{2,1,0:T(8,128)(2,1)} dynamic-update-slice(bf16[1,12,1178880]{2,1,0:T(8,128)(2,1)} %get-tuple-element.619, bf16[1,1,1178880]{2,1,0:T(2,128)(2,1)} %reshape.1194, u32[]{:T(128)S(6)} %multiply.153, u32[]{:T(128)S(6)} %multiply.155, u32[]{} %constant.890..sunk) | dynamic-update-slice | bytes 4715524
  3108.3 84.1 %dynamic-update-slice.29 = bf16[1,12,1178880]{2,1,0:T(8,128)(2,1)} dynamic-update-slice(bf16[1,12,1178880]{2,1,0:T(8,128)(2,1)} %get-tuple-element.619, bf16[1,1,1178880]{2,1,0:T(2,128)(2,1)} %reshape.1194, u32[]{:T(128)S(6)} %multiply.153, u32[]{:T(128)S(6)} %multiply.155, u32[]{} %constant.890..sunk) | dynamic-update-slice | bytes 4715524
  3199.1 84.1 %dynamic-update-slice.29 = bf16[1,12,1178880]{2,1,0:T(8,128)(2,1)} dynamic-update-slice(bf16[1,12,1178880]{2,1,0:T(8,128)(2,1)} %get-tuple-element.619, bf16[1,1,1178880]{2,1,0:T(2,128)(2,1)} %reshape.1194, u32[]{:T(128)S(6)} %multiply.153, u32[]{:T(128)S(6)} %multiply.155, u32[]{} %constant.890..sunk) | dynamic-update-slice | bytes 4715524
  3290.0 84.1 %dynamic-update-slice.29 = bf16[1,12,1178880]{2,1,0:T(8,128)(2,1)} dynamic-update-slice(bf16[1,12,1178880]{2,1,0:T(8,128)(2,1)} %get-tuple-element.619, bf16[1,1,1178880]{2,1,0:T(2,128)(2,1)} %reshape.1194, u32[]{:T(128)S(6)} %multiply.153, u32[]{:T(128)S(6)} %multiply.155, u32[]{} %constant.890..sunk) | dynamic-update-slice | bytes 4715524
  3380.8 84.1 %dynamic-update-slice.29 = bf16[1,12,1178880]{2,1,0:T(8,128)(2,1)} dynamic-update-slice(bf16[1,12,1178880]{2,1,0:T(8,128)(2,1)} %get-tuple-element.619, bf16[1,1,1178880]{2,1,0:T(2,128)(2,1)} %reshape.1194, u32[]{:T(128)S(6)} %multiply.153, u32[]{:T(128)S(6)} %multiply.155, u32[]{} %constant.890..sunk) | dynamic-update-slice | bytes 4715524
  3471.6 84.1 %dynamic-update-slice.29 = bf16[1,12,1178880]{2,1,0:T(8,128)(2,1)} dynamic-update-slice(bf16[1,12,1178880]{2,1,0:T(8,128)(2,1)} %get-tuple-element.619, bf16[1,1,1178880]{2,1,0:T(2,128)(2,1)} %reshape.1194, u32[]{:T(128)S(6)} %multiply.153, u32[]{:T(128)S(6)} %multiply.155, u32[]{} %constant.890..sunk) | dynamic-update-slice | bytes 4715524
  3562.4 84.4 %dynamic-update-slice.29 = bf16[1,12,1178880]{2,1,0:T(8,128)(2,1)} dynamic-update-slice(bf16[1,12,1178880]{2,1,0:T(8,128)(2,1)} %get-tuple-element.619, bf16[1,1,1178880]{2,1,0:T(2,128)(2,1)} %reshape.1194, u32[]{:T(128)S(6)} %multiply.153, u32[]{:T(128)S(6)} %multiply.155, u32[]{} %constant.890..sunk) | dynamic-update-slice | bytes 4715524
  3653.5 84.4 %dynamic-update-slice.29 = bf16[1,12,1178880]{2,1,0:T(8,128)(2,1)} dynamic-update-slice(bf16[1,12,1178880]{2,1,0:T(8,128)(2,1)} %get-tuple-element.619, bf16[1,1,1178880]{2,1,0:T(2,128)(2,1)} %reshape.1194, u32[]{:T(128)S(6)} %multiply.153, u32[]{:T(128)S(6)} %multiply.155, u32[]{} %constant.890..sunk) | dynamic-update-slice | bytes 4715524
  3744.5 84.4 %dynamic-update-slice.29 = bf16[1,12,1178880]{2,1,0:T(8,128)(2,1)} dynamic-update-slice(bf16[1,12,1178880]{2,1,0:T(8,128)(2,1)} %get-tuple-element.619, bf16[1,1,1178880]{2,1,0:T(2,128)(2,1)} %reshape.1194, u32[]{:T(128)S(6)} %multiply.153, u32[]{:T(128)S(6)} %multiply.155, u32[]{} %constant.890..sunk) | dynamic-update-slice | bytes 4715524
  3835.6 84.4 %dynamic-update-slice.29 = bf16[1,12,1178880]{2,1,0:T(8,128)(2,1)} dynamic-update-slice(bf16[1,12,1178880]{2,1,0:T(8,128)(2,1)} %get-tuple-element.619, bf16[1,1,1178880]{2,1,0:T(2,128)(2,1)} %reshape.1194, u32[]{:T(128)S(6)} %multiply.153, u32[]{:T(128)S(6)} %multiply.155, u32[]{} %constant.890..sunk) | dynamic-update-slice | bytes 4715524
  3920.0 67.1 %scatter_custom_fusion.5 = f32[4016,768]{1,0:T(8,128)} fusion(f32[4016,768]{1,0:T(8,128)} %convolution_multiply_fusion, s32[8192]{0:T(1024)S(1)} %bitcast.715, bf16[8192,768]{1,0:T(8,128)(2,1)} %all-gather.23.cloned.1.call-done, f32[]{:T(128)} %constant.123.clone.1, pred[8192]{0:T(1024)(128)(4,1)S(1)} %compare_and_fusion), kind=kCustom, calls=%fused_computation.25 | custom fusion | flops 18874368 | bytes 24928768 | tf_op jit(solution)/shard_map/scatter-add | solution.py:572
  4285.7 69.8 %reduce-scatter.24.cloned.1.call-done = bf16[7,96,768]{2,1,0:T(8,128)(2,1)} async-done(((bf16[7,768,768]{2,1,0:T(8,128)(2,1)}), bf16[7,96,768]{2,1,0:T(8,128)(2,1)}) %reduce-scatter.24.cloned.1.call-update) | async-done | bytes 1032208 | tf_op jit(solution)/shard_map/reduce_scatter | solution.py:372
  4453.2 70.7 %reduce-scatter.26.cloned.1.call-done = bf16[7,96,768]{2,1,0:T(8,128)(2,1)} async-done(((bf16[7,768,768]{2,1,0:T(8,128)(2,1)}), bf16[7,96,768]{2,1,0:T(8,128)(2,1)}) %reduce-scatter.26.cloned.1.call-update) | async-done | bytes 1032208 | tf_op jit(solution)/shard_map/reduce_scatter | solution.py:372
  4604.8 70.7 %reduce-scatter.28.cloned.1.call-done = bf16[7,96,768]{2,1,0:T(8,128)(2,1)} async-done(((bf16[7,768,768]{2,1,0:T(8,128)(2,1)}), bf16[7,96,768]{2,1,0:T(8,128)(2,1)}) %reduce-scatter.28.cloned.1.call-update) | async-done | bytes 1032208 | tf_op jit(solution)/shard_map/reduce_scatter | solution.py:372
  4756.5 70.6 %reduce-scatter.30.cloned.1.call-done = bf16[7,96,768]{2,1,0:T(8,128)(2,1)} async-done(((bf16[7,768,768]{2,1,0:T(8,128)(2,1)}), bf16[7,96,768]{2,1,0:T(8,128)(2,1)}) %reduce-scatter.30.cloned.1.call-update) | async-done | bytes 1032208 | tf_op jit(solution)/shard_map/reduce_scatter | solution.py:372
  4908.1 70.6 %reduce-scatter.32.cloned.1.call-done = bf16[7,96,768]{2,1,0:T(8,128)(2,1)} async-done(((bf16[7,768,768]{2,1,0:T(8,128)(2,1)}), bf16[7,96,768]{2,1,0:T(8,128)(2,1)}) %reduce-scatter.32.cloned.1.call-update) | async-done | bytes 1032208 | tf_op jit(solution)/shard_map/reduce_scatter | solution.py:372
  (970 shorter events, 3313.4 us)
Async XLA Ops:
  7.2 1455.7 %all-gather.15.cloned.1.call-start = ((), (), s32[]{:S(2)}) async-start(), calls=%async_computation.19 | async-start | bytes 55517184 | tf_op jit(solution)/shard_map/all_gather | solution.py:452
  14.9 1472.6 %all-gather.17.cloned.1.call-start = ((), (), s32[]{:S(2)}) async-start(), calls=%async_computation.20 | async-start | bytes 15925248 | tf_op jit(solution)/shard_map/all_gather | solution.py:448
  23.4 1655.1 %all-gather.19.cloned.1.call-start = ((), (), s32[]{:S(2)}) async-start(), calls=%async_computation.21 | async-start | bytes 21233664 | tf_op jit(solution)/shard_map/all_gather | solution.py:449
  1655.2 40.1 all-to-all-start
  1853.5 44.5 all-gather.21.cloned.1.call-start
  1873.0 120.4 %reduce-scatter.20.cloned.1.call-start = ((), (), s32[]{:S(2)}) async-start(), calls=%async_computation.23 | async-start | bytes 1769472 | tf_op jit(solution)/shard_map/reduce_scatter | solution.py:529
  2270.5 292.0 %reduce-scatter.38.cloned.1.call-start = ((), (), s32[]{:S(2)}) async-start(), calls=%async_computation.40 | async-start | bytes 15925248
  2462.8 282.5 %reduce-scatter.36.cloned.1.call-start = ((), (), s32[]{:S(2)}) async-start(), calls=%async_computation.39 | async-start | bytes 221184
  2478.0 1442.0 %all-gather.23.cloned.1.call-start = ((), (), s32[]{:S(2)}) async-start(), calls=%async_computation.24 | async-start | bytes 14155776 | tf_op jit(solution)/shard_map/all_gather | solution.py:571
  2491.1 1647.1 %reduce-scatter.34.cloned.1.call-start = ((), (), s32[]{:S(2)}) async-start(), calls=%async_computation.38 | async-start | bytes 221184
  2501.9 1653.4 %reduce-scatter.22.cloned.1.call-start = ((), (), s32[]{:S(2)}) async-start(), calls=%async_computation.26 | async-start | bytes 2211840 | tf_op jit(solution)/shard_map/reduce_scatter | solution.py:611
  2567.3 1589.9 %reduce-scatter.40.cloned.1.call-start = ((), (), s32[]{:S(2)}) async-start(), calls=%async_computation.41 | async-start | bytes 21233664
  2699.3 1515.7 %all-reduce.9.cloned.1.call-start = ((), (), s32[]{:S(2)}) async-start(), calls=%async_computation.25 | async-start | bytes 12337152 | tf_op jit(solution)/shard_map/psum | solution.py:604
  3994.8 360.6 %reduce-scatter.24.cloned.1.call-start = ((), (), s32[]{:S(2)}) async-start(), calls=%async_computation.27 | async-start | bytes 9289728 | tf_op jit(solution)/shard_map/reduce_scatter | solution.py:372
  4285.6 125.7 %all-gather.25.cloned.1.call-start = ((), (), s32[]{:S(2)}) async-start(), calls=%async_computation.28 | async-start | bytes 9289728 | tf_op jit(solution)/shard_map/all_gather | solution.py:373
  4355.5 168.4 %reduce-scatter.26.cloned.1.call-start = ((), (), s32[]{:S(2)}) async-start(), calls=%async_computation.29 | async-start | bytes 9289728 | tf_op jit(solution)/shard_map/reduce_scatter | solution.py:372
  4453.1 126.4 %all-gather.27.cloned.1.call-start = ((), (), s32[]{:S(2)}) async-start(), calls=%async_computation.30 | async-start | bytes 9289728 | tf_op jit(solution)/shard_map/all_gather | solution.py:373
  4523.9 151.5 %reduce-scatter.28.cloned.1.call-start = ((), (), s32[]{:S(2)}) async-start(), calls=%async_computation.31 | async-start | bytes 9289728 | tf_op jit(solution)/shard_map/reduce_scatter | solution.py:372
  4604.7 126.6 %all-gather.29.cloned.1.call-start = ((), (), s32[]{:S(2)}) async-start(), calls=%async_computation.32 | async-start | bytes 9289728 | tf_op jit(solution)/shard_map/all_gather | solution.py:373
  4675.5 151.7 %reduce-scatter.30.cloned.1.call-start = ((), (), s32[]{:S(2)}) async-start(), calls=%async_computation.33 | async-start | bytes 9289728 | tf_op jit(solution)/shard_map/reduce_scatter | solution.py:372
  4756.5 126.4 %all-gather.31.cloned.1.call-start = ((), (), s32[]{:S(2)}) async-start(), calls=%async_computation.34 | async-start | bytes 9289728 | tf_op jit(solution)/shard_map/all_gather | solution.py:373
  4827.2 151.5 %reduce-scatter.32.cloned.1.call-start = ((), (), s32[]{:S(2)}) async-start(), calls=%async_computation.35 | async-start | bytes 9289728 | tf_op jit(solution)/shard_map/reduce_scatter | solution.py:372
  4908.0 126.8 %all-gather.33.cloned.1.call-start = ((), (), s32[]{:S(2)}) async-start(), calls=%async_computation.36 | async-start | bytes 9289728 | tf_op jit(solution)/shard_map/all_gather | solution.py:373
  4978.7 132.8 %all-gather.35.cloned.1.call-start = ((), (), s32[]{:S(2)}) async-start(), calls=%async_computation.37 | async-start | bytes 4423680 | tf_op jit(solution)/shard_map/all_gather | solution.py:641
  (231 other events, 5200.3 us)
Sparse Core Ops, SparseCore 0:
  15.0 229.3 all-gather.14
  246.8 78.7 all-gather.16
  328.1 102.3 all-gather.18
  1873.1 24.7 all-gather.20
  1954.0 39.3 reduce-scatter.19
  2462.9 99.5 reduce-scatter.37
  2565.6 33.6 reduce-scatter.35
  2601.9 72.1 all-gather.22
  2678.0 33.4 reduce-scatter.33
  2714.2 38.4 reduce-scatter.21
  2756.8 125.1 reduce-scatter.39
  3994.9 219.9 all-reduce.8
  4285.7 69.6 reduce-scatter.23
  4357.4 53.9 all-gather.24
  4453.3 70.5 reduce-scatter.25
  4525.6 53.8 all-gather.26
  4604.9 70.5 reduce-scatter.27
  4677.4 53.9 all-gather.28
  4756.6 70.5 reduce-scatter.29
  4828.9 53.9 all-gather.30
  4908.1 70.5 reduce-scatter.31
  4980.8 53.9 all-gather.32
  5041.6 69.9 all-gather.34
where the time goes:
time: 5220 us; the launch traced here: 5140 us
  local copies, waits for them, and re-layouts  3210 us (61%)
  waiting for transfers between devices  926 us (18%)
  matrix products  442 us (8%)
  other arithmetic  379 us (7%)
  blocking collectives  118 us (2%)
    unnamed x558, local copies, waits for them, and re-layouts  2700 us
    reduce_scatter x5, waiting for transfers between devices, gram_of(): lax.psum_scatter(local.astype(jnp.bfloat16), 'mp', scatter_dimension=1, t...  352 us
    all_gather x5, waiting for transfers between devices, gram_of(): return lax.all_gather(summed, 'mp', axis=1, tiled=True)  255 us
    scatter x2, local copies, waits for them, and re-layouts, moe_forward(): jnp.zeros((experts, cap, D), jnp.bfloat16).at[routes, slots].set(normed_low)  143 us
    scatter x2, local copies, waits for them, and re-layouts, moe_backward(): jnp.zeros((experts, cap, D), jnp.bfloat16).at[routes, slots].set(d_rows)  123 us
    all_to_all x7, waiting for transfers between devices, swap_owners(): return lax.all_to_all(buffer, 'dp', split_axis=0, concat_axis=0, tiled=True)  116 us
  transfers between devices with their start and end apart: 30, of which 22 were waited for; matrix products, arithmetic and copies ran while one was open for 65% of the time, Pallas kernels for 0%

commit v1 on v0

v1 whole, which is shorter than its diff:
```python
from functools import partial
import math

import jax
import jax.numpy as jnp
from jax import lax
from jax.experimental import pallas as pl
from jax.experimental.pallas import tpu as pltpu
from jax.sharding import PartitionSpec as P

D = 768
HEADS = 12
HD = 64
FF = 3072
NS_ITERS = 5
STEP = 10


eps_norm = 1e-06
eps_gram = 1e-07
eps_adam = 1e-08
neg_fill = -1000000000.0
coef_a = 3.4445
coef_b = -4.775
coef_c = 2.0315
beta_one = 0.9
beta_two = 0.95
rate_matrix = 0.2
decay_matrix = 0.01
aux_weight = 0.01
enc_edges = (12, 16, 23, 32, 46, 64, 91)
dec_edges = (19, 21, 24, 27, 31, 35, 40, 46, 52, 59, 67, 77, 87, 99, 113)
highest = lax.Precision.HIGHEST


def normalize(rows, gain):
    inverse = lax.rsqrt(jnp.mean(rows * rows, axis=-1, keepdims=True) + eps_norm)
    return (rows * inverse * gain, inverse)


def normalize_back(rows, inverse, gain, grad):
    scaled = grad * gain
    d_rows = inverse * scaled - rows * inverse**3 * jnp.mean(scaled * rows, axis=-1, keepdims=True)
    return (d_rows, jnp.sum(grad * rows * inverse, axis=0))


def bucket_of(relative, causal):
    if causal:
        distance = jnp.maximum(-relative, 0)
        far = 16 + sum(((distance >= edge).astype(jnp.int32) for edge in dec_edges))
        return jnp.where(distance < 16, distance, far)
    distance = jnp.abs(relative)
    far = 8 + sum(((distance >= edge).astype(jnp.int32) for edge in enc_edges))
    return jnp.where(distance < 8, distance, far) + 16 * (relative > 0).astype(jnp.int32)


LANES = 128
CHUNK = 256
VMEM_LIMIT = 60 * 1024 * 1024


def params(count=1, **more):
    return pltpu.CompilerParams(
        dimension_semantics=("arbitrary",) * count, vmem_limit_bytes=VMEM_LIMIT, **more
    )


def dot_nn(left, right):
    return lax.dot_general(
        left, right, (((1,), (0,)), ((), ())), preferred_element_type=jnp.float32
    )


def dot_nt(left, right):
    return lax.dot_general(
        left, right, (((1,), (1,)), ((), ())), preferred_element_type=jnp.float32
    )


def dot_tn(left, right):
    return lax.dot_general(
        left, right, (((0,), (0,)), ((), ())), preferred_element_type=jnp.float32
    )


def own_lanes(rows, half):
    lane = lax.broadcasted_iota(jnp.int32, rows.shape, 1)
    keep = lane >= HD if half else lane < HD
    return jnp.where(keep, rows, jnp.zeros_like(rows))


def band_offsets():
    place = jnp.arange(4 * LANES, dtype=jnp.int32)
    return LANES - jnp.where(place < 3 * LANES, place, place - 4 * LANES)


def bias_parts(table, causal):
    count = table.shape[0]
    hot = (
        bucket_of(band_offsets(), causal)[:, None] == jnp.arange(count, dtype=jnp.int32)[None, :]
    ).astype(jnp.float32)
    band = jnp.dot(hot, table, precision=highest).T[:, None, :]
    ends = bucket_of(jnp.array([-2 * LANES, 2 * LANES], jnp.int32), causal)
    hot_ends = (ends[:, None] == jnp.arange(count, dtype=jnp.int32)[None, :]).astype(jnp.float32)
    far = jnp.dot(hot_ends, table, precision=highest)
    return band, far, hot, hot_ends


def bias_sums(sums, hot, hot_ends):
    per_place = sums[:, 0, :]
    near = per_place[:, : 4 * LANES]
    far = jnp.sum(per_place[:, 4 * LANES :].reshape(-1, 2, LANES), axis=2)
    return jnp.dot(hot.T, near.T, precision=highest) + jnp.dot(
        hot_ends.T, far.T, precision=highest
    )


def scores_of(keys, queries, head, chunk, far_ref, band, causal):
    scores = dot_nt(keys, queries) * HD ** (-0.5)
    len_k, width = scores.shape
    if band is not None:
        rows = []
        for a in range(len_k // LANES):
            columns = []
            for b in range(width // LANES):
                apart = a - (chunk * (width // LANES) + b)
                if apart < -1:
                    bias = far_ref[0, head]
                elif apart > 1:
                    bias = far_ref[1, head]
                else:
                    bias = band[:, LANES * (1 - apart) : LANES * (2 - apart)]
                columns.append(
                    scores[LANES * a : LANES * a + LANES, LANES * b : LANES * b + LANES] + bias
                )
            rows.append(jnp.concatenate(columns, axis=1))
        scores = jnp.concatenate(rows, axis=0)
    if causal:
        allowed = lax.broadcasted_iota(jnp.int32, scores.shape, 0) <= (
            lax.broadcasted_iota(jnp.int32, scores.shape, 1) + chunk * width
        )
        scores = jnp.where(allowed, scores, neg_fill)
    return scores


def band_of(band_ref, half):
    row = jnp.broadcast_to(band_ref[half], (LANES, 4 * LANES))
    return pltpu.roll(row, 0, 1, stride=1, stride_axis=0)


def unband(sums):
    row = lax.broadcasted_iota(jnp.int32, sums.shape, 0)
    step = 1
    while step < LANES:
        sums = jnp.where(
            (row & step) != 0, pltpu.roll(sums, sums.shape[1] - step, 1), sums
        )
        step *= 2
    return jnp.sum(sums, axis=0, keepdims=True)


def attend_kernel(biased, causal, *refs):
    if biased:
        far_ref, band_ref, *refs = refs
    q_ref, k_ref, v_ref, out_ref, lse_ref = refs
    pair = pl.program_id(0)
    keys = k_ref[...]
    values_t = v_ref[...].T
    len_q = q_ref.shape[0]
    width = min(CHUNK, len_q)
    bands = [band_of(band_ref, half) if biased else None for half in range(2)]
    for chunk in range(len_q // width):
        span = pl.ds(chunk * width, width)
        queries = q_ref[span, :]
        parts = []
        for half in range(2):
            scores = scores_of(
                keys,
                own_lanes(queries, half),
                2 * pair + half,
                chunk,
                far_ref if biased else None,
                bands[half],
                causal,
            )
            top = jnp.max(scores, axis=0, keepdims=True)
            expo = jnp.exp(scores - top)
            total = jnp.sum(expo, axis=0, keepdims=True)
            probs = (expo * (1.0 / total)).astype(jnp.bfloat16)
            parts.append(dot_nn(values_t[HD * half : HD * half + HD], probs))
            lse_ref[half, :, span] = top + jnp.log(total)
        out_ref[span, :] = jnp.concatenate(parts, axis=0).T.astype(jnp.bfloat16)


def attend_back_kernel(biased, causal, *refs):
    if biased:
        far_ref, band_ref, *refs = refs
    q_ref, k_ref, v_ref, g_ref, lse_ref, dq_ref, dk_ref, dv_ref, *refs = refs
    if biased:
        sums_ref, dk_acc, dv_acc, near_acc, far_acc = refs
    else:
        dk_acc, dv_acc = refs
    pair = pl.program_id(0)
    keys = k_ref[...]
    keys_t = keys.T
    values = v_ref[...]
    len_q, len_k = q_ref.shape[0], k_ref.shape[0]
    width = min(CHUNK, len_q)
    scale = HD ** (-0.5)
    dk_acc[...] = jnp.zeros_like(dk_acc)
    dv_acc[...] = jnp.zeros_like(dv_acc)
    bands = [band_of(band_ref, half) if biased else None for half in range(2)]
    if biased:
        near_acc[...] = jnp.zeros_like(near_acc)
        far_acc[...] = jnp.zeros_like(far_acc)
    for chunk in range(len_q // width):
        span = pl.ds(chunk * width, width)
        parts = []
        for half in range(2):
            queries = own_lanes(q_ref[span, :], half)
            grads = own_lanes(g_ref[span, :], half)
            scores = scores_of(
                keys,
                queries,
                2 * pair + half,
                chunk,
                far_ref if biased else None,
                bands[half],
                causal,
            )
            probs = jnp.exp(scores - lse_ref[half, :, span])
            d_probs = dot_nt(values, grads)
            delta = jnp.sum(probs * d_probs, axis=0, keepdims=True)
            d_scores = (probs * (d_probs - delta)).astype(jnp.bfloat16)
            dk_acc[...] += dot_nn(d_scores, queries)
            dv_acc[...] += dot_nn(probs.astype(jnp.bfloat16), grads)
            parts.append(dot_nn(keys_t[HD * half : HD * half + HD], d_scores))
            if biased:
                groups = {}
                for a in range(len_k // LANES):
                    for b in range(width // LANES):
                        apart = a - (chunk * (width // LANES) + b)
                        if causal and apart > 0:
                            continue
                        groups.setdefault(max(-2, min(2, apart)), []).append(
                            d_scores[
                                LANES * a : LANES * a + LANES, LANES * b : LANES * b + LANES
                            ].astype(jnp.float32)
                        )
                for apart, blocks in groups.items():
                    total = sum(blocks[1:], blocks[0])
                    if abs(apart) < 2:
                        near_acc[half, :, LANES * (1 - apart) : LANES * (2 - apart)] += total
                    else:
                        side = 0 if apart < 0 else 1
                        far_acc[half, :, LANES * side : LANES * side + LANES] += total
        dq_ref[span, :] = (jnp.concatenate(parts, axis=0).T * scale).astype(jnp.bfloat16)
    dk_ref[...] = (dk_acc[...] * scale).astype(jnp.bfloat16)
    dv_ref[...] = dv_acc[...].astype(jnp.bfloat16)
    if biased:
        for half in range(2):
            sums_ref[half, :, : 4 * LANES] = unband(near_acc[half])
            sums_ref[half, :, 4 * LANES :] = jnp.sum(far_acc[half], axis=0, keepdims=True)


def pair_spec(rows, shift):
    return pl.BlockSpec((rows, LANES), lambda pair, shift=shift: (0, shift + pair))


def row_spec(width):
    return pl.BlockSpec((2, 1, width), lambda pair: (pair, 0, 0))


def attend_cost(len_q, len_k, dots):
    return pl.CostEstimate(
        flops=2 * dots * HEADS * len_q * len_k * HD,
        bytes_accessed=8 * D * (len_q + len_k),
        transcendentals=HEADS * len_q * len_k,
    )


def attend(query, keys, values, parts, causal):
    len_q, len_k = query[0].shape[0], keys[0].shape[0]
    biased = parts is not None
    pairs = D // LANES
    first = [parts[1], parts[0]] if biased else []
    first_specs = [pl.BlockSpec(memory_space=pltpu.SMEM), row_spec(4 * LANES)] if biased else []
    return pl.pallas_call(
        partial(attend_kernel, biased, causal),
        grid=(pairs,),
        in_specs=first_specs
        + [
            pair_spec(len_q, query[1] * pairs),
            pair_spec(len_k, keys[1] * pairs),
            pair_spec(len_k, values[1] * pairs),
        ],
        out_specs=[pair_spec(len_q, 0), row_spec(len_q)],
        out_shape=[
            jax.ShapeDtypeStruct((len_q, D), jnp.bfloat16),
            jax.ShapeDtypeStruct((HEADS, 1, len_q), jnp.float32),
        ],
        compiler_params=params(),
        cost_estimate=attend_cost(len_q, len_k, 2),
    )(*first, query[0], keys[0], values[0])


def attend_back(query, keys, values, parts, causal, logsum, d_mixed):
    len_q, len_k = query[0].shape[0], keys[0].shape[0]
    biased = parts is not None
    pairs = D // LANES
    first = [parts[1], parts[0]] if biased else []
    first_specs = [pl.BlockSpec(memory_space=pltpu.SMEM), row_spec(4 * LANES)] if biased else []
    low = jnp.bfloat16
    return pl.pallas_call(
        partial(attend_back_kernel, biased, causal),
        grid=(pairs,),
        in_specs=first_specs
        + [
            pair_spec(len_q, query[1] * pairs),
            pair_spec(len_k, keys[1] * pairs),
            pair_spec(len_k, values[1] * pairs),
            pair_spec(len_q, 0),
            row_spec(len_q),
        ],
        out_specs=[pair_spec(len_q, 0), pair_spec(len_k, 0), pair_spec(len_k, 0)]
        + ([row_spec(6 * LANES)] if biased else []),
        out_shape=[
            jax.ShapeDtypeStruct((len_q, D), low),
            jax.ShapeDtypeStruct((len_k, D), low),
            jax.ShapeDtypeStruct((len_k, D), low),
        ]
        + ([jax.ShapeDtypeStruct((HEADS, 1, 6 * LANES), jnp.float32)] if biased else []),
        scratch_shapes=[
            pltpu.VMEM((len_k, LANES), jnp.float32),
            pltpu.VMEM((len_k, LANES), jnp.float32),
        ]
        + (
            [
                pltpu.VMEM((2, LANES, 4 * LANES), jnp.float32),
                pltpu.VMEM((2, LANES, 2 * LANES), jnp.float32),
            ]
            if biased
            else []
        ),
        compiler_params=params(),
        cost_estimate=attend_cost(len_q, len_k, 5),
    )(*first, query[0], keys[0], values[0], d_mixed, logsum)


gelu_scale = math.sqrt(2.0 / math.pi)
gelu_cube = 0.044715


def expert_kernel(x_ref, wi_ref, wo_ref, pre_ref, out_ref, acc_ref):
    block = pl.program_id(0)
    pre = dot_nn(x_ref[...], wi_ref[0, 0])
    pre_ref[0] = pre
    bend = jnp.tanh(gelu_scale * (pre + gelu_cube * (pre * pre * pre)))
    hidden = (0.5 * pre * (1.0 + bend)).astype(jnp.bfloat16)
    part = dot_nt(hidden, wo_ref[0, 0])

    @pl.when(block == 0)
    def _():
        acc_ref[...] = part

    @pl.when(block > 0)
    def _():
        acc_ref[...] += part

    @pl.when(block == pl.num_programs(0) - 1)
    def _():
        out_ref[...] = acc_ref[...].astype(jnp.bfloat16)


def expert_forward(arrived, weights):
    rows = arrived.shape[0]
    blocks, unused, unused_too, cols = weights.shape
    whole = pl.BlockSpec((rows, D), lambda j: (0, 0))
    return pl.pallas_call(
        expert_kernel,
        grid=(blocks,),
        in_specs=[
            whole,
            pl.BlockSpec((1, 1, D, cols), lambda j: (j, 0, 0, 0)),
            pl.BlockSpec((1, 1, D, cols), lambda j: (j, 1, 0, 0)),
        ],
        out_specs=[pl.BlockSpec((1, rows, cols), lambda j: (j, 0, 0)), whole],
        out_shape=[
            jax.ShapeDtypeStruct((blocks, rows, cols), jnp.float32),
            jax.ShapeDtypeStruct((rows, D), jnp.bfloat16),
        ],
        scratch_shapes=[pltpu.VMEM((rows, D), jnp.float32)],
        compiler_params=params(),
        cost_estimate=pl.CostEstimate(
            flops=4 * rows * D * FF,
            bytes_accessed=4 * D * FF + 4 * rows * (FF + D),
            transcendentals=rows * FF,
        ),
    )(arrived, weights, weights)


def expert_back_kernel(x_ref, g_ref, pre_ref, wi_ref, wo_ref, dw_ref, back_ref, acc_ref):
    block = pl.program_id(0)
    arrived = x_ref[...]
    grads = g_ref[...]
    pre = pre_ref[0]
    square = pre * pre
    bend = jnp.tanh(gelu_scale * (pre + gelu_cube * (square * pre)))
    half = 0.5 * (1.0 + bend)
    hidden = (pre * half).astype(jnp.bfloat16)
    slope = half + 0.5 * pre * (1.0 - bend * bend) * (
        gelu_scale * (1.0 + 3.0 * gelu_cube * square)
    )
    d_pre = (dot_nn(grads, wo_ref[0, 0]) * slope).astype(jnp.bfloat16)
    dw_ref[0, 0] = dot_tn(arrived, d_pre).astype(jnp.bfloat16)
    dw_ref[0, 1] = dot_tn(grads, hidden).astype(jnp.bfloat16)
    part = dot_nt(d_pre, wi_ref[0, 0])

    @pl.when(block == 0)
    def _():
        acc_ref[...] = part

    @pl.when(block > 0)
    def _():
        acc_ref[...] += part

    @pl.when(block == pl.num_programs(0) - 1)
    def _():
        back_ref[...] = acc_ref[...].astype(jnp.bfloat16)


def expert_backward(arrived, d_arrived, pre, weights):
    rows = arrived.shape[0]
    blocks, unused, unused_too, cols = weights.shape
    whole = pl.BlockSpec((rows, D), lambda j: (0, 0))
    return pl.pallas_call(
        expert_back_kernel,
        grid=(blocks,),
        in_specs=[
            whole,
            whole,
            pl.BlockSpec((1, rows, cols), lambda j: (j, 0, 0)),
            pl.BlockSpec((1, 1, D, cols), lambda j: (j, 0, 0, 0)),
            pl.BlockSpec((1, 1, D, cols), lambda j: (j, 1, 0, 0)),
        ],
        out_specs=[pl.BlockSpec((1, 2, D, cols), lambda j: (j, 0, 0, 0)), whole],
        out_shape=[
            jax.ShapeDtypeStruct((blocks, 2, D, cols), jnp.bfloat16),
            jax.ShapeDtypeStruct((rows, D), jnp.bfloat16),
        ],
        scratch_shapes=[pltpu.VMEM((rows, D), jnp.float32)],
        compiler_params=params(),
        cost_estimate=pl.CostEstimate(
            flops=8 * rows * D * FF,
            bytes_accessed=8 * D * FF + 4 * rows * (FF + 2 * D),
            transcendentals=rows * FF,
        ),
    )(arrived, d_arrived, pre, weights, weights)


def embed_kernel(unroll, ids_ref, table_ref, out_ref, list_ref, count_ref, held, rows, sem):
    chunk = pl.program_id(0)
    vocab = table_ref.shape[0]
    span = out_ref.shape[0]

    @pl.when(chunk == 0)
    def _():
        copy = pltpu.make_async_copy(table_ref, held.at[pl.ds(0, vocab)], sem)
        copy.start()
        held[pl.ds(vocab, 8), :] = jnp.zeros((8, D), jnp.float32)
        copy.wait()

    def some(step, found):
        for inner in range(unroll):
            row = step * unroll + inner
            source = ids_ref[chunk * span + row]
            rows[pl.ds(row, 1), :] = held[pl.ds(source, 1), :]
            list_ref[chunk * span + found] = row
            found = found + (source < vocab).astype(jnp.int32)
        return found

    count_ref[chunk] = lax.fori_loop(0, span // unroll, some, jnp.int32(0))
    out_ref[...] = rows[...].astype(jnp.bfloat16)


def embed(ids, table, span):
    count = ids.shape[0]
    vocab = table.shape[0]
    smem = pl.BlockSpec(memory_space=pltpu.SMEM)
    return pl.pallas_call(
        partial(embed_kernel, 8),
        grid=(count // span,),
        in_specs=[smem, pl.BlockSpec(memory_space=pl.ANY)],
        out_specs=[pl.BlockSpec((span, D), lambda j: (j, 0)), smem, smem],
        out_shape=[
            jax.ShapeDtypeStruct((count, D), jnp.bfloat16),
            jax.ShapeDtypeStruct((count,), jnp.int32),
            jax.ShapeDtypeStruct((count // span,), jnp.int32),
        ],
        scratch_shapes=[
            pltpu.VMEM((vocab + 8, D), jnp.float32),
            pltpu.VMEM((span, D), jnp.float32),
            pltpu.SemaphoreType.DMA,
        ],
        compiler_params=params(),
        cost_estimate=pl.CostEstimate(
            flops=0, bytes_accessed=4 * vocab * D + 2 * count * D, transcendentals=0
        ),
    )(ids, table)


def unembed_kernel(
    ids_ref, list_ref, count_ref, first_ref, enc_ref, dec_ref, out_ref, total, rows, sem
):
    chunk = pl.program_id(0)
    span = rows.shape[0]
    enc_rows = enc_ref.shape[1]

    @pl.when(chunk == 0)
    def _():
        copy = pltpu.make_async_copy(first_ref, total, sem)
        copy.start()
        copy.wait()

    rows[pl.ds(0, enc_rows), :] = enc_ref[0].astype(jnp.float32)
    rows[pl.ds(enc_rows, span - enc_rows), :] = dec_ref[0].astype(jnp.float32)

    def one(step, carry):
        row = list_ref[chunk * span + step]
        place = ids_ref[chunk * span + row]
        total[pl.ds(place, 1), :] += rows[pl.ds(row, 1), :]
        return carry

    lax.fori_loop(0, count_ref[chunk], one, 0)

    @pl.when(chunk == pl.num_programs(0) - 1)
    def _():
        out_ref[...] = total[...].astype(jnp.bfloat16)


def unembed(ids, listed, counts, first, enc, dec):
    chunks, enc_rows, unused = enc.shape
    dec_rows = dec.shape[1]
    vocab = first.shape[0]
    smem = pl.BlockSpec(memory_space=pltpu.SMEM)
    return pl.pallas_call(
        unembed_kernel,
        grid=(chunks,),
        in_specs=[
            smem,
            smem,
            smem,
            pl.BlockSpec(memory_space=pl.ANY),
            pl.BlockSpec((1, enc_rows, D), lambda j: (j, 0, 0)),
            pl.BlockSpec((1, dec_rows, D), lambda j: (j, 0, 0)),
        ],
        out_specs=pl.BlockSpec((vocab, D), lambda j: (0, 0)),
        out_shape=jax.ShapeDtypeStruct((vocab, D), jnp.bfloat16),
        scratch_shapes=[
            pltpu.VMEM((vocab, D), jnp.float32),
            pltpu.VMEM((enc_rows + dec_rows, D), jnp.float32),
            pltpu.SemaphoreType.DMA,
        ],
        compiler_params=params(),
        cost_estimate=pl.CostEstimate(
            flops=0,
            bytes_accessed=6 * vocab * D + 2 * chunks * (enc_rows + dec_rows) * D,
            transcendentals=0,
        ),
    )(ids, listed, counts, first, enc, dec)


def newton_kernel(x_ref, out_ref, gram_ref, poly_ref):
    blocks = x_ref.shape[1] // D

    def gram(source):
        for j in range(blocks):
            part = source[:, D * j : D * j + D]
            product = dot_nt(part, part)
            if j:
                gram_ref[...] += product
            else:
                gram_ref[...] = product

    gram(x_ref)
    row = lax.broadcasted_iota(jnp.int32, (D, D), 0)
    column = lax.broadcasted_iota(jnp.int32, (D, D), 1)
    whole = gram_ref[...].astype(jnp.bfloat16).astype(jnp.float32)
    scale = jnp.sum(jnp.where(row == column, whole, 0.0), keepdims=True) + eps_gram
    root = lax.rsqrt(scale)
    inverse = 1.0 / scale

    def step(source, factor, outer):
        product = gram_ref[...].astype(jnp.bfloat16)
        if factor is not None:
            product = (product.astype(jnp.float32) * factor).astype(jnp.bfloat16)
        poly_ref[...] = (
            coef_b * product.astype(jnp.float32) + coef_c * dot_nn(product, product)
        ).astype(jnp.bfloat16)
        for j in range(blocks):
            part = source[:, D * j : D * j + D]
            fresh = coef_a * part.astype(jnp.float32) + dot_nn(poly_ref[...], part)
            if outer is not None:
                fresh = fresh * outer
            out_ref[:, D * j : D * j + D] = fresh.astype(jnp.bfloat16)

    step(x_ref, inverse, root)

    def turn(index, carry):
        gram(out_ref)
        step(out_ref, None, None)
        return carry

    lax.fori_loop(1, NS_ITERS, turn, 0)


def newton(matrix):
    cols = matrix.shape[1]
    vmem = pl.BlockSpec(memory_space=pltpu.VMEM)
    return pl.pallas_call(
        newton_kernel,
        in_specs=[vmem],
        out_specs=vmem,
        out_shape=jax.ShapeDtypeStruct(matrix.shape, jnp.bfloat16),
        scratch_shapes=[pltpu.VMEM((D, D), jnp.float32), pltpu.VMEM((D, D), jnp.bfloat16)],
        compiler_params=pltpu.CompilerParams(vmem_limit_bytes=VMEM_LIMIT),
        cost_estimate=pl.CostEstimate(
            flops=NS_ITERS * (4 * D * D * cols + 2 * D * D * D),
            bytes_accessed=4 * D * cols,
            transcendentals=0,
        ),
    )(matrix)


def project(rows, stored):
    flat = stored.reshape(-1, D)
    return dot_nt(rows, flat)


def swap_owners(buffer):
    return lax.all_to_all(buffer, "dp", split_axis=0, concat_axis=0, tiled=True)


def dispatch(places, count):
    slot = lax.broadcasted_iota(jnp.int32, (count, places.shape[0]), 0)
    return (slot == places[None, :]).astype(jnp.bfloat16)


def route_places(routes, experts, cap):
    hot = (routes[:, None] == jnp.arange(experts, dtype=jnp.int32)[None, :]).astype(jnp.float32)
    rows = routes.shape[0]
    earlier = (
        lax.broadcasted_iota(jnp.int32, (rows, rows), 1)
        < lax.broadcasted_iota(jnp.int32, (rows, rows), 0)
    ).astype(jnp.bfloat16)
    ranks = dot_nn(earlier, hot.astype(jnp.bfloat16))
    slots = jnp.sum(hot * ranks, axis=1).astype(jnp.int32)
    return hot, routes * cap + slots


def moe_forward(resid, gain, router, weights, hot, places, cap):
    experts = router.shape[1]
    normed, inverse = normalize(resid, gain)
    normed_low = normed.astype(jnp.bfloat16)
    probs = jax.nn.softmax(
        jnp.dot(normed_low.astype(jnp.float32), router, precision=highest), axis=-1
    )
    spread = dispatch(places, experts * cap)
    buffer = dot_nn(spread, normed_low).astype(jnp.bfloat16)
    arrived = swap_owners(buffer.reshape(experts, cap, D)).reshape(-1, D)
    pre, result = expert_forward(arrived, weights)
    returned = swap_owners(result.reshape(experts, cap, D)).reshape(-1, D)
    outputs = dot_tn(spread, returned)
    gate = jnp.sum(probs * hot, axis=1)
    kept = (normed_low, inverse, probs, gate, arrived, pre, outputs)
    return (resid + gate[:, None] * outputs, kept)


def moe_backward(resid, gain, router, weights, hot, places, cap, kept, grad, aux_scale, frac):
    normed_low, inverse, probs, gate, arrived, pre, outputs = kept
    experts = router.shape[1]
    d_gate = jnp.sum(grad * outputs, axis=1)
    d_rows = (gate[:, None] * grad).astype(jnp.bfloat16)
    spread = dispatch(places, experts * cap)
    buffer = dot_nn(spread, d_rows).astype(jnp.bfloat16)
    d_arrived = swap_owners(buffer.reshape(experts, cap, D)).reshape(-1, D)
    d_weights, d_back = expert_backward(arrived, d_arrived, pre, weights)
    returned = swap_owners(d_back.reshape(experts, cap, D)).reshape(-1, D)
    d_normed = dot_tn(spread, returned)
    d_probs = hot * d_gate[:, None] + aux_scale * frac[None, :]
    d_logits = probs * (d_probs - jnp.sum(probs * d_probs, axis=-1, keepdims=True))
    d_router = jnp.dot(normed_low.astype(jnp.float32).T, d_logits, precision=highest)
    d_normed = d_normed + jnp.dot(d_logits, router.T, precision=highest)
    d_resid, d_gain = normalize_back(resid, inverse, gain, d_normed)
    return (grad + d_resid, d_gain, d_router, d_weights)


def self_forward(resid, gain, weights, parts, causal):
    normed, inverse = normalize(resid, gain)
    normed = normed.astype(jnp.bfloat16)
    joined = project(normed, weights[0:3]).astype(jnp.bfloat16)
    mixed, logsum = attend((joined, 0), (joined, 1), (joined, 2), parts, causal)
    return (resid + project(mixed, weights[3]), (resid, inverse, normed, joined, mixed, logsum))


def self_backward(gain, weights, parts, causal, kept, grad):
    resid, inverse, normed, joined, mixed, logsum = kept
    grad_low = grad.astype(jnp.bfloat16)
    d_mixed = dot_nn(grad_low, weights[3]).astype(jnp.bfloat16)
    d_query, d_key, d_value, sums = attend_back(
        (joined, 0), (joined, 1), (joined, 2), parts, causal, logsum, d_mixed
    )
    d_normed = (
        dot_nn(d_query, weights[0]) + dot_nn(d_key, weights[1]) + dot_nn(d_value, weights[2])
    )
    d_weights = [
        dot_tn(d_query, normed),
        dot_tn(d_key, normed),
        dot_tn(d_value, normed),
        dot_tn(grad_low, mixed),
    ]
    d_resid, d_gain = normalize_back(resid, inverse, gain, d_normed)
    return (grad + d_resid, d_gain, d_weights, bias_sums(sums, parts[2], parts[3]))


def cross_forward(resid, gain, weights, memory):
    normed, inverse = normalize(resid, gain)
    normed = normed.astype(jnp.bfloat16)
    query = project(normed, weights[0]).astype(jnp.bfloat16)
    joined = project(memory, weights[1:3]).astype(jnp.bfloat16)
    mixed, logsum = attend((query, 0), (joined, 0), (joined, 1), None, False)
    kept = (resid, inverse, normed, query, joined, mixed, logsum)
    return (resid + project(mixed, weights[3]), kept)


def cross_backward(gain, weights, memory, kept, grad):
    resid, inverse, normed, query, joined, mixed, logsum = kept
    grad_low = grad.astype(jnp.bfloat16)
    d_mixed = dot_nn(grad_low, weights[3]).astype(jnp.bfloat16)
    d_query, d_key, d_value = attend_back(
        (query, 0), (joined, 0), (joined, 1), None, False, logsum, d_mixed
    )
    d_normed = dot_nn(d_query, weights[0])
    d_memory = dot_nn(d_key, weights[1]) + dot_nn(d_value, weights[2])
    d_weights = [
        dot_tn(d_query, normed),
        dot_tn(d_key, memory),
        dot_tn(d_value, memory),
        dot_tn(grad_low, mixed),
    ]
    d_resid, d_gain = normalize_back(resid, inverse, gain, d_normed)
    return (grad + d_resid, d_gain, d_weights, d_memory)


def route_share(routes, experts):
    flat_routes = routes.reshape(-1)
    hot = (flat_routes[None, :] == jnp.arange(experts, dtype=jnp.int32)[:, None]).astype(
        jnp.float32
    )
    return jnp.sum(hot, axis=1) / flat_routes.shape[0]


def adam(weight, first, second, grad, rate, decay):
    first = beta_one * first + (1 - beta_one) * grad
    second = beta_two * second + (1 - beta_two) * grad * grad
    update = first / (1 - beta_one**STEP) / (jnp.sqrt(second / (1 - beta_two**STEP)) + eps_adam)
    return (weight - rate * (update + decay * weight), first, second)


def share_columns(d_weights, groups):
    stacked = jnp.stack([part.astype(jnp.bfloat16) for part in d_weights])
    count = stacked.shape[0]
    split = jnp.transpose(stacked.reshape(count, groups, -1, D), (1, 0, 2, 3))
    return lax.psum_scatter(split, "mp", scatter_dimension=0, tiled=False)


def orthogonalize(dense_mom, expert_mom, groups):
    cols = expert_mom.shape[2]
    cols_dense = dense_mom.shape[1]
    split = D // cols
    count_expert, count_dense = expert_mom.shape[0], dense_mom.shape[0]
    depth = cols_dense * split
    frames = jnp.transpose(
        dense_mom.astype(jnp.bfloat16).reshape(count_dense, cols_dense, split, cols), (0, 2, 1, 3)
    ).reshape(count_dense, depth, cols)
    frames = jnp.pad(frames, ((0, 0), (0, D - depth), (0, 0)))
    spare = groups - count_expert - count_dense
    sent = jnp.concatenate(
        [expert_mom.astype(jnp.bfloat16), frames, jnp.zeros((spare, D, cols), jnp.bfloat16)],
        axis=0,
    )
    arrived = lax.all_to_all(sent, "mp", split_axis=0, concat_axis=0, tiled=True)
    whole = jnp.transpose(arrived, (1, 0, 2)).reshape(D, groups * cols)
    square = jnp.transpose(
        arrived[:, :depth].reshape(groups, split, cols_dense, cols), (0, 2, 1, 3)
    ).reshape(D, D)
    square = jnp.pad(square, ((0, 0), (0, groups * cols - D)))
    is_expert = lax.axis_index("mp") < count_expert
    result = newton(jnp.where(is_expert, whole, square))
    back_expert = jnp.transpose(result.reshape(D, groups, cols), (1, 0, 2))
    back_dense = jnp.transpose(
        result[:, :D].reshape(groups, cols_dense, split, cols), (0, 2, 1, 3)
    ).reshape(groups, depth, cols)
    back_dense = jnp.pad(back_dense, ((0, 0), (0, D - depth), (0, 0)))
    returned = lax.all_to_all(
        jnp.where(is_expert, back_expert, back_dense),
        "mp",
        split_axis=0,
        concat_axis=0,
        tiled=True,
    )
    dense_orth = jnp.transpose(
        returned[count_expert : count_expert + count_dense, :depth].reshape(
            count_dense, split, cols_dense, cols
        ),
        (0, 2, 1, 3),
    ).reshape(count_dense, cols_dense, D)
    return dense_orth, returned[:count_expert]


def on_device(
    src_ids,
    targets,
    loss_pos,
    loss_mask,
    routes_src,
    routes_tgt,
    dense_w,
    dense_m,
    expert_w,
    expert_m,
    table_w,
    table_m,
    table_v,
    gains_w,
    gains_m,
    gains_v,
    router_w,
    router_m,
    router_v,
    bias_w,
    bias_m,
    bias_v,
):
    groups = lax.axis_size("mp")
    column = lax.axis_index("mp")
    experts = lax.axis_size("dp")
    src_len = src_ids.shape[1]
    tgt_len = targets.shape[1]
    npos = loss_pos.shape[1]
    vocab_dev = table_w.shape[0]
    own_seq = lax.axis_index("dp") * groups + column
    rows_dev = src_len + tgt_len
    count_dense = dense_w.shape[0]
    low = jnp.bfloat16
    dense_local = dense_w.astype(low).reshape(count_dense, -1, D)
    enc_dense = lax.all_gather(dense_local[0:4], "mp", axis=1, tiled=True)
    expert_local = expert_w[:, :, 0].astype(low)
    dec_ids = jnp.concatenate(
        [jnp.zeros((targets.shape[0], 1), jnp.int32), targets[:, :-1]], axis=1
    )
    all_ids = jnp.concatenate([src_ids, dec_ids], axis=1).reshape(-1)
    local_ids = all_ids - column * vocab_dev
    inside = (local_ids >= 0) & (local_ids < vocab_dev)
    local_ids = jnp.where(inside, local_ids, vocab_dev)
    shared, listed, counts = embed(local_ids, table_w, rows_dev)
    embedded = lax.psum_scatter(shared, "mp", scatter_dimension=0, tiled=True).astype(jnp.float32)
    enc_expert = lax.all_gather(expert_local[0], "mp", axis=0, tiled=False)
    dec_dense = lax.all_gather(dense_local[4:12], "mp", axis=1, tiled=True)
    dec_expert = lax.all_gather(expert_local[1], "mp", axis=0, tiled=False)
    table_low = table_w.astype(low)
    own_src = lax.dynamic_slice_in_dim(routes_src, own_seq, 1, 0).reshape(-1)
    own_tgt = lax.dynamic_slice_in_dim(routes_tgt, own_seq, 1, 0).reshape(-1)
    cap_src = (5 * src_len + 4 * experts - 1) // (4 * experts)
    cap_tgt = (5 * tgt_len + 4 * experts - 1) // (4 * experts)
    total_src = routes_src.shape[0] * routes_src.shape[1]
    total_tgt = routes_tgt.shape[0] * routes_tgt.shape[1]
    frac_src = route_share(routes_src, experts)
    frac_tgt = route_share(routes_tgt, experts)
    hot_src, places_src = route_places(own_src, experts, cap_src)
    hot_tgt, places_tgt = route_places(own_tgt, experts, cap_tgt)
    enc_parts = bias_parts(bias_w[0], False)
    dec_parts = bias_parts(bias_w[1], True)
    enc_mid, enc_kept = self_forward(embedded[:src_len], gains_w[0], enc_dense, enc_parts, False)
    dec_mid, dec_kept = self_forward(
        embedded[src_len:], gains_w[3], dec_dense[0:4], dec_parts, True
    )
    enc_out, enc_moe = moe_forward(
        enc_mid, gains_w[1], router_w[0], enc_expert, hot_src, places_src, cap_src
    )
    memory_float, memory_inv = normalize(enc_out, gains_w[2])
    memory = memory_float.astype(low)
    dec_crossed, cross_kept = cross_forward(dec_mid, gains_w[4], dec_dense[4:8], memory)
    dec_result, dec_moe = moe_forward(
        dec_crossed, gains_w[5], router_w[1], dec_expert, hot_tgt, places_tgt, cap_tgt
    )
    final_float, final_inv = normalize(dec_result, gains_w[6])
    final_low = final_float.astype(low)
    head_scale = D ** (-0.5)
    own_pos = lax.dynamic_slice_in_dim(loss_pos, column, 1, 0).reshape(-1)
    pick = (
        own_pos[:, None] == lax.broadcasted_iota(jnp.int32, (npos, tgt_len), 1)
    ).astype(low)
    chosen = dot_nn(pick, final_low).astype(low)
    gathered = lax.all_gather(chosen, "mp", axis=0, tiled=True)
    logits = dot_nt(gathered, table_low) * head_scale
    wanted = jnp.take_along_axis(targets, loss_pos, axis=1).reshape(-1) - column * vocab_dev
    hits = jnp.arange(vocab_dev, dtype=jnp.int32)[None, :] == wanted[:, None]
    top = jnp.max(logits, axis=1)
    stats = lax.all_gather(
        jnp.stack(
            [
                top,
                jnp.sum(jnp.exp(logits - top[:, None]), axis=1),
                jnp.sum(jnp.where(hits, logits, 0.0), axis=1),
            ]
        ),
        "mp",
        axis=0,
        tiled=False,
    )
    all_top = jnp.max(stats[:, 0], axis=0)
    expsum = jnp.sum(stats[:, 1] * jnp.exp(stats[:, 0] - all_top[None, :]), axis=0)
    picked = jnp.sum(stats[:, 2], axis=0)
    logsum = all_top + jnp.log(expsum)
    mask_rows = loss_mask.reshape(-1).astype(jnp.float32)
    own_loss = jnp.sum(
        lax.dynamic_slice_in_dim(mask_rows * (logsum - picked), column * npos, npos)
    )
    own_count = jnp.sum(lax.dynamic_slice_in_dim(mask_rows, column * npos, npos))
    d_logits = (
        mask_rows[:, None] * (jnp.exp(logits - logsum[:, None]) - hits.astype(jnp.float32))
    ).astype(low)
    d_shares = lax.all_to_all(
        (dot_nn(d_logits, table_low) * head_scale).astype(low).reshape(groups, npos, D),
        "mp",
        split_axis=0,
        concat_axis=0,
        tiled=True,
    )
    table_grad = dot_tn(d_logits, gathered) * head_scale
    d_chosen = jnp.sum(d_shares.astype(jnp.float32), axis=0).astype(low)
    d_final = dot_tn(pick, d_chosen)
    d_dec, gain_final = normalize_back(dec_result, final_inv, gains_w[6], d_final)
    d_dec, gain_dec_moe, dec_router, dec_dw = moe_backward(
        dec_crossed,
        gains_w[5],
        router_w[1],
        dec_expert,
        hot_tgt,
        places_tgt,
        cap_tgt,
        dec_moe,
        d_dec,
        aux_weight * experts / total_tgt,
        frac_tgt,
    )
    dec_share = lax.psum_scatter(dec_dw, "mp", scatter_dimension=0, tiled=False)
    d_dec, gain_cross, cross_dw, d_memory = cross_backward(
        gains_w[4], dec_dense[4:8], memory, cross_kept, d_dec
    )
    d_enc, gain_memory = normalize_back(enc_out, memory_inv, gains_w[2], d_memory)
    d_dec, gain_self, self_dw, dec_bias = self_backward(
        gains_w[3], dec_dense[0:4], dec_parts, True, dec_kept, d_dec
    )
    dec_rows = lax.all_gather(d_dec.astype(low), "mp", axis=0, tiled=False)
    dec_cols = share_columns(self_dw + cross_dw, groups)
    d_enc, gain_enc_moe, enc_router, enc_dw = moe_backward(
        enc_mid,
        gains_w[1],
        router_w[0],
        enc_expert,
        hot_src,
        places_src,
        cap_src,
        enc_moe,
        d_enc,
        aux_weight * experts / total_src,
        frac_src,
    )
    enc_share = lax.psum_scatter(enc_dw, "mp", scatter_dimension=0, tiled=False)
    d_enc, gain_enc, enc_self_dw, enc_bias = self_backward(
        gains_w[0], enc_dense, enc_parts, False, enc_kept, d_enc
    )
    enc_rows = lax.all_gather(d_enc.astype(low), "mp", axis=0, tiled=False)
    enc_cols = share_columns(enc_self_dw, groups)
    table_sum = unembed(local_ids, listed, counts, table_grad, enc_rows, dec_rows)
    table_piece = lax.psum_scatter(table_sum, "dp", scatter_dimension=0, tiled=True).astype(
        jnp.float32
    )
    dense_share = jnp.concatenate([enc_cols, dec_cols], axis=0)
    per_dev = -(-count_dense // experts)
    filler = per_dev * experts - count_dense
    dense_piece = lax.psum_scatter(
        jnp.pad(dense_share, ((0, filler), (0, 0), (0, 0))),
        "dp",
        scatter_dimension=0,
        tiled=True,
    ).astype(jnp.float32)
    expert_share = jnp.stack([enc_share, dec_share]).astype(jnp.float32)
    gains_grad = jnp.stack(
        [gain_enc, gain_enc_moe, gain_memory, gain_self, gain_cross, gain_dec_moe, gain_final]
    )
    router_grad = jnp.stack([enc_router, dec_router])
    bias_grad = jnp.stack([enc_bias, dec_bias])
    load_src = jnp.sum(enc_moe[2], axis=0)
    load_tgt = jnp.sum(dec_moe[2], axis=0)
    gains_grad, router_grad, bias_grad, loss_sum, count, load_src, load_tgt = lax.psum(
        (gains_grad, router_grad, bias_grad, own_loss, own_count, load_src, load_tgt),
        ("dp", "mp"),
    )
    squares = (
        jnp.sum(dense_piece * dense_piece)
        + jnp.sum(expert_share * expert_share)
        + jnp.sum(table_piece * table_piece)
    )
    squares = lax.psum(squares, ("dp", "mp"))
    squares = squares + sum(
        (jnp.sum(part * part) for part in (gains_grad, router_grad, bias_grad))
    )
    grad_norm = jnp.sqrt(squares)
    clip = 1.0 / jnp.maximum(grad_norm, 1.0)
    aux = (
        aux_weight
        * experts
        * (jnp.sum(frac_src * load_src) / total_src + jnp.sum(frac_tgt * load_tgt) / total_tgt)
    )
    loss = jnp.stack([loss_sum + aux, count])
    old_piece = lax.dynamic_slice_in_dim(
        jnp.pad(dense_m, ((0, filler), (0, 0))), lax.axis_index("dp") * per_dev, per_dev, 0
    ).reshape(per_dev, -1, D)
    piece_moment = 0.5 * old_piece + clip * dense_piece
    expert_moment = 0.5 * expert_m + clip * expert_share[:, :, None]
    moment_flat = lax.all_gather(piece_moment.astype(low), "dp", axis=0, tiled=True)[:count_dense]
    dense_moment = moment_flat.reshape(count_dense, -1).astype(jnp.float32)
    cols = expert_w.shape[4]
    piece_orth, expert_orth = orthogonalize(
        piece_moment, expert_moment.reshape(-1, D, cols), groups
    )
    dense_orth = lax.all_gather(piece_orth, "dp", axis=0, tiled=True)[:count_dense]
    dense_orth = dense_orth.reshape(count_dense, -1).astype(jnp.float32)
    keep_rate = 1 - rate_matrix * decay_matrix
    dense_new = dense_w * keep_rate - rate_matrix * 0.2 * math.sqrt(D) * dense_orth
    expert_new = expert_w * keep_rate - rate_matrix * 0.2 * math.sqrt(
        max(D, FF)
    ) * expert_orth.astype(jnp.float32).reshape(expert_w.shape)
    piece_rows = table_m.shape[0]
    table_clipped = clip * table_piece
    table_new, table_first, table_second = adam(
        lax.dynamic_slice_in_dim(table_w, lax.axis_index("dp") * piece_rows, piece_rows, 0),
        table_m,
        table_v,
        table_clipped,
        1.5,
        0.01,
    )

    def part_of(array, like):
        size = like.shape[1]
        return lax.dynamic_slice_in_dim(array, column * size, size, 1)

    gains_new, gains_first, gains_second = adam(
        part_of(gains_w, gains_m), gains_m, gains_v, clip * part_of(gains_grad, gains_m), 0.5, 0.0
    )
    router_new, router_first, router_second = adam(
        part_of(router_w, router_m),
        router_m,
        router_v,
        clip * part_of(router_grad, router_m),
        0.02,
        0.01,
    )
    bias_new, bias_first, bias_second = adam(
        part_of(bias_w, bias_m), bias_m, bias_v, clip * part_of(bias_grad, bias_m), 0.5, 0.0
    )
    return (
        loss,
        grad_norm,
        dense_new,
        dense_moment,
        dense_new.astype(low),
        expert_new,
        expert_moment,
        expert_new.astype(low),
        table_new,
        table_clipped,
        table_second,
        gains_new,
        gains_first,
        gains_second,
        router_new,
        router_first,
        router_second,
        bias_new,
        bias_first,
        bias_second,
    )


def solution(mesh):
    in_specs = (
        P("dp", None),
        P("dp", None),
        P("dp", None),
        P("dp", None),
        P(),
        P(),
        P(None, "mp"),
        P(None, "mp"),
        P(None, None, "dp", None, "mp"),
        P(None, None, "dp", None, "mp"),
        P("mp", None),
        P(("mp", "dp"), None),
        P(("mp", "dp"), None),
        P(),
        P(None, "mp"),
        P(None, "mp"),
        P(),
        P(None, "mp", None),
        P(None, "mp", None),
        P(),
        P(None, "mp", None),
        P(None, "mp", None),
    )
    out_specs = (
        P(),
        P(),
        P(None, "mp"),
        P(None, "mp"),
        P(None, "mp"),
        P(None, None, "dp", None, "mp"),
        P(None, None, "dp", None, "mp"),
        P(None, None, "dp", None, "mp"),
        P(("mp", "dp"), None),
        P(("mp", "dp"), None),
        P(("mp", "dp"), None),
        P(None, "mp"),
        P(None, "mp"),
        P(None, "mp"),
        P(None, "mp", None),
        P(None, "mp", None),
        P(None, "mp", None),
        P(None, "mp", None),
        P(None, "mp", None),
        P(None, "mp", None),
    )
    return jax.shard_map(
        on_device, mesh=mesh, in_specs=in_specs, out_specs=out_specs, check_vma=False
    )
```

time: 5220 us -> 1600 us (0.31); the launches traced: 5140 us -> 1580 us
  local copies, waits for them, and re-layouts: 3210 us -> 77.4 us
  Pallas kernels: 0 us -> 319 us
  matrix products: 442 us -> 151 us
  other arithmetic: 379 us -> 108 us
  waiting for transfers between devices: 926 us -> 668 us
  blocking collectives: 118 us -> 184 us
    unnamed x558 -> x332, local copies, waits for them, and re-layouts: 2700 us -> 36.3 us
    pallas_call x0 -> x13, Pallas kernels: none -> 319 us  [the longest x1 62.3 us: embed(): pl.pallas_call(partial(embed_kernel, 8), grid=(count // span,), in_specs=...]
    dot_general x103 -> x54, matrix products: 429 us -> 140 us  [the longest x20 55.1 us: dot_nn(): lax.dot_general(left, right, (((1,), (0,)), ((), ())), preferred_element_...]
    reduce_scatter x7 -> x4, waiting for transfers between devices: 392 us -> 108 us  [the longest x1 82.7 us: on_device(): lax.psum_scatter(shared, 'mp', scatter_dimension=0, tiled=True)]
    scatter x4 -> x0, local copies, waits for them, and re-layouts: 266 us -> none  [the longest x2 143 us: moe_forward(): jnp.zeros((experts, cap, D), jnp.bfloat16).at[routes, slots].set(normed_low)]
    unnamed x27 -> x16, waiting for transfers between devices: 52.7 us -> 190 us
    all_gather x10 -> x8, waiting for transfers between devices: 304 us -> 169 us  [the longest x1 61.2 us: on_device(): enc_rows = lax.all_gather(d_enc.astype(low), 'mp', axis=0, tiled=False)]
    all_to_all x0 -> x2, waiting for transfers between devices: none -> 102 us  [the longest x1 53.1 us: orthogonalize(): lax.all_to_all(sent, 'mp', split_axis=0, concat_axis=0, tiled=True)]
  transfers between devices with their start and end apart: 30 -> 25, of which waited for: 22 -> 18; matrix products, arithmetic and copies ran while one was open for 65% -> 19% of each run, Pallas kernels for 0% -> 10%
where the time goes in v1:
time: 1600 us; the launch traced here: 1580 us
  waiting for transfers between devices  668 us (42%)
  Pallas kernels  319 us (20%)
  blocking collectives  184 us (12%)
  matrix products  151 us (9%)
  other arithmetic  108 us (7%)
  local copies, waits for them, and re-layouts  77.4 us (5%)
  starting transfers between devices  49.8 us (3%)
  between operations  24.9 us (2%)
    unnamed x16, waiting for transfers between devices  190 us
    unnamed x1, blocking collectives  110 us
    all_to_all x8, waiting for transfers between devices, swap_owners(): return lax.all_to_all(buffer, 'dp', split_axis=0, concat_axis=0, tiled=True)  87.9 us
    reduce_scatter x1, waiting for transfers between devices, on_device(): lax.psum_scatter(shared, 'mp', scatter_dimension=0, tiled=True)  82.7 us
    pallas_call x1, Pallas kernels, embed(): pl.pallas_call(partial(embed_kernel, 8), grid=(count // span,), in_specs=...  62.3 us
    all_gather x1, waiting for transfers between devices, on_device(): enc_rows = lax.all_gather(d_enc.astype(low), 'mp', axis=0, tiled=False)  61.2 us
    all_gather x1, waiting for transfers between devices, on_device(): enc_expert = lax.all_gather(expert_local[0], 'mp', axis=0, tiled=False)  57 us
    dot_general x20, matrix products, dot_nn(): lax.dot_general(left, right, (((1,), (0,)), ((), ())), preferred_element_...  55.1 us
  transfers between devices with their start and end apart: 25, of which 18 were waited for; matrix products, arithmetic and copies ran while one was open for 19% of the time, Pallas kernels for 10%

profile of v1, /device:TPU:2, one launch (start us, length us, event | category | flops | bytes accessed | tf_op | source)
XLA Modules:
  0.0 1581.6 jit_solution(69666189666172256)
XLA Ops:
  11.7 62.3 %shard_map.383 = (bf16[8192,768]{1,0:T(8,128)(2,1)}, s32[8192]{0:T(1024)}, s32[8]{0:T(128)}) custom-call(s32[8192]{0:T(1024)} %bitcast_select_fusion.ids_ref, f32[4016,768]{1,0:T(8,128)} %table_ref.1), custom_call_target="tpu_custom_call" | custom-call | bytes 24920064 | tf_op jit(solution)/shard_map/pallas_call | solution.py:490
  84.9 82.7 %reduce-scatter.13.cloned.1.call-done = bf16[1024,768]{1,0:T(8,128)(2,1)} async-done(((bf16[8192,768]{1,0:T(8,128)(2,1)}), bf16[1024,768]{1,0:T(8,128)(2,1)}) %reduce-scatter.13.cloned.1.call-update) | async-done | bytes 1572880 | tf_op jit(solution)/shard_map/reduce_scatter | solution.py:867
  176.4 26.4 %shard_map.385 = (bf16[768,768]{1,0:T(8,128)(2,1)}, f32[12,1,768]{2,1,0:T(1,128)}) custom-call(f32[2,12]{1,0:T(2,128)} %fusion.90.refs_0_, f32[12,1,512]{2,1,0:T(1,128)} %broadcast_in_dim.15.refs_1_, bf16[768,2304]{1,0:T(8,128)(2,1)} %convolution_convert_fusion.refs_2_.refs_3_.refs_4_, bf16[768,2304]{1,0:T(8,128)(2,1)} %convolution_convert_fusion.refs_2_.refs_3_.refs_4_, ...), custom_call_target="tpu_custom_call" | custom-call | flops 1811939328 | bytes 9437184 | tf_op jit(solution)/shard_map/pallas_call | solution.py:288
  233.3 57.0 %all-gather.26.cloned.1.call-done = bf16[8,2,1,768,384]{4,3,2,1,0:T(8,128)(2,1)} async-done(((bf16[1,2,1,768,384]{4,3,2,1,0:T(8,128)(2,1)}), bf16[8,2,1,768,384]{4,3,2,1,0:T(8,128)(2,1)}) %all-gather.26.cloned.1.call-update) | async-done | bytes 9437200 | tf_op jit(solution)/shard_map/all_gather | solution.py:868
  290.3 20.5 %shard_map.386 = (f32[8,960,384]{2,1,0:T(8,128)}, bf16[960,768]{1,0:T(8,128)(2,1)}) custom-call(bf16[960,768]{1,0:T(8,128)(2,1)} %bitcast.13.x_ref, bf16[8,2,768,384]{3,2,1,0:T(8,128)(2,1)} %bitcast.413, bf16[8,2,768,384]{3,2,1,0:T(8,128)(2,1)} %bitcast.414), custom_call_target="tpu_custom_call" | custom-call | flops 9059696640 | bytes 24182784 | tf_op jit(solution)/shard_map/pallas_call | solution.py:379
  336.8 14.2 all-to-all-done.1
  484.7 15.2 multiply_convert_fusion.1
  499.9 24.3 %all_to_all.55 = bf16[8,128,768]{2,1,0:T(8,128)(2,1)} all-to-all(bf16[8,128,768]{2,1,0:T(8,128)(2,1)S(1)} %bitcast.381), channel_id=1, replica_groups=mesh['dp'=4,'mp'=8] {'mp'}, dimensions={0} | all-to-all | bytes 3145728 | tf_op jit(solution)/shard_map/all_to_all | solution.py:934
  551.9 16.9 %shard_map.389 = (bf16[8,2,768,384]{3,2,1,0:T(8,128)(2,1)}, bf16[320,768]{1,0:T(8,128)(2,1)}) custom-call(bf16[320,768]{1,0:T(8,128)(2,1)} %bitcast.24.x_ref, bf16[320,768]{1,0:T(8,128)(2,1)} %bitcast.41.g_ref, f32[8,320,384]{2,1,0:T(8,128)} %get-tuple-element.54.pre_ref, bf16[8,2,768,384]{3,2,1,0:T(8,128)(2,1)} %bitcast.337, bf16[8,2,768,384]{3,2,1,0:T(8,128)(2,1)} %bitcast.338), custom_call_target="tpu_custom_call" | custom-call | flops 6039797760 | bytes 24772608 | tf_op jit(solution)/shard_map/pallas_call | solution.py:436
  656.2 34.3 %shard_map.391 = (bf16[8,2,768,384]{3,2,1,0:T(8,128)(2,1)}, bf16[960,768]{1,0:T(8,128)(2,1)}) custom-call(bf16[960,768]{1,0:T(8,128)(2,1)} %bitcast.13.x_ref, bf16[960,768]{1,0:T(8,128)(2,1)} %bitcast.47.g_ref, f32[8,960,384]{2,1,0:T(8,128)} %get-tuple-element.59.pre_ref, bf16[8,2,768,384]{3,2,1,0:T(8,128)(2,1)} %bitcast.415, bf16[8,2,768,384]{3,2,1,0:T(8,128)(2,1)} %bitcast.416), custom_call_target="tpu_custom_call" | custom-call | flops 18119393280 | bytes 36569088 | tf_op jit(solution)/shard_map/pallas_call | solution.py:436
  708.8 20.6 %all-to-all-done.8 = bf16[4,240,768]{2,1,0:T(8,128)(2,1)} async-done(((bf16[4,240,768]{2,1,0:T(8,128)(2,1)}), bf16[4,240,768]{2,1,0:T(8,128)(2,1)}, u32[]{:S(2)}, u32[]{:S(2)}) %all-to-all-start.8) | async-done | bytes 1474592 | tf_op jit(solution)/shard_map/all_to_all | solution.py:641
  742.0 29.8 %shard_map.392 = (bf16[768,768]{1,0:T(8,128)(2,1)}, bf16[768,768]{1,0:T(8,128)(2,1)}, bf16[768,768]{1,0:T(8,128)(2,1)}, f32[12,1,768]{2,1,0:T(1,128)}) custom-call(f32[2,12]{1,0:T(2,128)} %fusion.90.refs_0_, f32[12,1,512]{2,1,0:T(1,128)} %broadcast_in_dim.15.refs_1_, bf16[768,2304]{1,0:T(8,128)(2,1)} %convolution_convert_fusion.refs_2_.refs_3_.refs_4_, ...), custom_call_target="tpu_custom_call" | custom-call | flops 4529848320 | bytes 9437184 | tf_op jit(solution)/shard_map/pallas_call | solution.py:314
  781.0 186.9 %all-reduce.11.cloned.1.call-done = (bf16[8,8,96,768]{3,2,0,1:T(8,128)(2,1)}, bf16[8,4,96,768]{3,2,0,1:T(8,128)(2,1)}) async-done(((bf16[8,8,96,768]{3,2,0,1:T(8,128)(2,1)}, bf16[8,4,96,768]{3,2,0,1:T(8,128)(2,1)}), (bf16[8,8,96,768]{3,2,0,1:T(8,128)(2,1)}, bf16[8,4,96,768]{3,2,0,1:T(8,128)(2,1)})) %all-reduce.11.cloned.1.call-update) | async-done | bytes 14155792
  999.7 16.0 %convolution_multiply_fusion.first_ref = f32[4016,768]{1,0:T(8,128)} fusion(bf16[1024,768]{1,0:T(8,128)(2,1)S(1)} %copy-done.140, f32[1024,4016]{0,1:T(8,128)} %get-tuple-element.342, f32[1024]{0:T(1024)S(1)} %copy-done.120, f32[1024]{0:T(1024)S(1)} %copy-done.118, s32[1024]{0:T(1024)S(1)} %copy-done.96), kind=kOutput, calls=%fused_computation.10 | convolution fusion | flops 6348492800 | bytes 30371840 | tf_op jit(solution)/shard_map/dot_general | solution.py:81
  1020.5 25.2 %all-gather.32.cloned.1.call-done = bf16[2048,768]{1,0:T(8,128)(2,1)} async-done(((bf16[256,768]{1,0:T(8,128)(2,1)}), bf16[2048,768]{1,0:T(8,128)(2,1)}) %all-gather.32.cloned.1.call-update) | async-done | bytes 3145744 | tf_op jit(solution)/shard_map/all_gather | solution.py:966
  1045.6 61.2 %all-gather.30.cloned.1.call-done = bf16[6144,768]{1,0:T(8,128)(2,1)} async-done(((bf16[768,768]{1,0:T(8,128)(2,1)}), bf16[6144,768]{1,0:T(8,128)(2,1)}) %all-gather.30.cloned.1.call-update) | async-done | bytes 9437200 | tf_op jit(solution)/shard_map/all_gather | solution.py:985
  1106.8 23.6 %shard_map.394 = bf16[4016,768]{1,0:T(8,128)(2,1)} custom-call(s32[8192]{0:T(1024)} %bitcast_select_fusion.ids_ref, s32[8192]{0:T(1024)} %get-tuple-element.72.list_ref, s32[8]{0:T(128)} %get-tuple-element.73.count_ref, f32[4016,768]{1,0:T(8,128)} %convolution_multiply_fusion.first_ref, bf16[8,768,768]{2,1,0:T(8,128)(2,1)} %bitcast.349, ...), custom_call_target="tpu_custom_call" | custom-call | bytes 31088640 | tf_op jit(solution)/shard_map/pallas_call | solution.py:546
  1130.4 109.6 %fusion = bf16[1008,768]{1,0:T(8,128)(2,1)S(1)} fusion(bf16[4016,768]{1,0:T(8,128)(2,1)} %shard_map.394), kind=kCustom, calls=%all-reduce-scatter | all-reduce-scatter fusion | flops 3096577 | bytes 7717376
  1241.5 25.1 %reduce-scatter.17.cloned.1.call-done = bf16[1,2,768,384]{3,2,1,0:T(8,128)(2,1)} async-done(((bf16[8,2,768,384]{3,2,1,0:T(8,128)(2,1)}), bf16[1,2,768,384]{3,2,1,0:T(8,128)(2,1)}) %reduce-scatter.17.cloned.1.call-update) | async-done | bytes 1179664 | tf_op jit(solution)/shard_map/reduce_scatter | solution.py:981
  1276.3 41.8 %all-reduce.7 = (f32[]{:T(128)}, f32[7,768]{1,0:T(8,128)S(1)}, f32[2,768,4]{1,2,0:T(4,128)S(1)}, f32[2,32,12]{2,1,0:T(8,128)S(1)}, f32[1]{0:T(128)}, /*index=5*/f32[]{:T(128)}, f32[4]{0:T(128)S(1)}, f32[4]{0:T(128)S(1)}) all-reduce(f32[]{:T(128)S(6)} %add.696, f32[7,768]{1,0:T(8,128)S(1)} %stack.143, ...), channel_id=1, replica_groups=mesh['dp'=4,'mp'=8] {'dp','mp'}, use_global_device_ids=true, to_apply=%region_55.56 | all-reduce | flops 12299 | bytes 98392 | tf_op jit(solution)/shard_map/psum | solution.py:1017
  1337.2 53.1 %all-to-all-done.9 = bf16[8,768,384]{2,1,0:T(8,128)(2,1)} async-done(((bf16[8,768,384]{2,1,0:T(8,128)(2,1)}), bf16[8,768,384]{2,1,0:T(8,128)(2,1)}, u32[]{:S(2)}, u32[]{:S(2)}) %all-to-all-start.9) | async-done | bytes 4718624 | tf_op jit(solution)/shard_map/all_to_all | solution.py:792
  1399.5 54.5 %shard_map.395 = bf16[768,3072]{1,0:T(8,128)(2,1)} custom-call(bf16[768,3072]{1,0:T(8,128)(2,1)} %pad_select_fusion.x_ref), custom_call_target="tpu_custom_call" | custom-call | flops 40768634880 | bytes 9437184 | tf_op jit(solution)/shard_map/pallas_call | solution.py:620
  1473.8 49.1 %all-to-all-done.10 = bf16[8,768,384]{2,1,0:T(8,128)(2,1)} async-done(((bf16[8,768,384]{2,1,0:T(8,128)(2,1)}), bf16[8,768,384]{2,1,0:T(8,128)(2,1)}, u32[]{:S(2)}, u32[]{:S(2)}) %all-to-all-start.10) | async-done | bytes 4718624 | tf_op jit(solution)/shard_map/all_to_all | solution.py:805
  1550.2 14.8 all-gather.22.cloned.1.call-done
  (585 shorter events, 491.4 us)
Async XLA Ops:
  7.2 77.8 %all-gather.18.cloned.1.call-start = ((), (), s32[]{:S(2)}) async-start(), calls=%async_computation.17 | async-start | bytes 5308416 | tf_op jit(solution)/shard_map/all_gather | solution.py:857
  10.9 156.8 %reduce-scatter.13.cloned.1.call-start = ((), (), s32[]{:S(2)}) async-start(), calls=%async_computation.15 | async-start | bytes 14155776 | tf_op jit(solution)/shard_map/reduce_scatter | solution.py:867
  74.0 155.1 %all-gather.16.cloned.1.call-start = ((), (), s32[]{:S(2)}) async-start(), calls=%async_computation.16 | async-start | bytes 10616832 | tf_op jit(solution)/shard_map/all_gather | solution.py:869
  75.7 214.7 %all-gather.26.cloned.1.call-start = ((), (), s32[]{:S(2)}) async-start(), calls=%async_computation.24 | async-start | bytes 10616832 | tf_op jit(solution)/shard_map/all_gather | solution.py:868
  80.0 302.9 %all-gather.28.cloned.1.call-start = ((), (), s32[]{:S(2)}) async-start(), calls=%async_computation.25 | async-start | bytes 10616832 | tf_op jit(solution)/shard_map/all_gather | solution.py:870
  209.1 81.2 %all-to-all-start = ((bf16[4,240,768]{2,1,0:T(8,128)(2,1)}), bf16[4,240,768]{2,1,0:T(8,128)(2,1)}, u32[]{:S(2)}, u32[]{:S(2)}) async-start(bf16[4,240,768]{2,1,0:T(8,128)(2,1)} %bitcast.385), calls=%async_computation.1 | async-start | bytes 2949120 | tf_op jit(solution)/shard_map/all_to_all | solution.py:641
  310.9 40.1 %all-to-all-start.1 = ((bf16[4,240,768]{2,1,0:T(8,128)(2,1)}), bf16[4,240,768]{2,1,0:T(8,128)(2,1)}, u32[]{:S(2)}, u32[]{:S(2)}) async-start(bf16[4,240,768]{2,1,0:T(8,128)(2,1)} %bitcast.384), calls=%async_computation.2 | async-start | bytes 2949120 | tf_op jit(solution)/shard_map/all_to_all | solution.py:641
  378.4 18.0 %all-to-all-start.2 = ((bf16[4,80,768]{2,1,0:T(8,128)(2,1)}), bf16[4,80,768]{2,1,0:T(8,128)(2,1)}, u32[]{:S(2)}, u32[]{:S(2)}) async-start(bf16[4,80,768]{2,1,0:T(8,128)(2,1)} %bitcast.376), calls=%async_computation.3 | async-start | bytes 983040 | tf_op jit(solution)/shard_map/all_to_all | solution.py:641
  407.8 17.6 %all-to-all-start.3 = ((bf16[4,80,768]{2,1,0:T(8,128)(2,1)}), bf16[4,80,768]{2,1,0:T(8,128)(2,1)}, u32[]{:S(2)}, u32[]{:S(2)}) async-start(bf16[4,80,768]{2,1,0:T(8,128)(2,1)} %bitcast.392), calls=%async_computation.4 | async-start | bytes 983040 | tf_op jit(solution)/shard_map/all_to_all | solution.py:641
  412.1 42.1 %all-gather.20.cloned.1.call-start = ((), (), s32[]{:S(2)}) async-start(), calls=%async_computation.18 | async-start | bytes 1769472 | tf_op jit(solution)/shard_map/all_gather | solution.py:905
  533.3 18.6 %all-to-all-start.5 = ((bf16[4,80,768]{2,1,0:T(8,128)(2,1)}), bf16[4,80,768]{2,1,0:T(8,128)(2,1)}, u32[]{:S(2)}, u32[]{:S(2)}) async-start(bf16[4,80,768]{2,1,0:T(8,128)(2,1)} %bitcast.377), calls=%async_computation.6 | async-start | bytes 983040 | tf_op jit(solution)/shard_map/all_to_all | solution.py:641
  617.1 39.1 %all-to-all-start.7 = ((bf16[4,240,768]{2,1,0:T(8,128)(2,1)}), bf16[4,240,768]{2,1,0:T(8,128)(2,1)}, u32[]{:S(2)}, u32[]{:S(2)}) async-start(bf16[4,240,768]{2,1,0:T(8,128)(2,1)} %bitcast.383), calls=%async_computation.8 | async-start | bytes 2949120 | tf_op jit(solution)/shard_map/all_to_all | solution.py:641
  690.5 38.9 %all-to-all-start.8 = ((bf16[4,240,768]{2,1,0:T(8,128)(2,1)}), bf16[4,240,768]{2,1,0:T(8,128)(2,1)}, u32[]{:S(2)}, u32[]{:S(2)}) async-start(bf16[4,240,768]{2,1,0:T(8,128)(2,1)} %bitcast.382), calls=%async_computation.9 | async-start | bytes 2949120 | tf_op jit(solution)/shard_map/all_to_all | solution.py:641
  695.0 272.9 %all-reduce.11.cloned.1.call-start = ((), (), s32[]{:S(2)}) async-start(), calls=%async_computation.28 | async-start | bytes 28311552
  779.8 238.9 %reduce-scatter.15.cloned.1.call-start = ((), (), s32[]{:S(2)}) async-start(), calls=%async_computation.19 | async-start | bytes 2211840 | tf_op jit(solution)/shard_map/reduce_scatter | solution.py:994
  973.1 72.6 %all-gather.32.cloned.1.call-start = ((), (), s32[]{:S(2)}) async-start(), calls=%async_computation.27 | async-start | bytes 3538944 | tf_op jit(solution)/shard_map/all_gather | solution.py:966
  980.5 126.3 %all-gather.30.cloned.1.call-start = ((), (), s32[]{:S(2)}) async-start(), calls=%async_computation.26 | async-start | bytes 10616832 | tf_op jit(solution)/shard_map/all_gather | solution.py:985
  991.1 250.5 %reduce-scatter.19.cloned.1.call-start = ((), (), s32[]{:S(2)}) async-start(), calls=%async_computation.21 | async-start | bytes 10616832 | tf_op jit(solution)/shard_map/reduce_scatter | solution.py:958
  991.8 274.8 %reduce-scatter.17.cloned.1.call-start = ((), (), s32[]{:S(2)}) async-start(), calls=%async_computation.20 | async-start | bytes 10616832 | tf_op jit(solution)/shard_map/reduce_scatter | solution.py:981
  1240.0 31.3 %collective-permute-start = (bf16[12,768]{1,0:T(8,128)(2,1)S(1)}, bf16[12,768]{1,0:T(8,128)(2,1)S(1)}, u32[]{:S(2)}, u32[]{:S(2)}) collective-permute-start(bf16[12,768]{1,0:T(8,128)(2,1)S(1)} %slice.254), channel_id=1, source_target_pairs={{0,8},{8,16},{16,24},{1,9},{9,17},{17,25},{2,10},{10,18},{18,26},{... | collective-permute-start | bytes 55304
  1332.6 57.7 %all-to-all-start.9 = ((bf16[8,768,384]{2,1,0:T(8,128)(2,1)}), bf16[8,768,384]{2,1,0:T(8,128)(2,1)}, u32[]{:S(2)}, u32[]{:S(2)}) async-start(bf16[8,768,384]{2,1,0:T(8,128)(2,1)} %fusion.4), calls=%async_computation.13 | async-start | bytes 9437184 | tf_op jit(solution)/shard_map/all_to_all | solution.py:792
  1463.4 59.5 %all-to-all-start.10 = ((bf16[8,768,384]{2,1,0:T(8,128)(2,1)}), bf16[8,768,384]{2,1,0:T(8,128)(2,1)}, u32[]{:S(2)}, u32[]{:S(2)}) async-start(bf16[8,768,384]{2,1,0:T(8,128)(2,1)} %fusion.5), calls=%async_computation.14 | async-start | bytes 9437184 | tf_op jit(solution)/shard_map/all_to_all | solution.py:805
  1469.7 67.8 %all-gather.24.cloned.1.call-start = ((), (), s32[]{:S(2)}) async-start(), calls=%async_computation.23 | async-start | bytes 2211840 | tf_op jit(solution)/shard_map/all_gather | solution.py:1034
  1470.4 94.5 %all-gather.22.cloned.1.call-start = ((), (), s32[]{:S(2)}) async-start(), calls=%async_computation.22 | async-start | bytes 2211840 | tf_op jit(solution)/shard_map/all_gather | solution.py:1040
  (159 other events, 1828.0 us)
Sparse Core Ops, SparseCore 0:
  11.0 40.1 all-gather.17
  74.2 93.4 reduce-scatter.12
  170.2 58.9 all-gather.15
  231.5 58.8 all-gather.25
  292.1 58.8 all-gather.27
  430.3 23.8 all-gather.19
  779.9 187.9 all-reduce.10
  973.2 38.4 reduce-scatter.14
  1014.2 31.4 all-gather.31
  1047.9 58.8 all-gather.29
  1110.3 76.3 reduce-scatter.18
  1190.1 76.4 reduce-scatter.16
  1472.6 40.1 all-gather.23
  1525.6 39.3 all-gather.21

commit v2 on v1

--- a/solution.py
+++ b/solution.py
@@ -55,7 +55,10 @@
 
 
 LANES = 128
-CHUNK = 256
+CHUNK = 768
+WIDE = 768
+FETCH = 128
+GIVE = 48
 VMEM_LIMIT = 60 * 1024 * 1024
 
 
@@ -116,7 +119,7 @@
 
 
 def scores_of(keys, queries, head, chunk, far_ref, band, causal):
-    scores = dot_nt(keys, queries) * HD ** (-0.5)
+    scores = dot_nt(keys, queries)
     len_k, width = scores.shape
     if band is not None:
         rows = []
@@ -171,7 +174,7 @@
     bands = [band_of(band_ref, half) if biased else None for half in range(2)]
     for chunk in range(len_q // width):
         span = pl.ds(chunk * width, width)
-        queries = q_ref[span, :]
+        queries = q_ref[span, :] * HD ** (-0.5)
         parts = []
         for half in range(2):
             scores = scores_of(
@@ -186,8 +189,8 @@
             top = jnp.max(scores, axis=0, keepdims=True)
             expo = jnp.exp(scores - top)
             total = jnp.sum(expo, axis=0, keepdims=True)
-            probs = (expo * (1.0 / total)).astype(jnp.bfloat16)
-            parts.append(dot_nn(values_t[HD * half : HD * half + HD], probs))
+            mixed = dot_nn(values_t[HD * half : HD * half + HD], expo.astype(jnp.bfloat16))
+            parts.append(mixed * (1.0 / total))
             lse_ref[half, :, span] = top + jnp.log(total)
         out_ref[span, :] = jnp.concatenate(parts, axis=0).T.astype(jnp.bfloat16)
 
@@ -217,7 +220,7 @@
         span = pl.ds(chunk * width, width)
         parts = []
         for half in range(2):
-            queries = own_lanes(q_ref[span, :], half)
+            queries = own_lanes(q_ref[span, :] * HD ** (-0.5), half)
             grads = own_lanes(g_ref[span, :], half)
             scores = scores_of(
                 keys,
@@ -255,7 +258,7 @@
                         side = 0 if apart < 0 else 1
                         far_acc[half, :, LANES * side : LANES * side + LANES] += total
         dq_ref[span, :] = (jnp.concatenate(parts, axis=0).T * scale).astype(jnp.bfloat16)
-    dk_ref[...] = (dk_acc[...] * scale).astype(jnp.bfloat16)
+    dk_ref[...] = dk_acc[...].astype(jnp.bfloat16)
     dv_ref[...] = dv_acc[...].astype(jnp.bfloat16)
     if biased:
         for half in range(2):
@@ -351,13 +354,17 @@
 gelu_cube = 0.044715
 
 
+def side_by_side(ref):
+    return jnp.concatenate([ref[j, 0] for j in range(ref.shape[0])], axis=1)
+
+
 def expert_kernel(x_ref, wi_ref, wo_ref, pre_ref, out_ref, acc_ref):
     block = pl.program_id(0)
-    pre = dot_nn(x_ref[...], wi_ref[0, 0])
+    pre = dot_nn(x_ref[...], side_by_side(wi_ref))
     pre_ref[0] = pre
     bend = jnp.tanh(gelu_scale * (pre + gelu_cube * (pre * pre * pre)))
     hidden = (0.5 * pre * (1.0 + bend)).astype(jnp.bfloat16)
-    part = dot_nt(hidden, wo_ref[0, 0])
+    part = dot_nt(hidden, side_by_side(wo_ref))
 
     @pl.when(block == 0)
     def _():
@@ -375,18 +382,19 @@
 def expert_forward(arrived, weights):
     rows = arrived.shape[0]
     blocks, unused, unused_too, cols = weights.shape
+    per = WIDE // cols
     whole = pl.BlockSpec((rows, D), lambda j: (0, 0))
     return pl.pallas_call(
         expert_kernel,
-        grid=(blocks,),
+        grid=(blocks // per,),
         in_specs=[
             whole,
-            pl.BlockSpec((1, 1, D, cols), lambda j: (j, 0, 0, 0)),
-            pl.BlockSpec((1, 1, D, cols), lambda j: (j, 1, 0, 0)),
+            pl.BlockSpec((per, 1, D, cols), lambda j: (j, 0, 0, 0)),
+            pl.BlockSpec((per, 1, D, cols), lambda j: (j, 1, 0, 0)),
         ],
-        out_specs=[pl.BlockSpec((1, rows, cols), lambda j: (j, 0, 0)), whole],
+        out_specs=[pl.BlockSpec((1, rows, WIDE), lambda j: (j, 0, 0)), whole],
         out_shape=[
-            jax.ShapeDtypeStruct((blocks, rows, cols), jnp.float32),
+            jax.ShapeDtypeStruct((blocks // per, rows, WIDE), jnp.float32),
             jax.ShapeDtypeStruct((rows, D), jnp.bfloat16),
         ],
         scratch_shapes=[pltpu.VMEM((rows, D), jnp.float32)],
@@ -411,10 +419,14 @@
     slope = half + 0.5 * pre * (1.0 - bend * bend) * (
         gelu_scale * (1.0 + 3.0 * gelu_cube * square)
     )
-    d_pre = (dot_nn(grads, wo_ref[0, 0]) * slope).astype(jnp.bfloat16)
-    dw_ref[0, 0] = dot_tn(arrived, d_pre).astype(jnp.bfloat16)
-    dw_ref[0, 1] = dot_tn(grads, hidden).astype(jnp.bfloat16)
-    part = dot_nt(d_pre, wi_ref[0, 0])
+    d_pre = (dot_nn(grads, side_by_side(wo_ref)) * slope).astype(jnp.bfloat16)
+    d_in = dot_tn(arrived, d_pre).astype(jnp.bfloat16)
+    d_out = dot_tn(grads, hidden).astype(jnp.bfloat16)
+    cols = dw_ref.shape[3]
+    for j in range(dw_ref.shape[0]):
+        dw_ref[j, 0] = d_in[:, cols * j : cols * j + cols]
+        dw_ref[j, 1] = d_out[:, cols * j : cols * j + cols]
+    part = dot_nt(d_pre, side_by_side(wi_ref))
 
     @pl.when(block == 0)
     def _():
@@ -432,18 +444,19 @@
 def expert_backward(arrived, d_arrived, pre, weights):
     rows = arrived.shape[0]
     blocks, unused, unused_too, cols = weights.shape
+    per = WIDE // cols
     whole = pl.BlockSpec((rows, D), lambda j: (0, 0))
     return pl.pallas_call(
         expert_back_kernel,
-        grid=(blocks,),
+        grid=(blocks // per,),
         in_specs=[
             whole,
             whole,
-            pl.BlockSpec((1, rows, cols), lambda j: (j, 0, 0)),
-            pl.BlockSpec((1, 1, D, cols), lambda j: (j, 0, 0, 0)),
-            pl.BlockSpec((1, 1, D, cols), lambda j: (j, 1, 0, 0)),
+            pl.BlockSpec((1, rows, WIDE), lambda j: (j, 0, 0)),
+            pl.BlockSpec((per, 1, D, cols), lambda j: (j, 0, 0, 0)),
+            pl.BlockSpec((per, 1, D, cols), lambda j: (j, 1, 0, 0)),
         ],
-        out_specs=[pl.BlockSpec((1, 2, D, cols), lambda j: (j, 0, 0, 0)), whole],
+        out_specs=[pl.BlockSpec((per, 2, D, cols), lambda j: (j, 0, 0, 0)), whole],
         out_shape=[
             jax.ShapeDtypeStruct((blocks, 2, D, cols), jnp.bfloat16),
             jax.ShapeDtypeStruct((rows, D), jnp.bfloat16),
@@ -458,178 +471,594 @@
     )(arrived, d_arrived, pre, weights, weights)
 
 
-def embed_kernel(unroll, ids_ref, table_ref, out_ref, list_ref, count_ref, held, rows, sem):
-    chunk = pl.program_id(0)
-    vocab = table_ref.shape[0]
-    span = out_ref.shape[0]
-
-    @pl.when(chunk == 0)
-    def _():
-        copy = pltpu.make_async_copy(table_ref, held.at[pl.ds(0, vocab)], sem)
-        copy.start()
-        held[pl.ds(vocab, 8), :] = jnp.zeros((8, D), jnp.float32)
-        copy.wait()
-
-    def some(step, found):
-        for inner in range(unroll):
-            row = step * unroll + inner
-            source = ids_ref[chunk * span + row]
-            rows[pl.ds(row, 1), :] = held[pl.ds(source, 1), :]
-            list_ref[chunk * span + found] = row
-            found = found + (source < vocab).astype(jnp.int32)
-        return found
-
-    count_ref[chunk] = lax.fori_loop(0, span // unroll, some, jnp.int32(0))
-    out_ref[...] = rows[...].astype(jnp.bfloat16)
-
-
-def embed(ids, table, span):
-    count = ids.shape[0]
-    vocab = table.shape[0]
-    smem = pl.BlockSpec(memory_space=pltpu.SMEM)
-    return pl.pallas_call(
-        partial(embed_kernel, 8),
-        grid=(count // span,),
-        in_specs=[smem, pl.BlockSpec(memory_space=pl.ANY)],
-        out_specs=[pl.BlockSpec((span, D), lambda j: (j, 0)), smem, smem],
-        out_shape=[
-            jax.ShapeDtypeStruct((count, D), jnp.bfloat16),
-            jax.ShapeDtypeStruct((count,), jnp.int32),
-            jax.ShapeDtypeStruct((count // span,), jnp.int32),
-        ],
-        scratch_shapes=[
-            pltpu.VMEM((vocab + 8, D), jnp.float32),
-            pltpu.VMEM((span, D), jnp.float32),
-            pltpu.SemaphoreType.DMA,
-        ],
-        compiler_params=params(),
-        cost_estimate=pl.CostEstimate(
-            flops=0, bytes_accessed=4 * vocab * D + 2 * count * D, transcendentals=0
-        ),
-    )(ids, table)
-
-
-def unembed_kernel(
-    ids_ref, list_ref, count_ref, first_ref, enc_ref, dec_ref, out_ref, total, rows, sem
-):
-    chunk = pl.program_id(0)
-    span = rows.shape[0]
-    enc_rows = enc_ref.shape[1]
-
-    @pl.when(chunk == 0)
-    def _():
-        copy = pltpu.make_async_copy(first_ref, total, sem)
-        copy.start()
-        copy.wait()
-
-    rows[pl.ds(0, enc_rows), :] = enc_ref[0].astype(jnp.float32)
-    rows[pl.ds(enc_rows, span - enc_rows), :] = dec_ref[0].astype(jnp.float32)
-
-    def one(step, carry):
-        row = list_ref[chunk * span + step]
-        place = ids_ref[chunk * span + row]
-        total[pl.ds(place, 1), :] += rows[pl.ds(row, 1), :]
-        return carry
-
-    lax.fori_loop(0, count_ref[chunk], one, 0)
-
-    @pl.when(chunk == pl.num_programs(0) - 1)
-    def _():
-        out_ref[...] = total[...].astype(jnp.bfloat16)
-
-
-def unembed(ids, listed, counts, first, enc, dec):
-    chunks, enc_rows, unused = enc.shape
-    dec_rows = dec.shape[1]
-    vocab = first.shape[0]
-    smem = pl.BlockSpec(memory_space=pltpu.SMEM)
-    return pl.pallas_call(
-        unembed_kernel,
-        grid=(chunks,),
-        in_specs=[
-            smem,
-            smem,
-            smem,
-            pl.BlockSpec(memory_space=pl.ANY),
-            pl.BlockSpec((1, enc_rows, D), lambda j: (j, 0, 0)),
-            pl.BlockSpec((1, dec_rows, D), lambda j: (j, 0, 0)),
-        ],
-        out_specs=pl.BlockSpec((vocab, D), lambda j: (0, 0)),
-        out_shape=jax.ShapeDtypeStruct((vocab, D), jnp.bfloat16),
-        scratch_shapes=[
-            pltpu.VMEM((vocab, D), jnp.float32),
-            pltpu.VMEM((enc_rows + dec_rows, D), jnp.float32),
-            pltpu.SemaphoreType.DMA,
-        ],
-        compiler_params=params(),
-        cost_estimate=pl.CostEstimate(
-            flops=0,
-            bytes_accessed=6 * vocab * D + 2 * chunks * (enc_rows + dec_rows) * D,
-            transcendentals=0,
-        ),
-    )(ids, listed, counts, first, enc, dec)
-
-
-def newton_kernel(x_ref, out_ref, gram_ref, poly_ref):
-    blocks = x_ref.shape[1] // D
-
-    def gram(source):
-        for j in range(blocks):
-            part = source[:, D * j : D * j + D]
-            product = dot_nt(part, part)
-            if j:
-                gram_ref[...] += product
-            else:
-                gram_ref[...] = product
-
-    gram(x_ref)
+def mirror(left, right, store):
+    tile = 2 * LANES
+    for a in range(0, D, tile):
+        block = dot_nt(left[a : a + tile, :], right[: a + tile, :])
+        store(slice(a, a + tile), slice(0, a + tile), block)
+        if a:
+            store(slice(0, a), slice(a, a + tile), block[:, :a].T)
+
+
+def newton_gram(source, gram_ref):
+    def keep(rows, columns, block):
+        gram_ref[rows, columns] = block
+
+    mirror(source, source, keep)
+
+
+def newton_poly(product, poly_ref):
+    def keep(rows, columns, block):
+        poly_ref[rows, columns] = (
+            coef_b * product[rows, columns].astype(jnp.float32) + coef_c * block
+        ).astype(jnp.bfloat16)
+
+    mirror(product, product, keep)
+
+
+def newton_apply(source, poly_ref, j, outer):
+    part = source[:, D * j : D * j + D]
+    fresh = coef_a * part.astype(jnp.float32) + dot_nn(poly_ref[...], part)
+    if outer is not None:
+        fresh = fresh * outer
+    source[:, D * j : D * j + D] = fresh.astype(jnp.bfloat16)
+
+
+def newton_rounds(source, gram_ref, poly_ref, between, finish):
+    blocks = source.shape[1] // D
+    newton_gram(source, gram_ref)
     row = lax.broadcasted_iota(jnp.int32, (D, D), 0)
     column = lax.broadcasted_iota(jnp.int32, (D, D), 1)
     whole = gram_ref[...].astype(jnp.bfloat16).astype(jnp.float32)
     scale = jnp.sum(jnp.where(row == column, whole, 0.0), keepdims=True) + eps_gram
-    root = lax.rsqrt(scale)
-    inverse = 1.0 / scale
-
-    def step(source, factor, outer):
-        product = gram_ref[...].astype(jnp.bfloat16)
-        if factor is not None:
-            product = (product.astype(jnp.float32) * factor).astype(jnp.bfloat16)
-        poly_ref[...] = (
-            coef_b * product.astype(jnp.float32) + coef_c * dot_nn(product, product)
-        ).astype(jnp.bfloat16)
+    newton_poly((whole * (1.0 / scale)).astype(jnp.bfloat16), poly_ref)
+    for j in range(blocks):
+        newton_apply(source, poly_ref, j, lax.rsqrt(scale))
+
+    def turn(index, carry):
+        newton_gram(source, gram_ref)
+        newton_poly(gram_ref[...].astype(jnp.bfloat16), poly_ref)
         for j in range(blocks):
-            part = source[:, D * j : D * j + D]
-            fresh = coef_a * part.astype(jnp.float32) + dot_nn(poly_ref[...], part)
-            if outer is not None:
-                fresh = fresh * outer
-            out_ref[:, D * j : D * j + D] = fresh.astype(jnp.bfloat16)
-
-    step(x_ref, inverse, root)
-
-    def turn(index, carry):
-        gram(out_ref)
-        step(out_ref, None, None)
+            newton_apply(source, poly_ref, j, None)
         return carry
 
-    lax.fori_loop(1, NS_ITERS, turn, 0)
-
-
-def newton(matrix):
-    cols = matrix.shape[1]
+    lax.fori_loop(1, NS_ITERS - 1, turn, 0)
+    between()
+    newton_gram(source, gram_ref)
+    newton_poly(gram_ref[...].astype(jnp.bfloat16), poly_ref)
+    for j in range(blocks):
+        newton_apply(source, poly_ref, j, None)
+        finish(j)
+
+
+def newton_kernel(
+    groups,
+    experts,
+    expert_ref,
+    dense_ref,
+    expert_out,
+    dense_out,
+    moment_out,
+    held,
+    held_dense,
+    matrix,
+    square,
+    gram_ref,
+    poly_ref,
+    land_expert,
+    land_dense,
+    all_dense,
+    all_moment,
+    send_sem,
+    in_sem,
+    back_send_sem,
+    back_sem,
+    orth_send_sem,
+    orth_sem,
+    moment_send_sem,
+    moment_sem,
+):
+    me = lax.axis_index("mp")
+    along = lax.axis_index("dp")
+    own = me // 2
+    count_expert, count_dense = expert_ref.shape[0], dense_ref.shape[0]
+    cols, cols_dense = expert_ref.shape[2], dense_ref.shape[1]
+    is_expert = ((me % 2) == 0) & (own < count_expert)
+    is_dense = ((me % 2) == 1) & (own < count_dense)
+    per = D // cols
+    barrier = pltpu.get_barrier_semaphore()
+    for step in range(1, groups):
+        other = lax.rem(me + step, groups)
+        pl.semaphore_signal(
+            barrier, inc=1, device_id={"mp": other}, device_id_type=pl.DeviceIdType.MESH
+        )
+    for step in range(1, experts):
+        other = lax.rem(along + step, experts)
+        pl.semaphore_signal(
+            barrier, inc=1, device_id={"dp": other}, device_id_type=pl.DeviceIdType.MESH
+        )
+    pl.semaphore_wait(barrier, groups + experts - 2)
+
+    def remote(source, target, sent, landed, device):
+        return pltpu.make_async_remote_copy(
+            src_ref=source,
+            dst_ref=target,
+            send_sem=sent,
+            recv_sem=landed,
+            device_id={"mp": device},
+            device_id_type=pl.DeviceIdType.MESH,
+        )
+
+    def outward(index, source):
+        dense = index >= count_expert
+        place = index - count_expert if dense else index
+        held_ref = held_dense if dense else held
+        own_ref = dense_ref if dense else expert_ref
+        return remote(
+            own_ref.at[place],
+            held_ref.at[source],
+            send_sem.at[index],
+            in_sem.at[source],
+            2 * place + (1 if dense else 0),
+        )
+
+    def sideways(step, source, orth):
+        return pltpu.make_async_remote_copy(
+            src_ref=land_dense if orth else dense_ref,
+            dst_ref=(all_dense if orth else all_moment).at[source],
+            send_sem=(orth_send_sem if orth else moment_send_sem).at[step],
+            recv_sem=(orth_sem if orth else moment_sem).at[source],
+            device_id={"dp": lax.rem(along + step, experts)},
+            device_id_type=pl.DeviceIdType.MESH,
+        )
+
+    total = count_expert + count_dense
+    owners = [2 * e for e in range(count_expert)] + [2 * d + 1 for d in range(count_dense)]
+    for index in range(total):
+
+        @pl.when(me != owners[index])
+        def _(index=index):
+            outward(index, me).start()
+
+    for step in range(1, experts):
+        sideways(step, along, False).start()
+
+    for step in range(1, groups):
+        source = lax.rem(me + step, groups)
+
+        @pl.when(is_expert)
+        def _(source=source):
+            outward(0, source).wait_recv()
+
+        @pl.when(is_dense)
+        def _(source=source):
+            outward(count_expert, source).wait_recv()
+
+    for index in range(total):
+
+        @pl.when(me != owners[index])
+        def _(index=index):
+            outward(index, me).wait_send()
+
+    def backward_expert(target):
+        return remote(
+            held.at[target],
+            land_expert.at[own],
+            back_send_sem.at[target],
+            back_sem.at[own],
+            target,
+        )
+
+    def backward_dense(target):
+        return remote(
+            held_dense.at[target],
+            land_dense.at[own],
+            back_send_sem.at[target],
+            back_sem.at[count_expert + own],
+            target,
+        )
+
+    def share_dense():
+        for index in range(count_expert, total):
+
+            @pl.when(me != owners[index])
+            def _(index=index):
+                landing = land_dense.at[index - count_expert]
+                remote(
+                    landing, landing, send_sem.at[index], back_sem.at[index], owners[index]
+                ).wait_recv()
+
+        for step in range(1, experts):
+            sideways(step, along, True).start()
+
+    def nothing():
+        return None
+
+    @pl.when(is_expert)
+    def _():
+        held[me] = expert_ref[own]
+        for j in range(groups // per):
+            matrix[:, D * j : D * j + D] = jnp.concatenate(
+                [held[per * j + inner] for inner in range(per)], axis=1
+            )
+
+        def finish(j):
+            for inner in range(per):
+                target = per * j + inner
+                held[target] = matrix[:, cols * target : cols * target + cols]
+
+                @pl.when(me != target)
+                def _(target=target):
+                    backward_expert(target).start()
+
+        newton_rounds(matrix, gram_ref, poly_ref, share_dense, finish)
+        land_expert[own] = held[me]
+        for target in range(groups):
+
+            @pl.when(me != target)
+            def _(target=target):
+                backward_expert(target).wait_send()
+
+    @pl.when(is_dense)
+    def _():
+        held_dense[me] = dense_ref[own]
+        for source in range(groups):
+            square[cols_dense * source : cols_dense * source + cols_dense, :] = held_dense[source]
+
+        def finish(j):
+            for target in range(groups):
+                held_dense[target] = square[
+                    cols_dense * target : cols_dense * target + cols_dense, :
+                ]
+
+                @pl.when(me != target)
+                def _(target=target):
+                    backward_dense(target).start()
+
+        newton_rounds(square, gram_ref, poly_ref, nothing, finish)
+        land_dense[own] = held_dense[me]
+        share_dense()
+        for target in range(groups):
+
+            @pl.when(me != target)
+            def _(target=target):
+                backward_dense(target).wait_send()
+
+    @pl.when(jnp.logical_not(is_expert | is_dense))
+    def _():
+        share_dense()
+
+    for index in range(count_expert):
+
+        @pl.when(me != owners[index])
+        def _(index=index):
+            landing = land_expert.at[index]
+            remote(
+                landing, landing, send_sem.at[index], back_sem.at[index], owners[index]
+            ).wait_recv()
+
+    all_dense[along] = land_dense[...]
+    all_moment[along] = dense_ref[...]
+    for step in range(1, experts):
+        sideways(step, lax.rem(along + step, experts), True).wait_recv()
+        sideways(step, lax.rem(along + step, experts), False).wait_recv()
+        sideways(step, along, True).wait_send()
+        sideways(step, along, False).wait_send()
+    expert_out[...] = land_expert[...]
+    dense_out[...] = all_dense[...]
+    moment_out[...] = all_moment[...]
+
+
+def newton(dense_mom, expert_mom, groups, experts):
+    cols, cols_dense = expert_mom.shape[2], dense_mom.shape[1]
+    count_expert, count_dense = expert_mom.shape[0], dense_mom.shape[0]
+    low = jnp.bfloat16
     vmem = pl.BlockSpec(memory_space=pltpu.VMEM)
+    dma = pltpu.SemaphoreType.DMA
     return pl.pallas_call(
-        newton_kernel,
+        partial(newton_kernel, groups, experts),
+        in_specs=[vmem, vmem],
+        out_specs=[vmem, vmem, vmem],
+        out_shape=[
+            jax.ShapeDtypeStruct(expert_mom.shape, low),
+            jax.ShapeDtypeStruct((experts,) + dense_mom.shape, low),
+            jax.ShapeDtypeStruct((experts,) + dense_mom.shape, low),
+        ],
+        scratch_shapes=[
+            pltpu.VMEM((groups, D, cols), low),
+            pltpu.VMEM((groups, cols_dense, D), low),
+            pltpu.VMEM((D, groups * cols), low),
+            pltpu.VMEM((D, D), low),
+            pltpu.VMEM((D, D), jnp.float32),
+            pltpu.VMEM((D, D), low),
+            pltpu.VMEM(expert_mom.shape, low),
+            pltpu.VMEM(dense_mom.shape, low),
+            pltpu.VMEM((experts,) + dense_mom.shape, low),
+            pltpu.VMEM((experts,) + dense_mom.shape, low),
+            dma((count_expert + count_dense,)),
+            dma((groups,)),
+            dma((groups,)),
+            dma((count_expert + count_dense,)),
+            dma((experts,)),
+            dma((experts,)),
+            dma((experts,)),
+            dma((experts,)),
+        ],
+        compiler_params=pltpu.CompilerParams(
+            vmem_limit_bytes=VMEM_LIMIT, collective_id=1, has_side_effects=True
+        ),
+        cost_estimate=pl.CostEstimate(
+            flops=NS_ITERS * (4 * D * D * FF + 2 * D * D * D),
+            bytes_accessed=40 * D * FF,
+            transcendentals=0,
+        ),
+    )(expert_mom.astype(low), dense_mom.astype(low))
+
+
+def total_kernel(
+    groups, experts, x_ref, out_ref, land_row, land_col, send_sem, row_sem, send_col_sem, col_sem
+):
+    across, along = lax.axis_index("mp"), lax.axis_index("dp")
+    barrier = pltpu.get_barrier_semaphore()
+    mesh_id = pl.DeviceIdType.MESH
+    for step in range(1, groups):
+        other = lax.rem(across + step, groups)
+        pl.semaphore_signal(barrier, inc=1, device_id={"mp": other}, device_id_type=mesh_id)
+    for step in range(1, experts):
+        other = lax.rem(along + step, experts)
+        pl.semaphore_signal(barrier, inc=1, device_id={"dp": other}, device_id_type=mesh_id)
+    pl.semaphore_wait(barrier, groups + experts - 2)
+
+    def to_row(step, source):
+        return pltpu.make_async_remote_copy(
+            src_ref=x_ref,
+            dst_ref=land_row.at[source],
+            send_sem=send_sem.at[step],
+            recv_sem=row_sem.at[source],
+            device_id={"mp": lax.rem(across + step, groups)},
+            device_id_type=mesh_id,
+        )
+
+    def to_col(step, source):
+        return pltpu.make_async_remote_copy(
+            src_ref=out_ref,
+            dst_ref=land_col.at[source],
+            send_sem=send_col_sem.at[step],
+            recv_sem=col_sem.at[source],
+            device_id={"dp": lax.rem(along + step, experts)},
+            device_id_type=mesh_id,
+        )
+
+    for step in range(1, groups):
+        to_row(step, across).start()
+    land_row[across] = x_ref[...]
+    for step in range(1, groups):
+        to_row(step, lax.rem(across + step, groups)).wait_recv()
+    total = land_row[0]
+    for source in range(1, groups):
+        total = total + land_row[source]
+    out_ref[...] = total
+    for step in range(1, experts):
+        to_col(step, along).start()
+    land_col[along] = total
+    for step in range(1, experts):
+        to_col(step, lax.rem(along + step, experts)).wait_recv()
+    for step in range(1, groups):
+        to_row(step, across).wait_send()
+    for step in range(1, experts):
+        to_col(step, along).wait_send()
+    total = land_col[0]
+    for source in range(1, experts):
+        total = total + land_col[source]
+    out_ref[...] = total
+
+
+def total_of(array, groups, experts, collective):
+    vmem = pl.BlockSpec(memory_space=pltpu.VMEM)
+    dma = pltpu.SemaphoreType.DMA
+    return pl.pallas_call(
+        partial(total_kernel, groups, experts),
         in_specs=[vmem],
         out_specs=vmem,
-        out_shape=jax.ShapeDtypeStruct(matrix.shape, jnp.bfloat16),
-        scratch_shapes=[pltpu.VMEM((D, D), jnp.float32), pltpu.VMEM((D, D), jnp.bfloat16)],
-        compiler_params=pltpu.CompilerParams(vmem_limit_bytes=VMEM_LIMIT),
+        out_shape=jax.ShapeDtypeStruct(array.shape, array.dtype),
+        scratch_shapes=[
+            pltpu.VMEM((groups,) + array.shape, array.dtype),
+            pltpu.VMEM((experts,) + array.shape, array.dtype),
+            dma((groups,)),
+            dma((groups,)),
+            dma((experts,)),
+            dma((experts,)),
+        ],
+        compiler_params=pltpu.CompilerParams(
+            vmem_limit_bytes=16 * 1024 * 1024, collective_id=collective, has_side_effects=True
+        ),
         cost_estimate=pl.CostEstimate(
-            flops=NS_ITERS * (4 * D * D * cols + 2 * D * D * D),
-            bytes_accessed=4 * D * cols,
-            transcendentals=0,
+            flops=0, bytes_accessed=30000000, transcendentals=0
         ),
-    )(matrix)
+    )(array)
+
+
+def lookup_kernel(vocab, wanted_ref, table_ref, out_ref, acc_ref):
+    block = pl.program_id(0)
+    height = table_ref.shape[0]
+    place = lax.broadcasted_iota(jnp.int32, (wanted_ref.shape[0], height), 1) + block * height
+    pick = (wanted_ref[...] == place).astype(jnp.bfloat16)
+    row = lax.broadcasted_iota(jnp.int32, table_ref.shape, 0) + block * height
+    table = jnp.where(row < vocab, table_ref[...], 0.0).astype(jnp.bfloat16)
+    part = dot_nn(pick, table)
+
+    @pl.when(block == 0)
+    def _():
+        acc_ref[...] = part
+
+    @pl.when(block > 0)
+    def _():
+        acc_ref[...] += part
+
+    @pl.when(block == pl.num_programs(0) - 1)
+    def _():
+        out_ref[...] = acc_ref[...].astype(jnp.bfloat16)
+
+
+def lookup(wanted, table):
+    count = wanted.shape[0]
+    vocab = table.shape[0]
+    height = 1024
+    whole = pl.BlockSpec((count, D), lambda j: (0, 0))
+    return pl.pallas_call(
+        partial(lookup_kernel, vocab),
+        grid=(-(-vocab // height),),
+        in_specs=[
+            pl.BlockSpec((count, 1), lambda j: (0, 0)),
+            pl.BlockSpec((height, D), lambda j: (j, 0)),
+        ],
+        out_specs=whole,
+        out_shape=jax.ShapeDtypeStruct((count, D), jnp.bfloat16),
+        scratch_shapes=[pltpu.VMEM((count, D), jnp.float32)],
+        compiler_params=params(),
+        cost_estimate=pl.CostEstimate(
+            flops=2 * count * vocab * D, bytes_accessed=4 * vocab * D, transcendentals=0
+        ),
+    )(wanted[:, None], table)
+
+
+def dense_kernel(
+    groups,
+    experts,
+    enc_ref,
+    dec_ref,
+    out_ref,
+    land,
+    summed,
+    land_enc,
+    land_dec,
+    send_sem,
+    land_sem,
+    enc_send_sem,
+    enc_sem,
+    dec_send_sem,
+    dec_sem,
+):
+    across, along = lax.axis_index("mp"), lax.axis_index("dp")
+    count = enc_ref.shape[1]
+    per_enc, per_dec = land_enc.shape[1], land_dec.shape[1]
+    barrier = pltpu.get_barrier_semaphore()
+    mesh_id = pl.DeviceIdType.MESH
+    for step in range(1, groups):
+        other = lax.rem(across + step, groups)
+        pl.semaphore_signal(barrier, inc=1, device_id={"mp": other}, device_id_type=mesh_id)
+    for step in range(1, experts):
+        other = lax.rem(along + step, experts)
+        pl.semaphore_signal(barrier, inc=1, device_id={"dp": other}, device_id_type=mesh_id)
+    pl.semaphore_wait(barrier, groups + experts - 2)
+
+    def to_row(step, source):
+        other = lax.rem(across + step, groups)
+        return pltpu.make_async_remote_copy(
+            src_ref=enc_ref.at[other],
+            dst_ref=land.at[source],
+            send_sem=send_sem.at[step],
+            recv_sem=land_sem.at[source],
+            device_id={"mp": other},
+            device_id_type=mesh_id,
+        )
+
+    def to_col(step, source, dec):
+        other = lax.rem(along + step, experts)
+        per = per_dec if dec else per_enc
+        return pltpu.make_async_remote_copy(
+            src_ref=(dec_ref if dec else summed).at[pl.ds(other * per, per)],
+            dst_ref=(land_dec if dec else land_enc).at[source],
+            send_sem=(dec_send_sem if dec else enc_send_sem).at[step],
+            recv_sem=(dec_sem if dec else enc_sem).at[source],
+            device_id={"dp": other},
+            device_id_type=mesh_id,
+        )
+
+    for step in range(1, groups):
+        to_row(step, across).start()
+    for step in range(1, experts):
+        to_col(step, along, True).start()
+    land[across] = enc_ref[across]
+    land_dec[along] = dec_ref[pl.ds(along * per_dec, per_dec)]
+    for step in range(1, groups):
+        to_row(step, lax.rem(across + step, groups)).wait_recv()
+
+    for index in range(count):
+        total = land[0, index].astype(jnp.float32)
+        for source in range(1, groups):
+            total = total + land[source, index].astype(jnp.float32)
+        summed[index] = total.astype(jnp.bfloat16)
+    for index in range(count, summed.shape[0]):
+        summed[index] = jnp.zeros(summed.shape[1:], jnp.bfloat16)
+    for step in range(1, experts):
+        to_col(step, along, False).start()
+    land_enc[along] = summed[pl.ds(along * per_enc, per_enc)]
+    for step in range(1, groups):
+        to_row(step, across).wait_send()
+    for step in range(1, experts):
+        source = lax.rem(along + step, experts)
+        to_col(step, source, True).wait_recv()
+        to_col(step, source, False).wait_recv()
+        to_col(step, along, True).wait_send()
+        to_col(step, along, False).wait_send()
+    for landed, per, first in ((land_enc, per_enc, 0), (land_dec, per_dec, per_enc)):
+        for index in range(per):
+            total = landed[0, index].astype(jnp.float32)
+            for source in range(1, experts):
+                total = total + landed[source, index].astype(jnp.float32)
+            out_ref[first + index] = total
+
+
+def dense_total(enc, dec, groups, experts):
+    count, cols = enc.shape[1], enc.shape[2]
+    per_enc, per_dec = -(-count // experts), -(-dec.shape[0] // experts)
+    dec = jnp.pad(dec, ((0, per_dec * experts - dec.shape[0]), (0, 0), (0, 0)))
+    vmem = pl.BlockSpec(memory_space=pltpu.VMEM)
+    dma = pltpu.SemaphoreType.DMA
+    low = jnp.bfloat16
+    return pl.pallas_call(
+        partial(dense_kernel, groups, experts),
+        in_specs=[vmem, vmem],
+        out_specs=vmem,
+        out_shape=jax.ShapeDtypeStruct((per_enc + per_dec, cols, D), jnp.float32),
+        scratch_shapes=[
+            pltpu.VMEM(enc.shape, low),
+            pltpu.VMEM((per_enc * experts, cols, D), low),
+            pltpu.VMEM((experts, per_enc, cols, D), low),
+            pltpu.VMEM((experts, per_dec, cols, D), low),
+            dma((groups,)),
+            dma((groups,)),
+            dma((experts,)),
+            dma((experts,)),
+            dma((experts,)),
+            dma((experts,)),
+        ],
+        compiler_params=pltpu.CompilerParams(
+            vmem_limit_bytes=VMEM_LIMIT, collective_id=4, has_side_effects=True
+        ),
+        cost_estimate=pl.CostEstimate(
+            flops=0, bytes_accessed=200000000, transcendentals=0
+        ),
+    )(enc, dec)
+
+
+def piece_of(array, count, experts):
+    along = lax.axis_index("dp")
+    pieces = []
+    for part in (array[:count], array[count:]):
+        per = -(-part.shape[0] // experts)
+        spare = per * experts - part.shape[0]
+        part = jnp.pad(part, ((0, spare),) + ((0, 0),) * (part.ndim - 1))
+        pieces.append(lax.dynamic_slice_in_dim(part, along * per, per, 0))
+    return jnp.concatenate(pieces, axis=0)
+
+
+def whole_of(pieces, count, rest):
+    per = -(-count // pieces.shape[0])
+    first = pieces[:, :per].reshape((-1,) + pieces.shape[2:])[:count]
+    second = pieces[:, per:].reshape((-1,) + pieces.shape[2:])[:rest]
+    return jnp.concatenate([first, second], axis=0)
 
 
 def project(rows, stored):
@@ -658,41 +1087,101 @@
     return hot, routes * cap + slots
 
 
-def moe_forward(resid, gain, router, weights, hot, places, cap):
+def moe_send(resid, gain, router, hot, places, cap):
     experts = router.shape[1]
     normed, inverse = normalize(resid, gain)
     normed_low = normed.astype(jnp.bfloat16)
+    buffer = dot_nn(dispatch(places, experts * cap), normed_low).astype(jnp.bfloat16)
+    arrived = swap_owners(buffer.reshape(experts, cap, D)).reshape(-1, D)
     probs = jax.nn.softmax(
         jnp.dot(normed_low.astype(jnp.float32), router, precision=highest), axis=-1
     )
-    spread = dispatch(places, experts * cap)
-    buffer = dot_nn(spread, normed_low).astype(jnp.bfloat16)
-    arrived = swap_owners(buffer.reshape(experts, cap, D)).reshape(-1, D)
+    gate = jnp.sum(probs * hot, axis=1)
+    return arrived, (normed_low, inverse, probs, gate)
+
+
+def moe_expert(weights, cap, arrived):
     pre, result = expert_forward(arrived, weights)
-    returned = swap_owners(result.reshape(experts, cap, D)).reshape(-1, D)
-    outputs = dot_tn(spread, returned)
-    gate = jnp.sum(probs * hot, axis=1)
-    kept = (normed_low, inverse, probs, gate, arrived, pre, outputs)
-    return (resid + gate[:, None] * outputs, kept)
-
-
-def moe_backward(resid, gain, router, weights, hot, places, cap, kept, grad, aux_scale, frac):
+    return pre, swap_owners(result.reshape(-1, cap, D)).reshape(-1, D)
+
+
+def moe_receive(resid, places, arrived, pre, returned, sent):
+    outputs = dot_tn(dispatch(places, returned.shape[0]), returned)
+    return (resid + sent[3][:, None] * outputs, sent + (arrived, pre, outputs))
+
+
+def moe_back_send(places, cap, kept, grad):
     normed_low, inverse, probs, gate, arrived, pre, outputs = kept
-    experts = router.shape[1]
+    experts = arrived.shape[0] // cap
+    d_rows = (gate[:, None] * grad).astype(jnp.bfloat16)
+    buffer = dot_nn(dispatch(places, experts * cap), d_rows).astype(jnp.bfloat16)
+    return swap_owners(buffer.reshape(experts, cap, D)).reshape(-1, D)
+
+
+def moe_back_expert(weights, cap, kept, d_arrived):
+    normed_low, inverse, probs, gate, arrived, pre, outputs = kept
+    experts = arrived.shape[0] // cap
+    d_weights, d_back = expert_backward(arrived, d_arrived, pre, weights)
+    return d_weights, swap_owners(d_back.reshape(experts, cap, D)).reshape(-1, D)
+
+
+def moe_back_receive(resid, gain, router, hot, places, kept, grad, returned, aux_scale, frac):
+    normed_low, inverse, probs, gate, arrived, pre, outputs = kept
     d_gate = jnp.sum(grad * outputs, axis=1)
-    d_rows = (gate[:, None] * grad).astype(jnp.bfloat16)
-    spread = dispatch(places, experts * cap)
-    buffer = dot_nn(spread, d_rows).astype(jnp.bfloat16)
-    d_arrived = swap_owners(buffer.reshape(experts, cap, D)).reshape(-1, D)
-    d_weights, d_back = expert_backward(arrived, d_arrived, pre, weights)
-    returned = swap_owners(d_back.reshape(experts, cap, D)).reshape(-1, D)
-    d_normed = dot_tn(spread, returned)
     d_probs = hot * d_gate[:, None] + aux_scale * frac[None, :]
     d_logits = probs * (d_probs - jnp.sum(probs * d_probs, axis=-1, keepdims=True))
     d_router = jnp.dot(normed_low.astype(jnp.float32).T, d_logits, precision=highest)
-    d_normed = d_normed + jnp.dot(d_logits, router.T, precision=highest)
+    d_normed = dot_tn(dispatch(places, returned.shape[0]), returned) + jnp.dot(
+        d_logits, router.T, precision=highest
+    )
     d_resid, d_gain = normalize_back(resid, inverse, gain, d_normed)
-    return (grad + d_resid, d_gain, d_router, d_weights)
+    return (grad + d_resid, d_gain, d_router)
+
+
+def ranks_of(ids, size):
+    count = ids.shape[0]
+    here, there = ids[:, None], ids[None, :]
+    before = lax.broadcasted_iota(jnp.int32, (count, count), 1) < lax.broadcasted_iota(
+        jnp.int32, (count, count), 0
+    )
+    again = jnp.max(((here == there) & before).astype(jnp.int32), axis=1)
+    owner = ids // size
+    lower = (there < here) & (there >= (owner * size)[:, None]) & (again[None, :] == 0)
+    return owner, jnp.sum(lower.astype(jnp.int32), axis=1)
+
+
+def slots_of(owner, rank, owners, width, turn):
+    slot = owner * width + rank - turn * width
+    slot = jnp.where((rank >= turn * width) & (rank < (turn + 1) * width), slot, -1)
+    return lax.broadcasted_iota(jnp.int32, (owners * width, rank.shape[0]), 0) == slot[None, :]
+
+
+def ids_in(hot, local, width):
+    return jnp.max(jnp.where(hot, local[None, :], -1), axis=1).reshape(-1, width)
+
+
+def exchange(array, axes):
+    return lax.all_to_all(array, axes, split_axis=0, concat_axis=0, tiled=True)
+
+
+def rows_into(landed, rows, count):
+    place = landed[None, :] == lax.broadcasted_iota(jnp.int32, (count, landed.shape[0]), 0)
+    return dot_nn(place.astype(jnp.bfloat16), rows)
+
+
+def in_lanes(parts):
+    flat = jnp.concatenate([part.reshape(-1) for part in parts])
+    rows = -(-flat.shape[0] // (8 * LANES)) * 8
+    return jnp.pad(flat, (0, rows * LANES - flat.shape[0])).reshape(rows, LANES)
+
+
+def from_lanes(array, parts):
+    flat = array.reshape(-1)
+    taken, out = 0, []
+    for part in parts:
+        out.append(flat[taken : taken + part.size].reshape(part.shape))
+        taken += part.size
+    return out
 
 
 def self_forward(resid, gain, weights, parts, causal):
@@ -768,54 +1257,11 @@
 
 
 def share_columns(d_weights, groups):
-    stacked = jnp.stack([part.astype(jnp.bfloat16) for part in d_weights])
-    count = stacked.shape[0]
-    split = jnp.transpose(stacked.reshape(count, groups, -1, D), (1, 0, 2, 3))
-    return lax.psum_scatter(split, "mp", scatter_dimension=0, tiled=False)
-
-
-def orthogonalize(dense_mom, expert_mom, groups):
-    cols = expert_mom.shape[2]
-    cols_dense = dense_mom.shape[1]
-    split = D // cols
-    count_expert, count_dense = expert_mom.shape[0], dense_mom.shape[0]
-    depth = cols_dense * split
-    frames = jnp.transpose(
-        dense_mom.astype(jnp.bfloat16).reshape(count_dense, cols_dense, split, cols), (0, 2, 1, 3)
-    ).reshape(count_dense, depth, cols)
-    frames = jnp.pad(frames, ((0, 0), (0, D - depth), (0, 0)))
-    spare = groups - count_expert - count_dense
-    sent = jnp.concatenate(
-        [expert_mom.astype(jnp.bfloat16), frames, jnp.zeros((spare, D, cols), jnp.bfloat16)],
-        axis=0,
-    )
-    arrived = lax.all_to_all(sent, "mp", split_axis=0, concat_axis=0, tiled=True)
-    whole = jnp.transpose(arrived, (1, 0, 2)).reshape(D, groups * cols)
-    square = jnp.transpose(
-        arrived[:, :depth].reshape(groups, split, cols_dense, cols), (0, 2, 1, 3)
-    ).reshape(D, D)
-    square = jnp.pad(square, ((0, 0), (0, groups * cols - D)))
-    is_expert = lax.axis_index("mp") < count_expert
-    result = newton(jnp.where(is_expert, whole, square))
-    back_expert = jnp.transpose(result.reshape(D, groups, cols), (1, 0, 2))
-    back_dense = jnp.transpose(
-        result[:, :D].reshape(groups, cols_dense, split, cols), (0, 2, 1, 3)
-    ).reshape(groups, depth, cols)
-    back_dense = jnp.pad(back_dense, ((0, 0), (0, D - depth), (0, 0)))
-    returned = lax.all_to_all(
-        jnp.where(is_expert, back_expert, back_dense),
-        "mp",
-        split_axis=0,
-        concat_axis=0,
-        tiled=True,
-    )
-    dense_orth = jnp.transpose(
-        returned[count_expert : count_expert + count_dense, :depth].reshape(
-            count_dense, split, cols_dense, cols
-        ),
-        (0, 2, 1, 3),
-    ).reshape(count_dense, cols_dense, D)
-    return dense_orth, returned[:count_expert]
+    split = jnp.concatenate(
+        [part.astype(jnp.bfloat16).reshape(groups, -1, D) for part in d_weights], axis=1
+    )
+    summed = lax.psum_scatter(split.reshape(-1, D), "mp", scatter_dimension=0, tiled=True)
+    return summed.reshape(len(d_weights), -1, D)
 
 
 def on_device(
@@ -850,25 +1296,47 @@
     npos = loss_pos.shape[1]
     vocab_dev = table_w.shape[0]
     own_seq = lax.axis_index("dp") * groups + column
-    rows_dev = src_len + tgt_len
     count_dense = dense_w.shape[0]
     low = jnp.bfloat16
     dense_local = dense_w.astype(low).reshape(count_dense, -1, D)
     enc_dense = lax.all_gather(dense_local[0:4], "mp", axis=1, tiled=True)
     expert_local = expert_w[:, :, 0].astype(low)
-    dec_ids = jnp.concatenate(
-        [jnp.zeros((targets.shape[0], 1), jnp.int32), targets[:, :-1]], axis=1
-    )
-    all_ids = jnp.concatenate([src_ids, dec_ids], axis=1).reshape(-1)
-    local_ids = all_ids - column * vocab_dev
-    inside = (local_ids >= 0) & (local_ids < vocab_dev)
-    local_ids = jnp.where(inside, local_ids, vocab_dev)
-    shared, listed, counts = embed(local_ids, table_w, rows_dev)
-    embedded = lax.psum_scatter(shared, "mp", scatter_dimension=0, tiled=True).astype(jnp.float32)
+    devices = experts * groups
+    piece_rows = table_m.shape[0]
+    own_src_ids = lax.dynamic_slice_in_dim(src_ids, column, 1, 0).reshape(-1)
+    own_targets = lax.dynamic_slice_in_dim(targets, column, 1, 0).reshape(-1)
+    own_ids = jnp.concatenate([own_src_ids, jnp.zeros((1,), jnp.int32), own_targets[:-1]])
+    shard, rank = ranks_of(own_ids, vocab_dev)
+    owner, owner_rank = ranks_of(own_ids, piece_rows)
+    local_ids = own_ids - shard * vocab_dev
+    piece_ids = own_ids - owner * piece_rows
+    owner = (owner % experts) * groups + owner // experts
+    needs = jnp.stack([jnp.max(rank) // FETCH + 1, jnp.max(owner_rank) // GIVE + 1])
+
+    def asked_of(turn):
+        return ids_in(slots_of(shard, rank, groups, FETCH, turn), local_ids, FETCH)
+
+    def fetched(turn, wanted):
+        rows = lookup(wanted.reshape(-1), table_w)
+        rows = exchange(rows.reshape(groups, FETCH, D), "mp")
+        hot = slots_of(shard, rank, groups, FETCH, turn).astype(low)
+        return dot_tn(hot, rows.reshape(-1, D))
+
+    noted = jnp.broadcast_to(jnp.pad(needs, (0, LANES - 2))[None, :], (groups, LANES))
+    asked = exchange(jnp.concatenate([asked_of(0), noted], axis=1), "mp")
+    needs = jnp.max(asked[:, FETCH:], axis=0, keepdims=True)
+    embedded = fetched(0, asked[:, :FETCH])
+    embedded, enc_dense = lax.optimization_barrier((embedded, enc_dense))
+    needs = jnp.max(lax.all_gather(jnp.tile(needs, (8, 1)), "dp", axis=0, tiled=True), axis=0)
+
+    def fetch_more(state):
+        turn, rows = state
+        return turn + 1, rows + fetched(turn, exchange(asked_of(turn), "mp"))
+
+    turns, embedded = lax.while_loop(
+        lambda state: state[0] < needs[0], fetch_more, (jnp.int32(1), embedded)
+    )
     enc_expert = lax.all_gather(expert_local[0], "mp", axis=0, tiled=False)
-    dec_dense = lax.all_gather(dense_local[4:12], "mp", axis=1, tiled=True)
-    dec_expert = lax.all_gather(expert_local[1], "mp", axis=0, tiled=False)
-    table_low = table_w.astype(low)
     own_src = lax.dynamic_slice_in_dim(routes_src, own_seq, 1, 0).reshape(-1)
     own_tgt = lax.dynamic_slice_in_dim(routes_tgt, own_seq, 1, 0).reshape(-1)
     cap_src = (5 * src_len + 4 * experts - 1) // (4 * experts)
@@ -882,18 +1350,27 @@
     enc_parts = bias_parts(bias_w[0], False)
     dec_parts = bias_parts(bias_w[1], True)
     enc_mid, enc_kept = self_forward(embedded[:src_len], gains_w[0], enc_dense, enc_parts, False)
-    dec_mid, dec_kept = self_forward(
-        embedded[src_len:], gains_w[3], dec_dense[0:4], dec_parts, True
-    )
-    enc_out, enc_moe = moe_forward(
-        enc_mid, gains_w[1], router_w[0], enc_expert, hot_src, places_src, cap_src
-    )
+    dec_local, late_table, enc_mid = lax.optimization_barrier((dense_local[4:8], table_w, enc_mid))
+    arrived, enc_sent = moe_send(enc_mid, gains_w[1], router_w[0], hot_src, places_src, cap_src)
+    dec_dense = lax.all_gather(dec_local, "mp", axis=1, tiled=True)
+    arrived, enc_expert, cross_local, dec_expert_local = lax.optimization_barrier(
+        (arrived, enc_expert, dense_local[8:12], expert_local[1])
+    )
+    cross_dense = lax.all_gather(cross_local, "mp", axis=1, tiled=True)
+    dec_expert = lax.all_gather(dec_expert_local, "mp", axis=0, tiled=False)
+    table_low = late_table.astype(low)
+    pre, returned = moe_expert(enc_expert, cap_src, arrived)
+    dec_mid, dec_kept = self_forward(embedded[src_len:], gains_w[3], dec_dense, dec_parts, True)
+    returned, dec_mid = lax.optimization_barrier((returned, dec_mid))
+    enc_out, enc_moe = moe_receive(enc_mid, places_src, arrived, pre, returned, enc_sent)
     memory_float, memory_inv = normalize(enc_out, gains_w[2])
     memory = memory_float.astype(low)
-    dec_crossed, cross_kept = cross_forward(dec_mid, gains_w[4], dec_dense[4:8], memory)
-    dec_result, dec_moe = moe_forward(
-        dec_crossed, gains_w[5], router_w[1], dec_expert, hot_tgt, places_tgt, cap_tgt
-    )
+    dec_crossed, cross_kept = cross_forward(dec_mid, gains_w[4], cross_dense, memory)
+    arrived, dec_sent = moe_send(
+        dec_crossed, gains_w[5], router_w[1], hot_tgt, places_tgt, cap_tgt
+    )
+    pre, returned = moe_expert(dec_expert, cap_tgt, arrived)
+    dec_result, dec_moe = moe_receive(dec_crossed, places_tgt, arrived, pre, returned, dec_sent)
     final_float, final_inv = normalize(dec_result, gains_w[6])
     final_low = final_float.astype(low)
     head_scale = D ** (-0.5)
@@ -904,7 +1381,9 @@
     chosen = dot_nn(pick, final_low).astype(low)
     gathered = lax.all_gather(chosen, "mp", axis=0, tiled=True)
     logits = dot_nt(gathered, table_low) * head_scale
-    wanted = jnp.take_along_axis(targets, loss_pos, axis=1).reshape(-1) - column * vocab_dev
+    at_pos = loss_pos[:, :, None] == lax.broadcasted_iota(jnp.int32, (1, 1, tgt_len), 2)
+    wanted = jnp.sum(jnp.where(at_pos, targets[:, None, :], 0), axis=2).reshape(-1)
+    wanted = wanted - column * vocab_dev
     hits = jnp.arange(vocab_dev, dtype=jnp.int32)[None, :] == wanted[:, None]
     top = jnp.max(logits, axis=1)
     stats = lax.all_gather(
@@ -938,66 +1417,75 @@
         concat_axis=0,
         tiled=True,
     )
-    table_grad = dot_tn(d_logits, gathered) * head_scale
+    d_logits, d_shares = lax.optimization_barrier((d_logits, d_shares))
+    table_grad = (dot_tn(d_logits, gathered) * head_scale).astype(low)
+    padded = -(-piece_rows // 16) * 16
+    table_grad = jnp.pad(
+        table_grad.reshape(experts, piece_rows, D), ((0, 0), (0, padded - piece_rows), (0, 0))
+    ).reshape(-1, D)
+    table_share = lax.psum_scatter(table_grad, "dp", scatter_dimension=0, tiled=True)
     d_chosen = jnp.sum(d_shares.astype(jnp.float32), axis=0).astype(low)
     d_final = dot_tn(pick, d_chosen)
     d_dec, gain_final = normalize_back(dec_result, final_inv, gains_w[6], d_final)
-    d_dec, gain_dec_moe, dec_router, dec_dw = moe_backward(
+    d_arrived = moe_back_send(places_tgt, cap_tgt, dec_moe, d_dec)
+    dec_dw, returned = moe_back_expert(dec_expert, cap_tgt, dec_moe, d_arrived)
+    dec_share = lax.psum_scatter(dec_dw, "mp", scatter_dimension=0, tiled=False)
+    d_dec, gain_dec_moe, dec_router = moe_back_receive(
         dec_crossed,
         gains_w[5],
         router_w[1],
-        dec_expert,
         hot_tgt,
         places_tgt,
-        cap_tgt,
         dec_moe,
         d_dec,
+        returned,
         aux_weight * experts / total_tgt,
         frac_tgt,
     )
-    dec_share = lax.psum_scatter(dec_dw, "mp", scatter_dimension=0, tiled=False)
     d_dec, gain_cross, cross_dw, d_memory = cross_backward(
-        gains_w[4], dec_dense[4:8], memory, cross_kept, d_dec
+        gains_w[4], cross_dense, memory, cross_kept, d_dec
     )
     d_enc, gain_memory = normalize_back(enc_out, memory_inv, gains_w[2], d_memory)
+    d_arrived = moe_back_send(places_src, cap_src, enc_moe, d_enc)
     d_dec, gain_self, self_dw, dec_bias = self_backward(
-        gains_w[3], dec_dense[0:4], dec_parts, True, dec_kept, d_dec
-    )
-    dec_rows = lax.all_gather(d_dec.astype(low), "mp", axis=0, tiled=False)
+        gains_w[3], dec_dense, dec_parts, True, dec_kept, d_dec
+    )
+    d_arrived, d_dec, table_share = lax.optimization_barrier((d_arrived, d_dec, table_share))
+    enc_dw, returned = moe_back_expert(enc_expert, cap_src, enc_moe, d_arrived)
     dec_cols = share_columns(self_dw + cross_dw, groups)
-    d_enc, gain_enc_moe, enc_router, enc_dw = moe_backward(
+    enc_share = lax.psum_scatter(enc_dw, "mp", scatter_dimension=0, tiled=False)
+    d_enc, gain_enc_moe, enc_router = moe_back_receive(
         enc_mid,
         gains_w[1],
         router_w[0],
-        enc_expert,
         hot_src,
         places_src,
-        cap_src,
         enc_moe,
         d_enc,
+        returned,
         aux_weight * experts / total_src,
         frac_src,
     )
-    enc_share = lax.psum_scatter(enc_dw, "mp", scatter_dimension=0, tiled=False)
+    d_enc, dec_share = lax.optimization_barrier((d_enc, dec_share))
     d_enc, gain_enc, enc_self_dw, enc_bias = self_backward(
         gains_w[0], enc_dense, enc_parts, False, enc_kept, d_enc
     )
-    enc_rows = lax.all_gather(d_enc.astype(low), "mp", axis=0, tiled=False)
-    enc_cols = share_columns(enc_self_dw, groups)
-    table_sum = unembed(local_ids, listed, counts, table_grad, enc_rows, dec_rows)
-    table_piece = lax.psum_scatter(table_sum, "dp", scatter_dimension=0, tiled=True).astype(
-        jnp.float32
-    )
-    dense_share = jnp.concatenate([enc_cols, dec_cols], axis=0)
-    per_dev = -(-count_dense // experts)
-    filler = per_dev * experts - count_dense
-    dense_piece = lax.psum_scatter(
-        jnp.pad(dense_share, ((0, filler), (0, 0), (0, 0))),
-        "dp",
-        scatter_dimension=0,
-        tiled=True,
-    ).astype(jnp.float32)
-    expert_share = jnp.stack([enc_share, dec_share]).astype(jnp.float32)
+    enc_parts = jnp.stack(
+        [part.astype(low).reshape(groups, -1, D) for part in enc_self_dw], axis=1
+    )
+    d_embedded = jnp.concatenate([d_enc, d_dec], axis=0).astype(low)
+
+    def given_ids(turn):
+        hot = slots_of(owner, owner_rank, devices, GIVE, turn)
+        return exchange(ids_in(hot, piece_ids, GIVE), ("dp", "mp")).reshape(-1)
+
+    def given_rows(turn):
+        hot = slots_of(owner, owner_rank, devices, GIVE, turn).astype(low)
+        rows = dot_nn(hot, d_embedded).astype(low).reshape(devices, GIVE, D)
+        return exchange(rows, ("dp", "mp")).reshape(-1, D)
+
+    landed, d_embedded = lax.optimization_barrier((given_ids(0), d_embedded))
+    arrived = given_rows(0)
     gains_grad = jnp.stack(
         [gain_enc, gain_enc_moe, gain_memory, gain_self, gain_cross, gain_dec_moe, gain_final]
     )
@@ -1005,16 +1493,32 @@
     bias_grad = jnp.stack([enc_bias, dec_bias])
     load_src = jnp.sum(enc_moe[2], axis=0)
     load_tgt = jnp.sum(dec_moe[2], axis=0)
-    gains_grad, router_grad, bias_grad, loss_sum, count, load_src, load_tgt = lax.psum(
-        (gains_grad, router_grad, bias_grad, own_loss, own_count, load_src, load_tgt),
-        ("dp", "mp"),
-    )
-    squares = (
-        jnp.sum(dense_piece * dense_piece)
-        + jnp.sum(expert_share * expert_share)
-        + jnp.sum(table_piece * table_piece)
-    )
-    squares = lax.psum(squares, ("dp", "mp"))
+    small = [gains_grad, router_grad, bias_grad, load_src, load_tgt, own_loss, own_count]
+    summed = total_of(in_lanes(small), groups, experts, 2)
+    dense_piece = dense_total(enc_parts, dec_cols, groups, experts)
+    arrived, summed, dense_piece = lax.optimization_barrier((arrived, summed, dense_piece))
+    table_piece = rows_into(landed, arrived, piece_rows)
+    gains_grad, router_grad, bias_grad, load_src, load_tgt, loss_sum, count = from_lanes(
+        summed, small
+    )
+
+    def give_more(state):
+        turn, total = state
+        return turn + 1, total + rows_into(given_ids(turn), given_rows(turn), piece_rows)
+
+    turns, table_piece = lax.while_loop(
+        lambda state: state[0] < needs[1], give_more, (jnp.int32(1), table_piece)
+    )
+    table_piece = table_piece + table_share[:piece_rows].astype(jnp.float32)
+    expert_share = jnp.stack([enc_share, dec_share]).astype(jnp.float32)
+    squares = jnp.zeros((8, LANES), jnp.float32)
+    for part in (dense_piece, expert_share, table_piece):
+        lanes = jnp.sum((part * part).reshape(-1, part.shape[-1]), axis=0)
+        squares = squares + jnp.pad(
+            jnp.sum(lanes.reshape(-1, min(LANES, math.gcd(lanes.shape[0], LANES))), axis=0),
+            (0, LANES - math.gcd(lanes.shape[0], LANES)),
+        )[None, :] * 0.125
+    squares = jnp.sum(total_of(squares, groups, experts, 3))
     squares = squares + sum(
         (jnp.sum(part * part) for part in (gains_grad, router_grad, bias_grad))
     )
@@ -1026,25 +1530,23 @@
         * (jnp.sum(frac_src * load_src) / total_src + jnp.sum(frac_tgt * load_tgt) / total_tgt)
     )
     loss = jnp.stack([loss_sum + aux, count])
-    old_piece = lax.dynamic_slice_in_dim(
-        jnp.pad(dense_m, ((0, filler), (0, 0))), lax.axis_index("dp") * per_dev, per_dev, 0
-    ).reshape(per_dev, -1, D)
+    old_piece = piece_of(dense_m, 4, experts).reshape(dense_piece.shape)
     piece_moment = 0.5 * old_piece + clip * dense_piece
     expert_moment = 0.5 * expert_m + clip * expert_share[:, :, None]
-    moment_flat = lax.all_gather(piece_moment.astype(low), "dp", axis=0, tiled=True)[:count_dense]
-    dense_moment = moment_flat.reshape(count_dense, -1).astype(jnp.float32)
     cols = expert_w.shape[4]
-    piece_orth, expert_orth = orthogonalize(
-        piece_moment, expert_moment.reshape(-1, D, cols), groups
-    )
-    dense_orth = lax.all_gather(piece_orth, "dp", axis=0, tiled=True)[:count_dense]
-    dense_orth = dense_orth.reshape(count_dense, -1).astype(jnp.float32)
+    expert_orth, dense_orth, dense_moment = newton(
+        piece_moment, expert_moment.reshape(-1, D, cols), groups, experts
+    )
+
+    def as_stored(pieces):
+        return whole_of(pieces, 4, count_dense - 4).reshape(count_dense, -1).astype(jnp.float32)
+
+    dense_moment, dense_orth = as_stored(dense_moment), as_stored(dense_orth)
     keep_rate = 1 - rate_matrix * decay_matrix
     dense_new = dense_w * keep_rate - rate_matrix * 0.2 * math.sqrt(D) * dense_orth
     expert_new = expert_w * keep_rate - rate_matrix * 0.2 * math.sqrt(
         max(D, FF)
     ) * expert_orth.astype(jnp.float32).reshape(expert_w.shape)
-    piece_rows = table_m.shape[0]
     table_clipped = clip * table_piece
     table_new, table_first, table_second = adam(
         lax.dynamic_slice_in_dim(table_w, lax.axis_index("dp") * piece_rows, piece_rows, 0),

time: 1600 us -> 1060 us (0.66)
  waiting for transfers between devices: 668 us -> 152 us
  blocking collectives: 184 us -> 103 us
  Pallas kernels: 319 us -> 392 us
    unnamed x16 -> x10, waiting for transfers between devices: 190 us -> 0.68 us
    all_gather x6 -> x3, waiting for transfers between devices: 112 us -> 0.02 us  [the longest x1 0.02 us: on_device(): dec_dense = lax.all_gather(dec_local, 'mp', axis=1, tiled=True)]
    unnamed x1 -> x0, blocking collectives: 110 us -> none
    all_to_all x2 -> x3, waiting for transfers between devices: 102 us -> 9.62 us  [exchange(): return lax.all_to_all(array, axes, split_axis=0, concat_axis=0, tiled=True)]
    pallas_call x7 -> x9, Pallas kernels: 224 us -> 315 us  [the longest x1 109 us: newton(): pl.pallas_call(partial(newton_kernel, groups, experts), in_specs=[vmem, v...]
    reduce_scatter x2, waiting for transfers between devices: 82.8 us -> 0.02 us  [the longest x1 0.02 us: share_columns(): lax.psum_scatter(split.reshape(-1, D), 'mp', scatter_dimension=0, tiled=T...]
    all_gather x1, waiting for transfers between devices: 57 us -> 0.01 us  [on_device(): enc_expert = lax.all_gather(expert_local[0], 'mp', axis=0, tiled=False)]
    all_to_all x0 -> x3, blocking collectives: none -> 56.4 us  [the longest x2 49.1 us: swap_owners(): return lax.all_to_all(buffer, 'dp', split_axis=0, concat_axis=0, tiled=True)]
  transfers between devices with their start and end apart: 25 -> 19, of which waited for: 18 -> 8; matrix products, arithmetic and copies ran while one was open for 19% -> 19% of each run, Pallas kernels for 10% -> 24%
where the time goes in v2:
time: 1060 us; the launch traced here: 1050 us
  Pallas kernels  392 us (37%)
  waiting for transfers between devices  152 us (14%)
  matrix products  148 us (14%)
  other arithmetic  106 us (10%)
  blocking collectives  103 us (10%)
  local copies, waits for them, and re-layouts  71.8 us (7%)
  starting transfers between devices  41.9 us (4%)
  between operations  27.3 us (3%)
    all_to_all x6, waiting for transfers between devices, swap_owners(): return lax.all_to_all(buffer, 'dp', split_axis=0, concat_axis=0, tiled=True)  118 us
    pallas_call x1, Pallas kernels, newton(): pl.pallas_call(partial(newton_kernel, groups, experts), in_specs=[vmem, v...  109 us
    pallas_call x2, Pallas kernels, total_of(): pl.pallas_call(partial(total_kernel, groups, experts), in_specs=[vmem], o...  67 us
    pallas_call x1, Pallas kernels, dense_total(): pl.pallas_call(partial(dense_kernel, groups, experts), in_specs=[vmem, vm...  60.8 us
    dot_general x22, matrix products, dot_nn(): lax.dot_general(left, right, (((1,), (0,)), ((), ())), preferred_element_...  59.7 us
    all_to_all x2, blocking collectives, swap_owners(): return lax.all_to_all(buffer, 'dp', split_axis=0, concat_axis=0, tiled=True)  49.1 us
    pallas_call x3, Pallas kernels, attend_back(): pl.pallas_call(partial(attend_back_kernel, biased, causal), grid=(pairs,)...  46.9 us
    pallas_call x2, Pallas kernels, expert_backward(): pl.pallas_call(expert_back_kernel, grid=(blocks // per,), in_specs=[whole...  41.5 us
  transfers between devices with their start and end apart: 19, of which 8 were waited for; matrix products, arithmetic and copies ran while one was open for 19% of the time, Pallas kernels for 24%

profile of v2, /device:TPU:2, one launch (start us, length us, event | category | flops | bytes accessed | tf_op | source)
XLA Modules:
  0.0 1051.3 jit_solution(15212283881089334238)
XLA Ops:
  37.2 11.8 %shard_map.383 = bf16[1024,768]{1,0:T(8,128)(2,1)} custom-call(s32[1024,1]{1,0:T(8,128)} %copy.126.wanted_ref, f32[4016,768]{1,0:T(8,128)} %table_ref.1), custom_call_target="tpu_custom_call" | custom-call | flops 6316621824 | bytes 12337152 | tf_op jit(solution)/shard_map/pallas_call | solution.py:908
  57.5 13.3 %all_gather.31 = s32[32,128]{1,0:T(8,128)S(1)} all-gather(s32[8,128]{1,0:T(8,128)S(1)} %tile.2), channel_id=1, replica_groups=mesh['dp'=4,'mp'=8] {'dp'}, dimensions={0}, use_global_device_ids=true | all-gather | bytes 20480 | tf_op jit(solution)/shard_map/all_gather | solution.py:1330
  100.9 14.3 %shard_map.384 = (bf16[768,768]{1,0:T(8,128)(2,1)}, f32[12,1,768]{2,1,0:T(1,128)}) custom-call(f32[2,12]{1,0:T(2,128)} %fusion.106.refs_0_, f32[12,1,512]{2,1,0:T(1,128)} %broadcast_in_dim.83.refs_1_, bf16[768,2304]{1,0:T(8,128)(2,1)} %convolution_convert_fusion.refs_2_.refs_3_.refs_4_, bf16[768,2304]{1,0:T(8,128)(2,1)} %convolution_convert_fusion.refs_2_.refs_3_.refs_4_, ...), custom_call_target="tpu_custom_call" | custom-call | flops 1811939328 | bytes 9437184 | tf_op jit(solution)/shard_map/pallas_call | solution.py:291
  132.1 32.0 %all-to-all-done.7 = bf16[4,240,768]{2,1,0:T(8,128)(2,1)} async-done(((bf16[4,240,768]{2,1,0:T(8,128)(2,1)}), bf16[4,240,768]{2,1,0:T(8,128)(2,1)}, u32[]{:S(2)}, u32[]{:S(2)}) %all-to-all-start.7) | async-done | bytes 1474592 | tf_op jit(solution)/shard_map/all_to_all | solution.py:1070
  166.4 16.2 %shard_map.385 = (f32[4,960,768]{2,1,0:T(8,128)}, bf16[960,768]{1,0:T(8,128)(2,1)}) custom-call(bf16[960,768]{1,0:T(8,128)(2,1)} %bitcast.21.x_ref, bf16[8,2,768,384]{3,2,1,0:T(8,128)(2,1)} %bitcast.417, bf16[8,2,768,384]{3,2,1,0:T(8,128)(2,1)} %bitcast.418), custom_call_target="tpu_custom_call" | custom-call | flops 9059696640 | bytes 24182784 | tf_op jit(solution)/shard_map/pallas_call | solution.py:387
  208.1 13.5 %all-to-all-done.8 = bf16[4,240,768]{2,1,0:T(8,128)(2,1)} async-done(((bf16[4,240,768]{2,1,0:T(8,128)(2,1)}), bf16[4,240,768]{2,1,0:T(8,128)(2,1)}, u32[]{:S(2)}, u32[]{:S(2)}) %all-to-all-start.8) | async-done | bytes 1474592 | tf_op jit(solution)/shard_map/all_to_all | solution.py:1070
  251.9 16.4 %all_to_all.109 = bf16[4,80,768]{2,1,0:T(8,128)(2,1)} all-to-all(bf16[4,80,768]{2,1,0:T(8,128)(2,1)S(1)} %bitcast.374), channel_id=1, replica_groups=mesh['dp'=4,'mp'=8] {'dp'}, dimensions={0} | all-to-all | bytes 983040 | tf_op jit(solution)/shard_map/all_to_all | solution.py:1070
  299.3 24.3 %all-gather.17.cloned.1.call-done = bf16[1024,768]{1,0:T(8,128)(2,1)} async-done(((bf16[128,768]{1,0:T(8,128)(2,1)}), bf16[1024,768]{1,0:T(8,128)(2,1)}) %all-gather.17.cloned.1.call-update) | async-done | bytes 1572880 | tf_op jit(solution)/shard_map/all_gather | solution.py:1382
  323.6 13.3 %multiply_reduce_fusion = (f32[1024]{0:T(1024)S(1)}, f32[1024,4016]{0,1:T(8,128)}) fusion(bf16[1024,768]{1,0:T(8,128)(2,1)} %all-gather.17.cloned.1.call-done, f32[4016,768]{1,0:T(8,128)} %get-tuple-element.664), kind=kOutput, calls=%fused_computation.20 | convolution fusion | flops 6327929856 | bytes 30363648 | tf_op jit(solution)/shard_map/dot_general | solution.py:78
  359.8 10.2 multiply_convert_fusion.2
  370.1 24.7 %all_to_all.110 = bf16[8,128,768]{2,1,0:T(8,128)(2,1)} all-to-all(bf16[8,128,768]{2,1,0:T(8,128)(2,1)S(1)} %bitcast.377), channel_id=1, replica_groups=mesh['dp'=4,'mp'=8] {'mp'}, dimensions={0} | all-to-all | bytes 3145728 | tf_op jit(solution)/shard_map/all_to_all | solution.py:1413
  421.0 32.7 %all_to_all.111 = bf16[4,80,768]{2,1,0:T(8,128)(2,1)} all-to-all(bf16[4,80,768]{2,1,0:T(8,128)(2,1)S(1)} %bitcast.373), channel_id=1, replica_groups=mesh['dp'=4,'mp'=8] {'dp'}, dimensions={0} | all-to-all | bytes 983040 | tf_op jit(solution)/shard_map/all_to_all | solution.py:1070
  453.7 14.3 %shard_map.389 = (bf16[8,2,768,384]{3,2,1,0:T(8,128)(2,1)}, bf16[320,768]{1,0:T(8,128)(2,1)}) custom-call(bf16[320,768]{1,0:T(8,128)(2,1)} %bitcast.361, bf16[320,768]{1,0:T(8,128)(2,1)} %bitcast.372, f32[4,320,768]{2,1,0:T(8,128)} %get-tuple-element.165.pre_ref, bf16[8,2,768,384]{3,2,1,0:T(8,128)(2,1)} %bitcast.333, bf16[8,2,768,384]{3,2,1,0:T(8,128)(2,1)} %bitcast.334), custom_call_target="tpu_custom_call" | custom-call | flops 6039797760 | bytes 24772608 | tf_op jit(solution)/shard_map/pallas_call | solution.py:449
  477.2 20.4 %all-to-all-done.13 = bf16[4,80,768]{2,1,0:T(8,128)(2,1)} async-done(((bf16[4,80,768]{2,1,0:T(8,128)(2,1)}), bf16[4,80,768]{2,1,0:T(8,128)(2,1)}, u32[]{:S(2)}, u32[]{:S(2)}) %all-to-all-start.13) | async-done | bytes 491552 | tf_op jit(solution)/shard_map/all_to_all | solution.py:1070
  505.2 11.2 %shard_map.390 = (bf16[256,768]{1,0:T(8,128)(2,1)}, bf16[768,768]{1,0:T(8,128)(2,1)}, bf16[768,768]{1,0:T(8,128)(2,1)}) custom-call(bf16[256,768]{1,0:T(8,128)(2,1)} %convolution_convert_fusion.20.refs_0_, bf16[768,1536]{1,0:T(8,128)(2,1)} %convolution_convert_fusion.2.refs_1_.refs_2_, bf16[768,1536]{1,0:T(8,128)(2,1)} %convolution_convert_fusion.2.refs_1_.refs_2_, ...), custom_call_target="tpu_custom_call" | custom-call | flops 1509949440 | bytes 6291456 | tf_op jit(solution)/shard_map/pallas_call | solution.py:317
  522.8 10.2 shard_map.391
  575.1 18.4 %all-to-all-done.14 = bf16[4,240,768]{2,1,0:T(8,128)(2,1)} async-done(((bf16[4,240,768]{2,1,0:T(8,128)(2,1)}), bf16[4,240,768]{2,1,0:T(8,128)(2,1)}, u32[]{:S(2)}, u32[]{:S(2)}) %all-to-all-start.14) | async-done | bytes 1474592 | tf_op jit(solution)/shard_map/all_to_all | solution.py:1070
  597.5 27.2 %shard_map.392 = (bf16[8,2,768,384]{3,2,1,0:T(8,128)(2,1)}, bf16[960,768]{1,0:T(8,128)(2,1)}) custom-call(bf16[960,768]{1,0:T(8,128)(2,1)} %bitcast.21.x_ref, bf16[960,768]{1,0:T(8,128)(2,1)} %bitcast.58.g_ref, f32[4,960,768]{2,1,0:T(8,128)} %get-tuple-element.177.pre_ref, bf16[8,2,768,384]{3,2,1,0:T(8,128)(2,1)} %bitcast.419, bf16[8,2,768,384]{3,2,1,0:T(8,128)(2,1)} %bitcast.420), custom_call_target="tpu_custom_call" | custom-call | flops 18119393280 | bytes 36569088 | tf_op jit(solution)/shard_map/pallas_call | solution.py:449
  641.2 23.5 %all-to-all-done.15 = bf16[4,240,768]{2,1,0:T(8,128)(2,1)} async-done(((bf16[4,240,768]{2,1,0:T(8,128)(2,1)}), bf16[4,240,768]{2,1,0:T(8,128)(2,1)}, u32[]{:S(2)}, u32[]{:S(2)}) %all-to-all-start.15) | async-done | bytes 1474592 | tf_op jit(solution)/shard_map/all_to_all | solution.py:1070
  677.7 25.4 %shard_map.393 = (bf16[768,768]{1,0:T(8,128)(2,1)}, bf16[768,768]{1,0:T(8,128)(2,1)}, bf16[768,768]{1,0:T(8,128)(2,1)}, f32[12,1,768]{2,1,0:T(1,128)}) custom-call(f32[2,12]{1,0:T(2,128)} %fusion.106.refs_0_, f32[12,1,512]{2,1,0:T(1,128)} %broadcast_in_dim.83.refs_1_, bf16[768,2304]{1,0:T(8,128)(2,1)} %convolution_convert_fusion.refs_2_.refs_3_.refs_4_, ...), custom_call_target="tpu_custom_call" | custom-call | flops 4529848320 | bytes 9437184 | tf_op jit(solution)/shard_map/pallas_call | solution.py:317
  734.3 47.8 %shard_map.394 = f32[104,128]{1,0:T(8,128)S(1)} custom-call(f32[104,128]{1,0:T(8,128)S(1)} %pad_bitcast_fusion.x_ref), custom_call_target="tpu_custom_call" | custom-call | bytes 30000000 | tf_op jit(solution)/shard_map/pallas_call | solution.py:859
  792.4 60.8 %shard_map.395 = f32[3,96,768]{2,1,0:T(8,128)} custom-call(bf16[8,4,96,768]{3,2,1,0:T(8,128)(2,1)} %pad_maximum_fusion.enc_ref, bf16[8,96,768]{2,1,0:T(8,128)(2,1)} %bitcast.386), custom_call_target="tpu_custom_call" | custom-call | bytes 200000000 | tf_op jit(solution)/shard_map/pallas_call | solution.py:1020
  876.1 19.2 %shard_map.396 = f32[8,128]{1,0:T(8,128)S(1)} custom-call(f32[8,128]{1,0:T(8,128)S(1)} %add.798.x_ref), custom_call_target="tpu_custom_call" | custom-call | bytes 30000000 | tf_op jit(solution)/shard_map/pallas_call | solution.py:859
  904.2 108.7 %shard_map.397 = (bf16[4,768,384]{2,1,0:T(8,128)(2,1)}, bf16[4,3,96,768]{3,2,1,0:T(8,128)(2,1)}, bf16[4,3,96,768]{3,2,1,0:T(8,128)(2,1)}) custom-call(bf16[4,768,384]{2,1,0:T(8,128)(2,1)} %bitcast.371, bf16[3,96,768]{2,1,0:T(8,128)(2,1)} %fusion.62.dense_ref), custom_call_target="tpu_custom_call" | custom-call | flops 40768634880 | bytes 94371840 | tf_op jit(solution)/shard_map/pallas_call | solution.py:758
  (625 shorter events, 415.2 us)
Async XLA Ops:
  7.2 78.7 %all-gather.11.cloned.1.call-start = ((), (), s32[]{:S(2)}) async-start(), calls=%async_computation.21 | async-start | bytes 5308416 | tf_op jit(solution)/shard_map/all_gather | solution.py:1302
  12.1 152.1 %all-gather.19.cloned.1.call-start = ((), (), s32[]{:S(2)}) async-start(), calls=%async_computation.29 | async-start | bytes 10616832 | tf_op jit(solution)/shard_map/all_gather | solution.py:1339
  17.1 175.9 %copy-start.64 = (s32[768]{0:T(1024)}, s32[768]{0:T(1024)S(1)}, u32[]{:S(2)}) copy-start(s32[768]{0:T(1024)S(1)} %fusion.127) | copy-start | bytes 9220
  18.3 104.3 %copy-start.127 = (s32[768]{0:T(1024)}, s32[768]{0:T(1024)S(1)}, u32[]{:S(2)}) copy-start(s32[768]{0:T(1024)S(1)} %get-tuple-element.461) | copy-start | bytes 9220
  49.1 32.0 %all-to-all-start.6 = ((bf16[8,128,768]{2,1,0:T(8,128)(2,1)}), bf16[8,128,768]{2,1,0:T(8,128)(2,1)S(1)}, u32[]{:S(2)}, u32[]{:S(2)}) async-start(bf16[8,128,768]{2,1,0:T(8,128)(2,1)} %bitcast.376), calls=%async_computation.6 | async-start | bytes 3145728 | tf_op jit(solution)/shard_map/all_to_all | solution.py:1164
  54.2 140.2 %all-gather.13.cloned.1.call-start = ((), (), s32[]{:S(2)}) async-start(), calls=%async_computation.22 | async-start | bytes 5308416 | tf_op jit(solution)/shard_map/all_gather | solution.py:1355
  54.2 111.8 %copy-start.151 = (s32[512]{0:T(512)}, s32[512]{0:T(512)S(1)}, u32[]{:S(2)}) copy-start(s32[512]{0:T(512)S(1)} %get-tuple-element.458) | copy-start | bytes 6148
  125.1 39.1 %all-to-all-start.7 = ((bf16[4,240,768]{2,1,0:T(8,128)(2,1)}), bf16[4,240,768]{2,1,0:T(8,128)(2,1)}, u32[]{:S(2)}, u32[]{:S(2)}) async-start(bf16[4,240,768]{2,1,0:T(8,128)(2,1)} %bitcast.381), calls=%async_computation.7 | async-start | bytes 2949120 | tf_op jit(solution)/shard_map/all_to_all | solution.py:1070
  130.1 101.4 %all-gather.15.cloned.1.call-start = ((), (), s32[]{:S(2)}) async-start(), calls=%async_computation.23 | async-start | bytes 5308416 | tf_op jit(solution)/shard_map/all_gather | solution.py:1359
  164.2 104.1 %all-gather.21.cloned.1.call-start = ((), (), s32[]{:S(2)}) async-start(), calls=%async_computation.30 | async-start | bytes 10616832 | tf_op jit(solution)/shard_map/all_gather | solution.py:1360
  182.6 39.1 %all-to-all-start.8 = ((bf16[4,240,768]{2,1,0:T(8,128)(2,1)}), bf16[4,240,768]{2,1,0:T(8,128)(2,1)}, u32[]{:S(2)}, u32[]{:S(2)}) async-start(bf16[4,240,768]{2,1,0:T(8,128)(2,1)} %bitcast.380), calls=%async_computation.8 | async-start | bytes 2949120 | tf_op jit(solution)/shard_map/all_to_all | solution.py:1070
  276.9 17.2 %all-to-all-start.10 = ((bf16[4,80,768]{2,1,0:T(8,128)(2,1)}), bf16[4,80,768]{2,1,0:T(8,128)(2,1)}, u32[]{:S(2)}, u32[]{:S(2)}) async-start(bf16[4,80,768]{2,1,0:T(8,128)(2,1)} %bitcast.390), calls=%async_computation.10 | async-start | bytes 983040 | tf_op jit(solution)/shard_map/all_to_all | solution.py:1070
  281.0 42.6 %all-gather.17.cloned.1.call-start = ((), (), s32[]{:S(2)}) async-start(), calls=%async_computation.24 | async-start | bytes 1769472 | tf_op jit(solution)/shard_map/all_gather | solution.py:1382
  284.2 215.0 %copy-start.85 = (f32[256,4]{0,1:T(4,128)}, f32[256,4]{0,1:T(4,128)S(1)}, u32[]{:S(2)}) copy-start(f32[256,4]{0,1:T(4,128)S(1)} %get-tuple-element.386) | copy-start | bytes 12292
  298.6 294.9 %reduce-scatter.5.cloned.1.call-start = ((), (), s32[]{:S(2)}) async-start(), calls=%async_computation.25 | async-start | bytes 7741440 | tf_op jit(solution)/shard_map/reduce_scatter | solution.py:1426
  414.1 259.5 %reduce-scatter.7.cloned.1.call-start = ((), (), s32[]{:S(2)}) async-start(), calls=%async_computation.26 | async-start | bytes 10616832 | tf_op jit(solution)/shard_map/reduce_scatter | solution.py:1432
  419.8 79.4 %copy-start.114 = (f32[256]{0:T(256)}, f32[256]{0:T(256)S(1)}, u32[]{:S(2)}) copy-start(f32[256]{0:T(256)S(1)} %get-tuple-element.381) | copy-start | bytes 3076
  468.1 29.5 %all-to-all-start.13 = ((bf16[4,80,768]{2,1,0:T(8,128)(2,1)}), bf16[4,80,768]{2,1,0:T(8,128)(2,1)}, u32[]{:S(2)}, u32[]{:S(2)}) async-start(bf16[4,80,768]{2,1,0:T(8,128)(2,1)} %bitcast.389), calls=%async_computation.13 | async-start | bytes 983040 | tf_op jit(solution)/shard_map/all_to_all | solution.py:1070
  472.3 320.1 %reduce-scatter.9.cloned.1.call-start = ((), (), s32[]{:S(2)}) async-start(), calls=%async_computation.27 | async-start | bytes 10616832 | tf_op jit(solution)/shard_map/reduce_scatter | solution.py:1263
  555.0 38.6 %all-to-all-start.14 = ((bf16[4,240,768]{2,1,0:T(8,128)(2,1)}), bf16[4,240,768]{2,1,0:T(8,128)(2,1)}, u32[]{:S(2)}, u32[]{:S(2)}) async-start(bf16[4,240,768]{2,1,0:T(8,128)(2,1)} %bitcast.378), calls=%async_computation.14 | async-start | bytes 2949120 | tf_op jit(solution)/shard_map/all_to_all | solution.py:1070
  593.5 31.2 %all-to-all-start.4 = ((s32[32,1,48]{2,1,0:T(1,128)}), s32[32,1,48]{2,1,0:T(1,128)}, u32[]{:S(2)}, u32[]{:S(2)}) async-start(s32[32,1,48]{2,1,0:T(1,128)} %all_to_all.65), calls=%async_computation.4 | async-start | bytes 32768 | tf_op jit(solution)/shard_map/all_to_all | solution.py:1164
  624.7 39.9 %all-to-all-start.15 = ((bf16[4,240,768]{2,1,0:T(8,128)(2,1)}), bf16[4,240,768]{2,1,0:T(8,128)(2,1)}, u32[]{:S(2)}, u32[]{:S(2)}) async-start(bf16[4,240,768]{2,1,0:T(8,128)(2,1)} %bitcast.379), calls=%async_computation.16 | async-start | bytes 2949120 | tf_op jit(solution)/shard_map/all_to_all | solution.py:1070
  629.4 244.4 %reduce-scatter.11.cloned.1.call-start = ((), (), s32[]{:S(2)}) async-start(), calls=%async_computation.28 | async-start | bytes 10616832 | tf_op jit(solution)/shard_map/reduce_scatter | solution.py:1456
  719.8 133.4 %all-to-all-start.16 = ((bf16[32,48,768]{2,1,0:T(8,128)(2,1)}), bf16[32,48,768]{2,1,0:T(8,128)(2,1)}, u32[]{:S(2)}, u32[]{:S(2)}) async-start(bf16[32,48,768]{2,1,0:T(8,128)(2,1)} %bitcast.367), calls=%async_computation.18 | async-start | bytes 4718592 | tf_op jit(solution)/shard_map/all_to_all | solution.py:1164
  (163 other events, 1419.8 us)
Sparse Core Ops, SparseCore 0:
  12.2 40.1 all-gather.10
  54.8 66.8 all-gather.18
  123.6 38.9 all-gather.12
  164.9 38.9 all-gather.14
  206.2 58.7 all-gather.20
  298.7 24.8 all-gather.16
  414.2 124.9 reduce-scatter.4
  543.2 80.8 reduce-scatter.6
  628.0 76.4 reduce-scatter.8
  708.3 99.4 reduce-scatter.10

commit v3 on v2

--- a/solution.py
+++ b/solution.py
@@ -534,11 +534,21 @@
 def newton_kernel(
     groups,
     experts,
-    expert_ref,
-    dense_ref,
+    squares_ref,
+    expert_old_ref,
+    expert_grad_ref,
+    dense_old_ref,
+    dense_grad_ref,
+    squares_out,
+    expert_moment_out,
     expert_out,
     dense_out,
     moment_out,
+    expert_ref,
+    dense_ref,
+    squares_row,
+    squares_sum,
+    squares_col,
     held,
     held_dense,
     matrix,
@@ -557,6 +567,10 @@
     orth_sem,
     moment_send_sem,
     moment_sem,
+    row_send_sem,
+    row_sem,
+    col_send_sem,
+    col_sem,
 ):
     me = lax.axis_index("mp")
     along = lax.axis_index("dp")
@@ -589,6 +603,57 @@
             device_id_type=pl.DeviceIdType.MESH,
         )
 
+    def to_row(step, source):
+        return remote(
+            squares_ref,
+            squares_row.at[source],
+            row_send_sem.at[step],
+            row_sem.at[source],
+            lax.rem(me + step, groups),
+        )
+
+    def to_col(step, source):
+        return pltpu.make_async_remote_copy(
+            src_ref=squares_sum,
+            dst_ref=squares_col.at[source],
+            send_sem=col_send_sem.at[step],
+            recv_sem=col_sem.at[source],
+            device_id={"dp": lax.rem(along + step, experts)},
+            device_id_type=pl.DeviceIdType.MESH,
+        )
+
+    for step in range(1, groups):
+        to_row(step, me).start()
+    squares_row[me] = squares_ref[...]
+    for step in range(1, groups):
+        to_row(step, lax.rem(me + step, groups)).wait_recv()
+    squares = squares_row[0]
+    for source in range(1, groups):
+        squares = squares + squares_row[source]
+    squares_sum[...] = squares
+    squares_col[along] = squares
+    for step in range(1, experts):
+        to_col(step, along).start()
+    for step in range(1, experts):
+        to_col(step, lax.rem(along + step, experts)).wait_recv()
+    squares = squares_col[0]
+    for source in range(1, experts):
+        squares = squares + squares_col[source]
+    squares_out[...] = squares
+    norm = jnp.sqrt(jnp.sum(squares, keepdims=True))
+    clip = 1.0 / jnp.maximum(norm, 1.0)
+    for index in range(count_dense):
+        moment = 0.5 * dense_old_ref[index] + clip * dense_grad_ref[index]
+        dense_ref[index] = moment.astype(jnp.bfloat16)
+    for index in range(count_expert):
+        moment = 0.5 * expert_old_ref[index] + clip * expert_grad_ref[index].astype(jnp.float32)
+        expert_moment_out[index] = moment
+        expert_ref[index] = moment.astype(jnp.bfloat16)
+    for step in range(1, groups):
+        to_row(step, me).wait_send()
+    for step in range(1, experts):
+        to_col(step, along).wait_send()
+
     def outward(index, source):
         dense = index >= count_expert
         place = index - count_expert if dense else index
@@ -749,38 +814,49 @@
     moment_out[...] = all_moment[...]
 
 
-def newton(dense_mom, expert_mom, groups, experts):
-    cols, cols_dense = expert_mom.shape[2], dense_mom.shape[1]
-    count_expert, count_dense = expert_mom.shape[0], dense_mom.shape[0]
+def newton(squares, expert_old, expert_grad, dense_old, dense_grad, groups, experts):
+    cols, cols_dense = expert_old.shape[2], dense_old.shape[1]
+    count_expert, count_dense = expert_old.shape[0], dense_old.shape[0]
     low = jnp.bfloat16
     vmem = pl.BlockSpec(memory_space=pltpu.VMEM)
     dma = pltpu.SemaphoreType.DMA
     return pl.pallas_call(
         partial(newton_kernel, groups, experts),
-        in_specs=[vmem, vmem],
-        out_specs=[vmem, vmem, vmem],
+        in_specs=[vmem] * 5,
+        out_specs=[vmem] * 5,
         out_shape=[
-            jax.ShapeDtypeStruct(expert_mom.shape, low),
-            jax.ShapeDtypeStruct((experts,) + dense_mom.shape, low),
-            jax.ShapeDtypeStruct((experts,) + dense_mom.shape, low),
+            jax.ShapeDtypeStruct(squares.shape, jnp.float32),
+            jax.ShapeDtypeStruct(expert_old.shape, jnp.float32),
+            jax.ShapeDtypeStruct(expert_old.shape, low),
+            jax.ShapeDtypeStruct((experts,) + dense_old.shape, low),
+            jax.ShapeDtypeStruct((experts,) + dense_old.shape, low),
         ],
         scratch_shapes=[
+            pltpu.VMEM(expert_old.shape, low),
+            pltpu.VMEM(dense_old.shape, low),
+            pltpu.VMEM((groups,) + squares.shape, jnp.float32),
+            pltpu.VMEM(squares.shape, jnp.float32),
+            pltpu.VMEM((experts,) + squares.shape, jnp.float32),
             pltpu.VMEM((groups, D, cols), low),
             pltpu.VMEM((groups, cols_dense, D), low),
             pltpu.VMEM((D, groups * cols), low),
             pltpu.VMEM((D, D), low),
             pltpu.VMEM((D, D), jnp.float32),
             pltpu.VMEM((D, D), low),
-            pltpu.VMEM(expert_mom.shape, low),
-            pltpu.VMEM(dense_mom.shape, low),
-            pltpu.VMEM((experts,) + dense_mom.shape, low),
-            pltpu.VMEM((experts,) + dense_mom.shape, low),
+            pltpu.VMEM(expert_old.shape, low),
+            pltpu.VMEM(dense_old.shape, low),
+            pltpu.VMEM((experts,) + dense_old.shape, low),
+            pltpu.VMEM((experts,) + dense_old.shape, low),
             dma((count_expert + count_dense,)),
             dma((groups,)),
             dma((groups,)),
             dma((count_expert + count_dense,)),
             dma((experts,)),
             dma((experts,)),
+            dma((experts,)),
+            dma((experts,)),
+            dma((groups,)),
+            dma((groups,)),
             dma((experts,)),
             dma((experts,)),
         ],
@@ -792,89 +868,81 @@
             bytes_accessed=40 * D * FF,
             transcendentals=0,
         ),
-    )(expert_mom.astype(low), dense_mom.astype(low))
-
-
-def total_kernel(
-    groups, experts, x_ref, out_ref, land_row, land_col, send_sem, row_sem, send_col_sem, col_sem
-):
-    across, along = lax.axis_index("mp"), lax.axis_index("dp")
+    )(squares, expert_old, expert_grad, dense_old, dense_grad)
+
+
+def gather_kernel(groups, x_ref, out_ref, land, send_sem, pass_sem, land_sem):
+    me = lax.axis_index("mp")
+    half, side = me // 2, me % 2
+    halves = groups // 2
+    sibling = me + 1 - 2 * side
     barrier = pltpu.get_barrier_semaphore()
     mesh_id = pl.DeviceIdType.MESH
-    for step in range(1, groups):
-        other = lax.rem(across + step, groups)
+    for step in range(1, halves):
+        other = 2 * lax.rem(half + step, halves) + side
         pl.semaphore_signal(barrier, inc=1, device_id={"mp": other}, device_id_type=mesh_id)
-    for step in range(1, experts):
-        other = lax.rem(along + step, experts)
-        pl.semaphore_signal(barrier, inc=1, device_id={"dp": other}, device_id_type=mesh_id)
-    pl.semaphore_wait(barrier, groups + experts - 2)
-
-    def to_row(step, source):
+    pl.semaphore_signal(barrier, inc=1, device_id={"mp": sibling}, device_id_type=mesh_id)
+    pl.semaphore_wait(barrier, halves)
+
+    def remote(source, index, sent, device):
         return pltpu.make_async_remote_copy(
-            src_ref=x_ref,
-            dst_ref=land_row.at[source],
-            send_sem=send_sem.at[step],
-            recv_sem=row_sem.at[source],
-            device_id={"mp": lax.rem(across + step, groups)},
+            src_ref=source,
+            dst_ref=land.at[index],
+            send_sem=sent,
+            recv_sem=land_sem.at[index],
+            device_id={"mp": device},
             device_id_type=mesh_id,
         )
 
-    def to_col(step, source):
-        return pltpu.make_async_remote_copy(
-            src_ref=out_ref,
-            dst_ref=land_col.at[source],
-            send_sem=send_col_sem.at[step],
-            recv_sem=col_sem.at[source],
-            device_id={"dp": lax.rem(along + step, experts)},
-            device_id_type=mesh_id,
-        )
-
-    for step in range(1, groups):
-        to_row(step, across).start()
-    land_row[across] = x_ref[...]
-    for step in range(1, groups):
-        to_row(step, lax.rem(across + step, groups)).wait_recv()
-    total = land_row[0]
-    for source in range(1, groups):
-        total = total + land_row[source]
-    out_ref[...] = total
-    for step in range(1, experts):
-        to_col(step, along).start()
-    land_col[along] = total
-    for step in range(1, experts):
-        to_col(step, lax.rem(along + step, experts)).wait_recv()
-    for step in range(1, groups):
-        to_row(step, across).wait_send()
-    for step in range(1, experts):
-        to_col(step, along).wait_send()
-    total = land_col[0]
-    for source in range(1, experts):
-        total = total + land_col[source]
-    out_ref[...] = total
-
-
-def total_of(array, groups, experts, collective):
+    def direct(step):
+        return remote(x_ref, me, send_sem.at[step], 2 * lax.rem(half + step, halves) + side)
+
+    def passed(step):
+        index = 2 * lax.rem(half + step, halves) + side
+        return remote(land.at[index], index, pass_sem.at[step], sibling)
+
+    for step in range(1, halves):
+        direct(step).start()
+    to_sibling = remote(x_ref, me, send_sem.at[0], sibling)
+    to_sibling.start()
+    land[me] = x_ref[...]
+    for step in range(1, halves):
+        index = 2 * lax.rem(half + step, halves) + side
+        remote(x_ref, index, send_sem.at[step], sibling).wait_recv()
+        passed(step).start()
+    for step in range(halves):
+        index = 2 * lax.rem(half + step, halves) + 1 - side
+        remote(x_ref, index, send_sem.at[step], sibling).wait_recv()
+    to_sibling.wait_send()
+    for step in range(1, halves):
+        direct(step).wait_send()
+        passed(step).wait_send()
+    out_ref[...] = land[...]
+
+
+def gathered_over(array, groups, collective):
     vmem = pl.BlockSpec(memory_space=pltpu.VMEM)
     dma = pltpu.SemaphoreType.DMA
+    shape = (groups,) + array.shape
     return pl.pallas_call(
-        partial(total_kernel, groups, experts),
+        partial(gather_kernel, groups),
         in_specs=[vmem],
         out_specs=vmem,
-        out_shape=jax.ShapeDtypeStruct(array.shape, array.dtype),
+        out_shape=jax.ShapeDtypeStruct(shape, array.dtype),
         scratch_shapes=[
-            pltpu.VMEM((groups,) + array.shape, array.dtype),
-            pltpu.VMEM((experts,) + array.shape, array.dtype),
+            pltpu.VMEM(shape, array.dtype),
+            dma((groups // 2,)),
+            dma((groups // 2,)),
             dma((groups,)),
-            dma((groups,)),
-            dma((experts,)),
-            dma((experts,)),
         ],
         compiler_params=pltpu.CompilerParams(
-            vmem_limit_bytes=16 * 1024 * 1024, collective_id=collective, has_side_effects=True
+            vmem_limit_bytes=(
+                4 * math.prod(shape) * array.dtype.itemsize + 2 * 1024 * 1024
+            ),
+            collective_id=collective,
+            has_side_effects=True,
         ),
-        cost_estimate=pl.CostEstimate(
-            flops=0, bytes_accessed=30000000, transcendentals=0
-        ),
+        cost_estimate=pl.CostEstimate(flops=0, bytes_accessed=20000000, transcendentals=0),
     )(array)
 
 
@@ -927,20 +995,35 @@
     experts,
     enc_ref,
     dec_ref,
+    small_ref,
     out_ref,
+    small_out,
+    land_pair,
+    paired,
     land,
     summed,
     land_enc,
     land_dec,
+    small_row,
+    small_sum,
+    small_col,
+    pair_send_sem,
+    pair_sem,
     send_sem,
     land_sem,
     enc_send_sem,
     enc_sem,
     dec_send_sem,
     dec_sem,
+    row_send_sem,
+    row_sem,
+    col_send_sem,
+    col_sem,
 ):
     across, along = lax.axis_index("mp"), lax.axis_index("dp")
-    count = enc_ref.shape[1]
+    half, side = across // 2, across % 2
+    halves = groups // 2
+    count = enc_ref.shape[2]
     per_enc, per_dec = land_enc.shape[1], land_dec.shape[1]
     barrier = pltpu.get_barrier_semaphore()
     mesh_id = pl.DeviceIdType.MESH
@@ -952,41 +1035,94 @@
         pl.semaphore_signal(barrier, inc=1, device_id={"dp": other}, device_id_type=mesh_id)
     pl.semaphore_wait(barrier, groups + experts - 2)
 
-    def to_row(step, source):
-        other = lax.rem(across + step, groups)
+    def remote(source, target, sent, landed, device):
         return pltpu.make_async_remote_copy(
-            src_ref=enc_ref.at[other],
-            dst_ref=land.at[source],
-            send_sem=send_sem.at[step],
-            recv_sem=land_sem.at[source],
-            device_id={"mp": other},
+            src_ref=source,
+            dst_ref=target,
+            send_sem=sent,
+            recv_sem=landed,
+            device_id=device,
             device_id_type=mesh_id,
+        )
+
+    def to_small_row(step, source):
+        return remote(
+            small_ref,
+            small_row.at[source],
+            row_send_sem.at[step],
+            row_sem.at[source],
+            {"mp": lax.rem(across + step, groups)},
+        )
+
+    def to_small_col(step, source):
+        return remote(
+            small_sum,
+            small_col.at[source],
+            col_send_sem.at[step],
+            col_sem.at[source],
+            {"dp": lax.rem(along + step, experts)},
+        )
+
+    def to_half(step, source):
+        other = lax.rem(half + step, halves)
+        return remote(
+            paired.at[other],
+            land.at[source],
+            send_sem.at[step],
+            land_sem.at[source],
+            {"mp": 2 * other + side},
         )
 
     def to_col(step, source, dec):
         other = lax.rem(along + step, experts)
         per = per_dec if dec else per_enc
-        return pltpu.make_async_remote_copy(
-            src_ref=(dec_ref if dec else summed).at[pl.ds(other * per, per)],
-            dst_ref=(land_dec if dec else land_enc).at[source],
-            send_sem=(dec_send_sem if dec else enc_send_sem).at[step],
-            recv_sem=(dec_sem if dec else enc_sem).at[source],
-            device_id={"dp": other},
-            device_id_type=mesh_id,
+        return remote(
+            (dec_ref if dec else summed).at[pl.ds(other * per, per)],
+            (land_dec if dec else land_enc).at[source],
+            (dec_send_sem if dec else enc_send_sem).at[step],
+            (dec_sem if dec else enc_sem).at[source],
+            {"dp": other},
         )
 
+    to_pair = remote(
+        enc_ref.at[1 - side],
+        land_pair,
+        pair_send_sem.at[0],
+        pair_sem.at[0],
+        {"mp": across + 1 - 2 * side},
+    )
+    to_pair.start()
     for step in range(1, groups):
-        to_row(step, across).start()
+        to_small_row(step, across).start()
     for step in range(1, experts):
         to_col(step, along, True).start()
-    land[across] = enc_ref[across]
+    small_row[across] = small_ref[...]
     land_dec[along] = dec_ref[pl.ds(along * per_dec, per_dec)]
+    to_pair.wait_recv()
+    for step in range(1, halves + 1):
+        other = lax.rem(half + step, halves)
+        for index in range(count):
+            paired[other, index] = (
+                enc_ref[side, other, index].astype(jnp.float32)
+                + land_pair[other, index].astype(jnp.float32)
+            ).astype(jnp.bfloat16)
+        if step < halves:
+            to_half(step, half).start()
+    land[half] = paired[half]
     for step in range(1, groups):
-        to_row(step, lax.rem(across + step, groups)).wait_recv()
-
+        to_small_row(step, lax.rem(across + step, groups)).wait_recv()
+    total = small_row[0]
+    for source in range(1, groups):
+        total = total + small_row[source]
+    small_sum[...] = total
+    small_col[along] = total
+    for step in range(1, experts):
+        to_small_col(step, along).start()
+    for step in range(1, halves):
+        to_half(step, lax.rem(half + step, halves)).wait_recv()
     for index in range(count):
         total = land[0, index].astype(jnp.float32)
-        for source in range(1, groups):
+        for source in range(1, halves):
             total = total + land[source, index].astype(jnp.float32)
         summed[index] = total.astype(jnp.bfloat16)
     for index in range(count, summed.shape[0]):
@@ -994,14 +1130,23 @@
     for step in range(1, experts):
         to_col(step, along, False).start()
     land_enc[along] = summed[pl.ds(along * per_enc, per_enc)]
+    to_pair.wait_send()
     for step in range(1, groups):
-        to_row(step, across).wait_send()
+        to_small_row(step, across).wait_send()
+    for step in range(1, halves):
+        to_half(step, half).wait_send()
     for step in range(1, experts):
         source = lax.rem(along + step, experts)
+        to_small_col(step, source).wait_recv()
         to_col(step, source, True).wait_recv()
         to_col(step, source, False).wait_recv()
+        to_small_col(step, along).wait_send()
         to_col(step, along, True).wait_send()
         to_col(step, along, False).wait_send()
+    total = small_col[0]
+    for source in range(1, experts):
+        total = total + small_col[source]
+    small_out[...] = total
     for landed, per, first in ((land_enc, per_enc, 0), (land_dec, per_dec, per_enc)):
         for index in range(per):
             total = landed[0, index].astype(jnp.float32)
@@ -1010,27 +1155,42 @@
             out_ref[first + index] = total
 
 
-def dense_total(enc, dec, groups, experts):
-    count, cols = enc.shape[1], enc.shape[2]
+def dense_total(enc, dec, small, groups, experts):
+    count, cols = enc.shape[2], enc.shape[3]
     per_enc, per_dec = -(-count // experts), -(-dec.shape[0] // experts)
     dec = jnp.pad(dec, ((0, per_dec * experts - dec.shape[0]), (0, 0), (0, 0)))
     vmem = pl.BlockSpec(memory_space=pltpu.VMEM)
     dma = pltpu.SemaphoreType.DMA
     low = jnp.bfloat16
+    halves = groups // 2
     return pl.pallas_call(
         partial(dense_kernel, groups, experts),
-        in_specs=[vmem, vmem],
-        out_specs=vmem,
-        out_shape=jax.ShapeDtypeStruct((per_enc + per_dec, cols, D), jnp.float32),
+        in_specs=[vmem, vmem, vmem],
+        out_specs=[vmem, vmem],
+        out_shape=[
+            jax.ShapeDtypeStruct((per_enc + per_dec, cols, D), jnp.float32),
+            jax.ShapeDtypeStruct(small.shape, jnp.float32),
+        ],
         scratch_shapes=[
-            pltpu.VMEM(enc.shape, low),
+            pltpu.VMEM(enc.shape[1:], low),
+            pltpu.VMEM(enc.shape[1:], low),
+            pltpu.VMEM(enc.shape[1:], low),
             pltpu.VMEM((per_enc * experts, cols, D), low),
             pltpu.VMEM((experts, per_enc, cols, D), low),
             pltpu.VMEM((experts, per_dec, cols, D), low),
+            pltpu.VMEM((groups,) + small.shape, jnp.float32),
+            pltpu.VMEM(small.shape, jnp.float32),
+            pltpu.VMEM((experts,) + small.shape, jnp.float32),
+            dma((1,)),
+            dma((1,)),
+            dma((halves,)),
+            dma((halves,)),
+            dma((experts,)),
+            dma((experts,)),
+            dma((experts,)),
+            dma((experts,)),
             dma((groups,)),
             dma((groups,)),
-            dma((experts,)),
-            dma((experts,)),
             dma((experts,)),
             dma((experts,)),
         ],
@@ -1040,7 +1200,7 @@
         cost_estimate=pl.CostEstimate(
             flops=0, bytes_accessed=200000000, transcendentals=0
         ),
-    )(enc, dec)
+    )(enc, dec, small)
 
 
 def piece_of(array, count, experts):
@@ -1311,31 +1471,42 @@
     local_ids = own_ids - shard * vocab_dev
     piece_ids = own_ids - owner * piece_rows
     owner = (owner % experts) * groups + owner // experts
-    needs = jnp.stack([jnp.max(rank) // FETCH + 1, jnp.max(owner_rank) // GIVE + 1])
+    fetch_turns = jnp.max(rank) // FETCH + 1
+    give_turns = jnp.max(owner_rank) // GIVE + 1
+    give_hot = (jnp.arange(piece_rows // GIVE + 2, dtype=jnp.int32) == give_turns).astype(
+        jnp.float32
+    )
 
     def asked_of(turn):
         return ids_in(slots_of(shard, rank, groups, FETCH, turn), local_ids, FETCH)
 
-    def fetched(turn, wanted):
+    def fetched(wanted):
         rows = lookup(wanted.reshape(-1), table_w)
-        rows = exchange(rows.reshape(groups, FETCH, D), "mp")
+        return exchange(rows.reshape(groups, FETCH, D), "mp").reshape(-1, D)
+
+    def placed(turn, rows):
         hot = slots_of(shard, rank, groups, FETCH, turn).astype(low)
-        return dot_tn(hot, rows.reshape(-1, D))
-
-    noted = jnp.broadcast_to(jnp.pad(needs, (0, LANES - 2))[None, :], (groups, LANES))
+        return dot_tn(hot, rows).astype(low)
+
+    noted = jnp.full((groups, LANES), fetch_turns)
     asked = exchange(jnp.concatenate([asked_of(0), noted], axis=1), "mp")
-    needs = jnp.max(asked[:, FETCH:], axis=0, keepdims=True)
-    embedded = fetched(0, asked[:, :FETCH])
-    embedded, enc_dense = lax.optimization_barrier((embedded, enc_dense))
-    needs = jnp.max(lax.all_gather(jnp.tile(needs, (8, 1)), "dp", axis=0, tiled=True), axis=0)
+    fetch_turns = jnp.max(asked[:, FETCH:])
+    rows = fetched(asked[:, :FETCH])
 
     def fetch_more(state):
-        turn, rows = state
-        return turn + 1, rows + fetched(turn, exchange(asked_of(turn), "mp"))
-
-    turns, embedded = lax.while_loop(
-        lambda state: state[0] < needs[0], fetch_more, (jnp.int32(1), embedded)
-    )
+        turn, more = state
+        return turn + 1, more + placed(turn, fetched(exchange(asked_of(turn), "mp")))
+
+    nothing = jnp.zeros((own_ids.shape[0], D), low)
+    more = lax.cond(
+        fetch_turns > 1,
+        lambda: lax.while_loop(
+            lambda state: state[0] < fetch_turns, fetch_more, (jnp.int32(1), nothing)
+        )[1],
+        lambda: nothing,
+    )
+    rows, more, enc_dense = lax.optimization_barrier((rows, more, enc_dense))
+    embedded = (placed(0, rows) + more).astype(jnp.float32)
     enc_expert = lax.all_gather(expert_local[0], "mp", axis=0, tiled=False)
     own_src = lax.dynamic_slice_in_dim(routes_src, own_seq, 1, 0).reshape(-1)
     own_tgt = lax.dynamic_slice_in_dim(routes_tgt, own_seq, 1, 0).reshape(-1)
@@ -1358,10 +1529,14 @@
     )
     cross_dense = lax.all_gather(cross_local, "mp", axis=1, tiled=True)
     dec_expert = lax.all_gather(dec_expert_local, "mp", axis=0, tiled=False)
-    table_low = late_table.astype(low)
+    padded = -(-piece_rows // 16) * 16
+    table_low = jnp.pad(
+        late_table.astype(low).reshape(experts, piece_rows, D),
+        ((0, 0), (0, padded - piece_rows), (0, 0)),
+    ).reshape(-1, D)
     pre, returned = moe_expert(enc_expert, cap_src, arrived)
     dec_mid, dec_kept = self_forward(embedded[src_len:], gains_w[3], dec_dense, dec_parts, True)
-    returned, dec_mid = lax.optimization_barrier((returned, dec_mid))
+    returned, dec_mid, table_low = lax.optimization_barrier((returned, dec_mid, table_low))
     enc_out, enc_moe = moe_receive(enc_mid, places_src, arrived, pre, returned, enc_sent)
     memory_float, memory_inv = normalize(enc_out, gains_w[2])
     memory = memory_float.astype(low)
@@ -1379,24 +1554,29 @@
         own_pos[:, None] == lax.broadcasted_iota(jnp.int32, (npos, tgt_len), 1)
     ).astype(low)
     chosen = dot_nn(pick, final_low).astype(low)
-    gathered = lax.all_gather(chosen, "mp", axis=0, tiled=True)
-    logits = dot_nt(gathered, table_low) * head_scale
+    gathered = gathered_over(chosen, groups, 5).reshape(-1, D)
+    place = jnp.arange(experts * padded, dtype=jnp.int32)
+    logits = jnp.where(
+        (place % padded < piece_rows)[None, :], dot_nt(gathered, table_low) * head_scale, -1e30
+    )
     at_pos = loss_pos[:, :, None] == lax.broadcasted_iota(jnp.int32, (1, 1, tgt_len), 2)
     wanted = jnp.sum(jnp.where(at_pos, targets[:, None, :], 0), axis=2).reshape(-1)
     wanted = wanted - column * vocab_dev
-    hits = jnp.arange(vocab_dev, dtype=jnp.int32)[None, :] == wanted[:, None]
+    here = (wanted >= 0) & (wanted < vocab_dev)
+    wanted = jnp.where(here, wanted + wanted // piece_rows * (padded - piece_rows), -1)
+    hits = place[None, :] == wanted[:, None]
     top = jnp.max(logits, axis=1)
-    stats = lax.all_gather(
+    stats = gathered_over(
         jnp.stack(
             [
                 top,
                 jnp.sum(jnp.exp(logits - top[:, None]), axis=1),
                 jnp.sum(jnp.where(hits, logits, 0.0), axis=1),
             ]
+            + [jnp.zeros_like(top)] * 5
         ),
-        "mp",
-        axis=0,
-        tiled=False,
+        groups,
+        6,
     )
     all_top = jnp.max(stats[:, 0], axis=0)
     expsum = jnp.sum(stats[:, 1] * jnp.exp(stats[:, 0] - all_top[None, :]), axis=0)
@@ -1410,19 +1590,11 @@
     d_logits = (
         mask_rows[:, None] * (jnp.exp(logits - logsum[:, None]) - hits.astype(jnp.float32))
     ).astype(low)
-    d_shares = lax.all_to_all(
-        (dot_nn(d_logits, table_low) * head_scale).astype(low).reshape(groups, npos, D),
-        "mp",
-        split_axis=0,
-        concat_axis=0,
-        tiled=True,
-    )
-    d_logits, d_shares = lax.optimization_barrier((d_logits, d_shares))
+    d_gathered = (dot_nn(d_logits, table_low) * head_scale).astype(low)
+    d_gathered, d_logits = lax.optimization_barrier((d_gathered, d_logits))
+    d_shares = exchange(d_gathered.reshape(groups, npos, D), "mp")
     table_grad = (dot_tn(d_logits, gathered) * head_scale).astype(low)
-    padded = -(-piece_rows // 16) * 16
-    table_grad = jnp.pad(
-        table_grad.reshape(experts, piece_rows, D), ((0, 0), (0, padded - piece_rows), (0, 0))
-    ).reshape(-1, D)
+    d_shares, table_grad = lax.optimization_barrier((d_shares, table_grad))
     table_share = lax.psum_scatter(table_grad, "dp", scatter_dimension=0, tiled=True)
     d_chosen = jnp.sum(d_shares.astype(jnp.float32), axis=0).astype(low)
     d_final = dot_tn(pick, d_chosen)
@@ -1471,7 +1643,11 @@
         gains_w[0], enc_dense, enc_parts, False, enc_kept, d_enc
     )
     enc_parts = jnp.stack(
-        [part.astype(low).reshape(groups, -1, D) for part in enc_self_dw], axis=1
+        [
+            jnp.swapaxes(part.astype(low).reshape(groups // 2, 2, -1, D), 0, 1)
+            for part in enc_self_dw
+        ],
+        axis=2,
     )
     d_embedded = jnp.concatenate([d_enc, d_dec], axis=0).astype(low)
 
@@ -1493,13 +1669,24 @@
     bias_grad = jnp.stack([enc_bias, dec_bias])
     load_src = jnp.sum(enc_moe[2], axis=0)
     load_tgt = jnp.sum(dec_moe[2], axis=0)
-    small = [gains_grad, router_grad, bias_grad, load_src, load_tgt, own_loss, own_count]
-    summed = total_of(in_lanes(small), groups, experts, 2)
-    dense_piece = dense_total(enc_parts, dec_cols, groups, experts)
+    small = [
+        gains_grad,
+        router_grad,
+        bias_grad,
+        load_src,
+        load_tgt,
+        own_loss,
+        own_count,
+        give_hot,
+    ]
+    dense_piece, summed = dense_total(enc_parts, dec_cols, in_lanes(small), groups, experts)
     arrived, summed, dense_piece = lax.optimization_barrier((arrived, summed, dense_piece))
     table_piece = rows_into(landed, arrived, piece_rows)
-    gains_grad, router_grad, bias_grad, load_src, load_tgt, loss_sum, count = from_lanes(
+    gains_grad, router_grad, bias_grad, load_src, load_tgt, loss_sum, count, give_hot = from_lanes(
         summed, small
+    )
+    give_turns = jnp.max(
+        jnp.where(give_hot > 0.0, jnp.arange(give_hot.shape[0], dtype=jnp.int32), 0)
     )
 
     def give_more(state):
@@ -1507,21 +1694,31 @@
         return turn + 1, total + rows_into(given_ids(turn), given_rows(turn), piece_rows)
 
     turns, table_piece = lax.while_loop(
-        lambda state: state[0] < needs[1], give_more, (jnp.int32(1), table_piece)
-    )
+        lambda state: state[0] < give_turns, give_more, (jnp.int32(1), table_piece)
+    )
+
     table_piece = table_piece + table_share[:piece_rows].astype(jnp.float32)
-    expert_share = jnp.stack([enc_share, dec_share]).astype(jnp.float32)
-    squares = jnp.zeros((8, LANES), jnp.float32)
+    expert_share = jnp.stack([enc_share, dec_share])
+    own_squares = sum((jnp.sum(part * part) for part in (gains_grad, router_grad, bias_grad)))
+    squares = jnp.full((8, LANES), own_squares / (8 * LANES * devices))
     for part in (dense_piece, expert_share, table_piece):
-        lanes = jnp.sum((part * part).reshape(-1, part.shape[-1]), axis=0)
-        squares = squares + jnp.pad(
-            jnp.sum(lanes.reshape(-1, min(LANES, math.gcd(lanes.shape[0], LANES))), axis=0),
-            (0, LANES - math.gcd(lanes.shape[0], LANES)),
-        )[None, :] * 0.125
-    squares = jnp.sum(total_of(squares, groups, experts, 3))
-    squares = squares + sum(
-        (jnp.sum(part * part) for part in (gains_grad, router_grad, bias_grad))
-    )
+        lanes = jnp.sum(jnp.square(part.astype(jnp.float32)).reshape(-1, part.shape[-1]), axis=0)
+        width = math.gcd(lanes.shape[0], LANES)
+        lanes = jnp.pad(jnp.sum(lanes.reshape(-1, width), axis=0), (0, LANES - width))
+        squares = squares + lanes[None, :] * 0.125
+    cols = expert_w.shape[4]
+    old_piece = piece_of(dense_m, 4, experts).reshape(dense_piece.shape)
+    squares, expert_moment, expert_orth, dense_orth, dense_moment = newton(
+        squares,
+        expert_m.reshape(-1, D, cols),
+        expert_share.reshape(-1, D, cols),
+        old_piece,
+        dense_piece,
+        groups,
+        experts,
+    )
+    expert_moment = expert_moment.reshape(expert_w.shape)
+    squares = jnp.sum(squares)
     grad_norm = jnp.sqrt(squares)
     clip = 1.0 / jnp.maximum(grad_norm, 1.0)
     aux = (
@@ -1530,13 +1727,6 @@
         * (jnp.sum(frac_src * load_src) / total_src + jnp.sum(frac_tgt * load_tgt) / total_tgt)
     )
     loss = jnp.stack([loss_sum + aux, count])
-    old_piece = piece_of(dense_m, 4, experts).reshape(dense_piece.shape)
-    piece_moment = 0.5 * old_piece + clip * dense_piece
-    expert_moment = 0.5 * expert_m + clip * expert_share[:, :, None]
-    cols = expert_w.shape[4]
-    expert_orth, dense_orth, dense_moment = newton(
-        piece_moment, expert_moment.reshape(-1, D, cols), groups, experts
-    )
 
     def as_stored(pieces):
         return whole_of(pieces, 4, count_dense - 4).reshape(count_dense, -1).astype(jnp.float32)

time: 1060 us -> 982 us (0.926)
  blocking collectives: 103 us -> 28.4 us
  Pallas kernels: 392 us -> 366 us
  local copies, waits for them, and re-layouts: 71.8 us -> 87.2 us
  starting transfers between devices: 41.9 us -> 55.2 us
    pallas_call x3, Pallas kernels: 176 us -> 144 us  [the longest x1 124 us: newton(): pl.pallas_call(partial(newton_kernel, groups, experts), in_specs=[vmem] *...]
    all_to_all x2 -> x0, blocking collectives: 32 us -> none  [the longest x1 24.7 us: on_device(): lax.all_to_all((dot_nn(d_logits, table_low) * head_scale).astype(low).res...]
    all_to_all x3 -> x5, waiting for transfers between devices: 9.62 us -> 34.9 us  [exchange(): return lax.all_to_all(array, axes, split_axis=0, concat_axis=0, tiled=True)]
    all_gather x1 -> x0, waiting for transfers between devices: 24.3 us -> none  [on_device(): gathered = lax.all_gather(chosen, 'mp', axis=0, tiled=True)]
    all_gather x2 -> x0, blocking collectives: 21.9 us -> none  [the longest x1 13.3 us: on_device(): lax.all_gather(jnp.tile(needs, (8, 1)), 'dp', axis=0, tiled=True)]
    all_to_all x2 -> x1, blocking collectives: 49.1 us -> 28.4 us  [swap_owners(): return lax.all_to_all(buffer, 'dp', split_axis=0, concat_axis=0, tiled=True)]
    unnamed x352 -> x290, local copies, waits for them, and re-layouts: 26.8 us -> 34.8 us
    all_to_all x3 -> x5, starting transfers between devices: 13.4 us -> 21.4 us  [exchange(): return lax.all_to_all(array, axes, split_axis=0, concat_axis=0, tiled=True)]
  transfers between devices with their start and end apart: 19 -> 21, of which waited for: 8 -> 9; matrix products, arithmetic and copies ran while one was open for 19% -> 23% of each run, Pallas kernels for 24% -> 22%
where the time goes in v3:
time: 982 us; the launch traced here: 970 us
  Pallas kernels  366 us (37%)
  waiting for transfers between devices  161 us (16%)
  matrix products  140 us (14%)
  other arithmetic  104 us (11%)
  local copies, waits for them, and re-layouts  87.2 us (9%)
  starting transfers between devices  55.2 us (6%)
  blocking collectives  28.4 us (3%)
  between operations  27.4 us (3%)
    all_to_all x7, waiting for transfers between devices, swap_owners(): return lax.all_to_all(buffer, 'dp', split_axis=0, concat_axis=0, tiled=True)  125 us
    pallas_call x1, Pallas kernels, newton(): pl.pallas_call(partial(newton_kernel, groups, experts), in_specs=[vmem] *...  124 us
    pallas_call x1, Pallas kernels, dense_total(): pl.pallas_call(partial(dense_kernel, groups, experts), in_specs=[vmem, vm...  66.7 us
    dot_general x22, matrix products, dot_nn(): lax.dot_general(left, right, (((1,), (0,)), ((), ())), preferred_element_...  60.8 us
    pallas_call x3, Pallas kernels, attend_back(): pl.pallas_call(partial(attend_back_kernel, biased, causal), grid=(pairs,)...  47 us
    pallas_call x2, Pallas kernels, expert_backward(): pl.pallas_call(expert_back_kernel, grid=(blocks // per,), in_specs=[whole...  41.5 us
    dot_general x19, matrix products, dot_tn(): lax.dot_general(left, right, (((0,), (0,)), ((), ())), preferred_element_...  37.8 us
    all_to_all x5, waiting for transfers between devices, exchange(): return lax.all_to_all(array, axes, split_axis=0, concat_axis=0, tiled=True)  34.9 us
  transfers between devices with their start and end apart: 21, of which 9 were waited for; matrix products, arithmetic and copies ran while one was open for 23% of the time, Pallas kernels for 22%

profile of v3, /device:TPU:2, one launch (start us, length us, event | category | flops | bytes accessed | tf_op | source)
XLA Modules:
  0.0 970.3 jit_solution(11679176006581534507)
XLA Ops:
  37.1 11.9 %shard_map.383 = bf16[1024,768]{1,0:T(8,128)(2,1)} custom-call(s32[1024,1]{1,0:T(8,128)} %copy.202.wanted_ref, f32[4016,768]{1,0:T(8,128)} %table_ref.1), custom_call_target="tpu_custom_call" | custom-call | flops 6316621824 | bytes 12337152 | tf_op jit(solution)/shard_map/pallas_call | solution.py:976
  56.8 23.9 %all-to-all-done.6 = bf16[8,128,768]{2,1,0:T(8,128)(2,1)S(1)} async-done(((bf16[8,128,768]{2,1,0:T(8,128)(2,1)}), bf16[8,128,768]{2,1,0:T(8,128)(2,1)S(1)}, u32[]{:S(2)}, u32[]{:S(2)}) %all-to-all-start.6) | async-done | bytes 1572896 | tf_op jit(solution)/shard_map/all_to_all | solution.py:1324
  96.7 14.3 %shard_map.384 = (bf16[768,768]{1,0:T(8,128)(2,1)}, f32[12,1,768]{2,1,0:T(1,128)}) custom-call(f32[2,12]{1,0:T(2,128)} %fusion.103.refs_0_, f32[12,1,512]{2,1,0:T(1,128)} %broadcast_in_dim.105.refs_1_, bf16[768,2304]{1,0:T(8,128)(2,1)} %convolution_convert_fusion.refs_2_.refs_3_.refs_4_, bf16[768,2304]{1,0:T(8,128)(2,1)} %convolution_convert_fusion.refs_2_.refs_3_.refs_4_, ...), custom_call_target="tpu_custom_call" | custom-call | flops 1811939328 | bytes 9437184 | tf_op jit(solution)/shard_map/pallas_call | solution.py:291
  129.5 31.8 %all-to-all-done.7 = bf16[4,240,768]{2,1,0:T(8,128)(2,1)} async-done(((bf16[4,240,768]{2,1,0:T(8,128)(2,1)}), bf16[4,240,768]{2,1,0:T(8,128)(2,1)}, u32[]{:S(2)}, u32[]{:S(2)}) %all-to-all-start.7) | async-done | bytes 1474592 | tf_op jit(solution)/shard_map/all_to_all | solution.py:1230
  162.4 16.2 %shard_map.385 = (f32[4,960,768]{2,1,0:T(8,128)}, bf16[960,768]{1,0:T(8,128)(2,1)}) custom-call(bf16[960,768]{1,0:T(8,128)(2,1)} %bitcast.17.x_ref, bf16[8,2,768,384]{3,2,1,0:T(8,128)(2,1)} %bitcast.457, bf16[8,2,768,384]{3,2,1,0:T(8,128)(2,1)} %bitcast.458), custom_call_target="tpu_custom_call" | custom-call | flops 9059696640 | bytes 24182784 | tf_op jit(solution)/shard_map/pallas_call | solution.py:387
  235.3 9.9 %shard_map.387 = (bf16[256,768]{1,0:T(8,128)(2,1)}, f32[12,1,256]{2,1,0:T(1,128)}) custom-call(bf16[256,768]{1,0:T(8,128)(2,1)} %convolution_convert_fusion.20.refs_0_, bf16[768,1536]{1,0:T(8,128)(2,1)} %convolution_convert_fusion.2.refs_1_.refs_2_, bf16[768,1536]{1,0:T(8,128)(2,1)} %convolution_convert_fusion.2.refs_1_.refs_2_), custom_call_target="tpu_custom_call" | custom-call | flops 603979776 | bytes 6291456 | tf_op jit(solution)/shard_map/pallas_call | solution.py:291
  254.0 12.0 %all-to-all-done.9 = bf16[4,80,768]{2,1,0:T(8,128)(2,1)S(1)} async-done(((bf16[4,80,768]{2,1,0:T(8,128)(2,1)}), bf16[4,80,768]{2,1,0:T(8,128)(2,1)S(1)}, u32[]{:S(2)}, u32[]{:S(2)}) %all-to-all-start.9) | async-done | bytes 491552 | tf_op jit(solution)/shard_map/all_to_all | solution.py:1230
  279.2 12.5 %all-to-all-done.10 = bf16[4,80,768]{2,1,0:T(8,128)(2,1)S(1)} async-done(((bf16[4,80,768]{2,1,0:T(8,128)(2,1)}), bf16[4,80,768]{2,1,0:T(8,128)(2,1)S(1)}, u32[]{:S(2)}, u32[]{:S(2)}) %all-to-all-start.10) | async-done | bytes 491552 | tf_op jit(solution)/shard_map/all_to_all | solution.py:1230
  293.4 12.9 %shard_map.389 = bf16[8,128,768]{2,1,0:T(8,128)(2,1)S(1)} custom-call(bf16[128,768]{1,0:T(8,128)(2,1)S(1)} %convolution_convert_fusion.21.x_ref), custom_call_target="tpu_custom_call" | custom-call | bytes 20000000 | tf_op jit(solution)/shard_map/pallas_call | solution.py:927
  306.3 9.7 %fusion.10 = (f32[1024]{0:T(1024)S(1)}, f32[1024,4032]{0,1:T(8,128)S(1)}) fusion(pred[4032]{0:T(1024)(128)(4,1)S(1)} %fusion.86, bf16[1024,768]{1,0:T(8,128)(2,1)S(1)} %bitcast.356, bf16[4032,768]{1,0:T(8,128)(2,1)} %bitcast.375), kind=kOutput, calls=%fused_computation.24 | convolution fusion | flops 6354172928 | bytes 24289216 | tf_op jit(solution)/shard_map/dot_general | solution.py:78
  329.4 9.1 multiply_convert_fusion
  338.6 13.8 %multiply_convert_fusion.2 = bf16[1024,768]{1,0:T(8,128)(2,1)} fusion(bf16[1024,4032]{0,1:T(8,128)(2,1)S(1)} %multiply_convert_fusion, bf16[4032,768]{1,0:T(8,128)(2,1)} %bitcast.376), kind=kOutput, calls=%fused_computation.52 | convolution fusion | flops 6343360512 | bytes 16023552 | tf_op jit(solution)/shard_map/dot_general | solution.py:72
  357.2 11.7 %multiply_convert_fusion.1 = bf16[4032,768]{1,0:T(8,128)(2,1)} fusion(bf16[1024,4032]{0,1:T(8,128)(2,1)} %copy-done.21, bf16[1024,768]{1,0:T(8,128)(2,1)S(1)} %bitcast.357), kind=kOutput, calls=%fused_computation.23 | convolution fusion | flops 6347980800 | bytes 16023552 | tf_op jit(solution)/shard_map/dot_general | solution.py:84
  380.7 28.4 %all_to_all.108 = bf16[4,80,768]{2,1,0:T(8,128)(2,1)} all-to-all(bf16[4,80,768]{2,1,0:T(8,128)(2,1)S(1)} %bitcast.413), channel_id=1, replica_groups=mesh['dp'=4,'mp'=8] {'dp'}, dimensions={0} | all-to-all | bytes 983040 | tf_op jit(solution)/shard_map/all_to_all | solution.py:1230
  409.1 14.3 %shard_map.391 = (bf16[8,2,768,384]{3,2,1,0:T(8,128)(2,1)}, bf16[320,768]{1,0:T(8,128)(2,1)}) custom-call(bf16[320,768]{1,0:T(8,128)(2,1)} %bitcast.399, bf16[320,768]{1,0:T(8,128)(2,1)} %bitcast.412, f32[4,320,768]{2,1,0:T(8,128)} %get-tuple-element.199.pre_ref, bf16[8,2,768,384]{3,2,1,0:T(8,128)(2,1)} %bitcast.360, bf16[8,2,768,384]{3,2,1,0:T(8,128)(2,1)} %bitcast.361), custom_call_target="tpu_custom_call" | custom-call | flops 6039797760 | bytes 24772608 | tf_op jit(solution)/shard_map/pallas_call | solution.py:449
  434.7 22.4 %all-to-all-done.13 = bf16[4,80,768]{2,1,0:T(8,128)(2,1)S(1)} async-done(((bf16[4,80,768]{2,1,0:T(8,128)(2,1)}), bf16[4,80,768]{2,1,0:T(8,128)(2,1)S(1)}, u32[]{:S(2)}, u32[]{:S(2)}) %all-to-all-start.13) | async-done | bytes 491552 | tf_op jit(solution)/shard_map/all_to_all | solution.py:1230
  462.7 11.2 %shard_map.392 = (bf16[256,768]{1,0:T(8,128)(2,1)}, bf16[768,768]{1,0:T(8,128)(2,1)}, bf16[768,768]{1,0:T(8,128)(2,1)}) custom-call(bf16[256,768]{1,0:T(8,128)(2,1)} %convolution_convert_fusion.20.refs_0_, bf16[768,1536]{1,0:T(8,128)(2,1)} %convolution_convert_fusion.2.refs_1_.refs_2_, bf16[768,1536]{1,0:T(8,128)(2,1)} %convolution_convert_fusion.2.refs_1_.refs_2_, ...), custom_call_target="tpu_custom_call" | custom-call | flops 1509949440 | bytes 6291456 | tf_op jit(solution)/shard_map/pallas_call | solution.py:317
  479.6 10.6 %shard_map.393 = (bf16[256,768]{1,0:T(8,128)(2,1)}, bf16[256,768]{1,0:T(8,128)(2,1)}, bf16[256,768]{1,0:T(8,128)(2,1)}, f32[12,1,768]{2,1,0:T(1,128)}) custom-call(f32[2,12]{1,0:T(2,128)} %fusion.102.refs_0_, f32[12,1,512]{2,1,0:T(1,128)} %broadcast_in_dim.106.refs_1_, bf16[256,2304]{1,0:T(8,128)(2,1)} %convolution_convert_fusion.1.refs_2_.refs_3_.refs_4_, ...), custom_call_target="tpu_custom_call" | custom-call | flops 503316480 | bytes 3145728 | tf_op jit(solution)/shard_map/pallas_call | solution.py:317
  530.5 17.9 %all-to-all-done.14 = bf16[4,240,768]{2,1,0:T(8,128)(2,1)} async-done(((bf16[4,240,768]{2,1,0:T(8,128)(2,1)}), bf16[4,240,768]{2,1,0:T(8,128)(2,1)}, u32[]{:S(2)}, u32[]{:S(2)}) %all-to-all-start.14) | async-done | bytes 1474592 | tf_op jit(solution)/shard_map/all_to_all | solution.py:1230
  551.4 27.2 %shard_map.394 = (bf16[8,2,768,384]{3,2,1,0:T(8,128)(2,1)}, bf16[960,768]{1,0:T(8,128)(2,1)}) custom-call(bf16[960,768]{1,0:T(8,128)(2,1)} %bitcast.17.x_ref, bf16[960,768]{1,0:T(8,128)(2,1)} %bitcast.55.g_ref, f32[4,960,768]{2,1,0:T(8,128)} %get-tuple-element.211.pre_ref, bf16[8,2,768,384]{3,2,1,0:T(8,128)(2,1)} %bitcast.459, bf16[8,2,768,384]{3,2,1,0:T(8,128)(2,1)} %bitcast.460), custom_call_target="tpu_custom_call" | custom-call | flops 18119393280 | bytes 36569088 | tf_op jit(solution)/shard_map/pallas_call | solution.py:449
  590.1 28.4 %all-to-all-done.15 = bf16[4,240,768]{2,1,0:T(8,128)(2,1)} async-done(((bf16[4,240,768]{2,1,0:T(8,128)(2,1)}), bf16[4,240,768]{2,1,0:T(8,128)(2,1)}, u32[]{:S(2)}, u32[]{:S(2)}) %all-to-all-start.15) | async-done | bytes 1474592 | tf_op jit(solution)/shard_map/all_to_all | solution.py:1230
  630.7 25.3 %shard_map.395 = (bf16[768,768]{1,0:T(8,128)(2,1)}, bf16[768,768]{1,0:T(8,128)(2,1)}, bf16[768,768]{1,0:T(8,128)(2,1)}, f32[12,1,768]{2,1,0:T(1,128)}) custom-call(f32[2,12]{1,0:T(2,128)} %fusion.103.refs_0_, f32[12,1,512]{2,1,0:T(1,128)} %broadcast_in_dim.105.refs_1_, bf16[768,2304]{1,0:T(8,128)(2,1)} %convolution_convert_fusion.refs_2_.refs_3_.refs_4_, ...), custom_call_target="tpu_custom_call" | custom-call | flops 4529848320 | bytes 9437184 | tf_op jit(solution)/shard_map/pallas_call | solution.py:317
  708.3 66.7 %shard_map.396 = (f32[3,96,768]{2,1,0:T(8,128)}, f32[104,128]{1,0:T(8,128)}) custom-call(bf16[2,4,4,96,768]{4,3,2,1,0:T(8,128)(2,1)} %pad_maximum_fusion.enc_ref, bf16[8,96,768]{2,1,0:T(8,128)(2,1)} %bitcast.420, f32[104,128]{1,0:T(8,128)} %pad_bitcast_fusion.small_ref), custom_call_target="tpu_custom_call" | custom-call | bytes 200000000 | tf_op jit(solution)/shard_map/pallas_call | solution.py:1166
  804.6 124.5 %shard_map.397 = (f32[8,128]{1,0:T(8,128)}, f32[4,768,384]{2,1,0:T(8,128)}, bf16[4,768,384]{2,1,0:T(8,128)(2,1)}, bf16[4,3,96,768]{3,2,1,0:T(8,128)(2,1)}, bf16[4,3,96,768]{3,2,1,0:T(8,128)(2,1)}) custom-call(f32[8,128]{1,0:T(8,128)} %add.822.squares_ref, f32[4,768,384]{2,1,0:T(8,128)} %bitcast.461, bf16[4,768,384]{2,1,0:T(8,128)(2,1)} %bitcast.406, ...), custom_call_target="tpu_custom_call" | custom-call | flops 40768634880 | bytes 94371840 | tf_op jit(solution)/shard_map/pallas_call | solution.py:823
  (572 shorter events, 377.7 us)
Async XLA Ops:
  7.2 73.5 %all-gather.8.cloned.1.call-start = ((), (), s32[]{:S(2)}) async-start(), calls=%async_computation.21 | async-start | bytes 5308416 | tf_op jit(solution)/shard_map/all_gather | solution.py:1462
  12.1 149.2 %all-gather.14.cloned.1.call-start = ((), (), s32[]{:S(2)}) async-start(), calls=%async_computation.28 | async-start | bytes 10616832 | tf_op jit(solution)/shard_map/all_gather | solution.py:1510
  25.8 7.5 all-to-all-start.5
  48.9 31.8 %all-to-all-start.6 = ((bf16[8,128,768]{2,1,0:T(8,128)(2,1)}), bf16[8,128,768]{2,1,0:T(8,128)(2,1)S(1)}, u32[]{:S(2)}, u32[]{:S(2)}) async-start(bf16[8,128,768]{2,1,0:T(8,128)(2,1)} %bitcast.415), calls=%async_computation.6 | async-start | bytes 3145728 | tf_op jit(solution)/shard_map/all_to_all | solution.py:1324
  54.0 151.7 %all-gather.10.cloned.1.call-start = ((), (), s32[]{:S(2)}) async-start(), calls=%async_computation.22 | async-start | bytes 5308416 | tf_op jit(solution)/shard_map/all_gather | solution.py:1526
  54.1 108.1 %copy-start.114 = (s32[512]{0:T(512)}, s32[512]{0:T(512)S(1)}, u32[]{:S(2)}) copy-start(s32[512]{0:T(512)S(1)} %get-tuple-element.526) | copy-start | bytes 6148
  88.6 128.0 %copy-start.2 = (f32[1024,768]{0,1:T(8,128)}, f32[1024,768]{0,1:T(8,128)S(1)}, u32[]{:S(2)}) copy-start(f32[1024,768]{0,1:T(8,128)S(1)} %add_convert_fusion.1) | copy-start | bytes 9437188
  117.3 390.5 %copy-start.94 = (s32[768]{0:T(1024)}, s32[768]{0:T(1024)S(1)}, u32[]{:S(2)}) copy-start(s32[768]{0:T(1024)S(1)} %add_reduce_fusion) | copy-start | bytes 9220
  122.6 38.7 %all-to-all-start.7 = ((bf16[4,240,768]{2,1,0:T(8,128)(2,1)}), bf16[4,240,768]{2,1,0:T(8,128)(2,1)}, u32[]{:S(2)}, u32[]{:S(2)}) async-start(bf16[4,240,768]{2,1,0:T(8,128)(2,1)} %bitcast.419), calls=%async_computation.7 | async-start | bytes 2949120 | tf_op jit(solution)/shard_map/all_to_all | solution.py:1230
  127.6 100.0 %all-gather.12.cloned.1.call-start = ((), (), s32[]{:S(2)}) async-start(), calls=%async_computation.23 | async-start | bytes 5308416 | tf_op jit(solution)/shard_map/all_gather | solution.py:1530
  161.3 104.6 %all-gather.16.cloned.1.call-start = ((), (), s32[]{:S(2)}) async-start(), calls=%async_computation.29 | async-start | bytes 10616832 | tf_op jit(solution)/shard_map/all_gather | solution.py:1531
  178.7 40.7 %all-to-all-start.8 = ((bf16[4,240,768]{2,1,0:T(8,128)(2,1)}), bf16[4,240,768]{2,1,0:T(8,128)(2,1)}, u32[]{:S(2)}, u32[]{:S(2)}) async-start(bf16[4,240,768]{2,1,0:T(8,128)(2,1)} %bitcast.417), calls=%async_computation.8 | async-start | bytes 2949120 | tf_op jit(solution)/shard_map/all_to_all | solution.py:1230
  248.4 17.5 %all-to-all-start.9 = ((bf16[4,80,768]{2,1,0:T(8,128)(2,1)}), bf16[4,80,768]{2,1,0:T(8,128)(2,1)S(1)}, u32[]{:S(2)}, u32[]{:S(2)}) async-start(bf16[4,80,768]{2,1,0:T(8,128)(2,1)} %bitcast.34), calls=%async_computation.9 | async-start | bytes 983040 | tf_op jit(solution)/shard_map/all_to_all | solution.py:1230
  275.3 16.4 %all-to-all-start.10 = ((bf16[4,80,768]{2,1,0:T(8,128)(2,1)}), bf16[4,80,768]{2,1,0:T(8,128)(2,1)S(1)}, u32[]{:S(2)}, u32[]{:S(2)}) async-start(bf16[4,80,768]{2,1,0:T(8,128)(2,1)} %bitcast.428), calls=%async_computation.10 | async-start | bytes 983040 | tf_op jit(solution)/shard_map/all_to_all | solution.py:1230
  352.3 24.3 %all-to-all-start.11 = ((bf16[8,128,768]{2,1,0:T(8,128)(2,1)}), bf16[8,128,768]{2,1,0:T(8,128)(2,1)}, u32[]{:S(2)}, u32[]{:S(2)}) async-start(bf16[8,128,768]{2,1,0:T(8,128)(2,1)} %bitcast.416), calls=%async_computation.11 | async-start | bytes 3145728 | tf_op jit(solution)/shard_map/all_to_all | solution.py:1324
  357.0 191.4 %reduce-scatter.5.cloned.1.call-start = ((), (), s32[]{:S(2)}) async-start(), calls=%async_computation.24 | async-start | bytes 7741440 | tf_op jit(solution)/shard_map/reduce_scatter | solution.py:1598
  376.7 249.8 %reduce-scatter.7.cloned.1.call-start = ((), (), s32[]{:S(2)}) async-start(), calls=%async_computation.25 | async-start | bytes 10616832 | tf_op jit(solution)/shard_map/reduce_scatter | solution.py:1604
  423.5 33.7 %all-to-all-start.13 = ((bf16[4,80,768]{2,1,0:T(8,128)(2,1)}), bf16[4,80,768]{2,1,0:T(8,128)(2,1)S(1)}, u32[]{:S(2)}, u32[]{:S(2)}) async-start(bf16[4,80,768]{2,1,0:T(8,128)(2,1)} %bitcast.50), calls=%async_computation.13 | async-start | bytes 983040 | tf_op jit(solution)/shard_map/all_to_all | solution.py:1230
  429.3 279.0 %reduce-scatter.9.cloned.1.call-start = ((), (), s32[]{:S(2)}) async-start(), calls=%async_computation.26 | async-start | bytes 10616832 | tf_op jit(solution)/shard_map/reduce_scatter | solution.py:1423
  510.4 38.0 %all-to-all-start.14 = ((bf16[4,240,768]{2,1,0:T(8,128)(2,1)}), bf16[4,240,768]{2,1,0:T(8,128)(2,1)}, u32[]{:S(2)}, u32[]{:S(2)}) async-start(bf16[4,240,768]{2,1,0:T(8,128)(2,1)} %bitcast.54), calls=%async_computation.14 | async-start | bytes 2949120 | tf_op jit(solution)/shard_map/all_to_all | solution.py:1230
  548.4 30.2 %all-to-all-start.4 = ((s32[32,1,48]{2,1,0:T(1,128)}), s32[32,1,48]{2,1,0:T(1,128)S(1)}, u32[]{:S(2)}, u32[]{:S(2)}) async-start(s32[32,1,48]{2,1,0:T(1,128)} %all_to_all.65), calls=%async_computation.4 | async-start | bytes 32768 | tf_op jit(solution)/shard_map/all_to_all | solution.py:1324
  578.6 39.9 %all-to-all-start.15 = ((bf16[4,240,768]{2,1,0:T(8,128)(2,1)}), bf16[4,240,768]{2,1,0:T(8,128)(2,1)}, u32[]{:S(2)}, u32[]{:S(2)}) async-start(bf16[4,240,768]{2,1,0:T(8,128)(2,1)} %bitcast.418), calls=%async_computation.16 | async-start | bytes 2949120 | tf_op jit(solution)/shard_map/all_to_all | solution.py:1230
  583.2 217.0 %reduce-scatter.11.cloned.1.call-start = ((), (), s32[]{:S(2)}) async-start(), calls=%async_computation.27 | async-start | bytes 10616832 | tf_op jit(solution)/shard_map/reduce_scatter | solution.py:1628
  669.4 105.6 %all-to-all-start.16 = ((bf16[32,48,768]{2,1,0:T(8,128)(2,1)}), bf16[32,48,768]{2,1,0:T(8,128)(2,1)}, u32[]{:S(2)}, u32[]{:S(2)}) async-start(bf16[32,48,768]{2,1,0:T(8,128)(2,1)} %bitcast.405), calls=%async_computation.18 | async-start | bytes 4718592 | tf_op jit(solution)/shard_map/all_to_all | solution.py:1324
  (133 other events, 1198.2 us)
Sparse Core Ops, SparseCore 0:
  12.2 40.1 all-gather.7
  54.8 66.6 all-gather.13
  123.5 38.9 all-gather.9
  164.2 38.9 all-gather.11
  205.4 58.8 all-gather.15
  376.8 123.1 reduce-scatter.4
  503.9 80.8 reduce-scatter.6
  588.7 76.4 reduce-scatter.8
  669.2 115.2 reduce-scatter.10

commit v4 on v3

--- a/solution.py
+++ b/solution.py
@@ -1521,22 +1521,22 @@
     enc_parts = bias_parts(bias_w[0], False)
     dec_parts = bias_parts(bias_w[1], True)
     enc_mid, enc_kept = self_forward(embedded[:src_len], gains_w[0], enc_dense, enc_parts, False)
-    dec_local, late_table, enc_mid = lax.optimization_barrier((dense_local[4:8], table_w, enc_mid))
+    dec_local, late_table, enc_mid = lax.optimization_barrier((dense_local[4:12], table_w, enc_mid))
     arrived, enc_sent = moe_send(enc_mid, gains_w[1], router_w[0], hot_src, places_src, cap_src)
-    dec_dense = lax.all_gather(dec_local, "mp", axis=1, tiled=True)
-    arrived, enc_expert, cross_local, dec_expert_local = lax.optimization_barrier(
-        (arrived, enc_expert, dense_local[8:12], expert_local[1])
-    )
-    cross_dense = lax.all_gather(cross_local, "mp", axis=1, tiled=True)
-    dec_expert = lax.all_gather(dec_expert_local, "mp", axis=0, tiled=False)
+    all_dense = lax.all_gather(dec_local, "mp", axis=1, tiled=True)
+    dec_dense, cross_dense = all_dense[0:4], all_dense[4:8]
     padded = -(-piece_rows // 16) * 16
     table_low = jnp.pad(
         late_table.astype(low).reshape(experts, piece_rows, D),
         ((0, 0), (0, padded - piece_rows), (0, 0)),
     ).reshape(-1, D)
+    arrived, enc_expert, dec_expert_local, table_low = lax.optimization_barrier(
+        (arrived, enc_expert, expert_local[1], table_low)
+    )
+    dec_expert = lax.all_gather(dec_expert_local, "mp", axis=0, tiled=False)
     pre, returned = moe_expert(enc_expert, cap_src, arrived)
     dec_mid, dec_kept = self_forward(embedded[src_len:], gains_w[3], dec_dense, dec_parts, True)
-    returned, dec_mid, table_low = lax.optimization_barrier((returned, dec_mid, table_low))
+    returned, dec_mid = lax.optimization_barrier((returned, dec_mid))
     enc_out, enc_moe = moe_receive(enc_mid, places_src, arrived, pre, returned, enc_sent)
     memory_float, memory_inv = normalize(enc_out, gains_w[2])
     memory = memory_float.astype(low)

time: 982 us -> 981 us (level)
    unnamed x290 -> x293, local copies, waits for them, and re-layouts: 34.8 us -> 34.3 us
  transfers between devices with their start and end apart: 21 -> 20, of which waited for: 9 -> 10; matrix products, arithmetic and copies ran while one was open for 23% -> 23% of each run, Pallas kernels for 22% -> 22%
where the time goes in v4:
time: 981 us; the launch traced here: 969 us
  Pallas kernels  367 us (37%)
  waiting for transfers between devices  159 us (16%)
  matrix products  141 us (14%)
  other arithmetic  103 us (10%)
  local copies, waits for them, and re-layouts  86.2 us (9%)
  starting transfers between devices  54.7 us (6%)
  blocking collectives  28.4 us (3%)
  between operations  27.8 us (3%)
    all_to_all x7, waiting for transfers between devices, swap_owners(): return lax.all_to_all(buffer, 'dp', split_axis=0, concat_axis=0, tiled=True)  125 us
    pallas_call x1, Pallas kernels, newton(): pl.pallas_call(partial(newton_kernel, groups, experts), in_specs=[vmem] *...  125 us
    pallas_call x1, Pallas kernels, dense_total(): pl.pallas_call(partial(dense_kernel, groups, experts), in_specs=[vmem, vm...  66.6 us
    dot_general x22, matrix products, dot_nn(): lax.dot_general(left, right, (((1,), (0,)), ((), ())), preferred_element_...  60.8 us
    pallas_call x3, Pallas kernels, attend_back(): pl.pallas_call(partial(attend_back_kernel, biased, causal), grid=(pairs,)...  46.9 us
    pallas_call x2, Pallas kernels, expert_backward(): pl.pallas_call(expert_back_kernel, grid=(blocks // per,), in_specs=[whole...  41.6 us
    dot_general x19, matrix products, dot_tn(): lax.dot_general(left, right, (((0,), (0,)), ((), ())), preferred_element_...  37.1 us
    all_to_all x5, waiting for transfers between devices, exchange(): return lax.all_to_all(array, axes, split_axis=0, concat_axis=0, tiled=True)  34.6 us
  transfers between devices with their start and end apart: 20, of which 10 were waited for; matrix products, arithmetic and copies ran while one was open for 23% of the time, Pallas kernels for 22%

profile of v4, /device:TPU:2, one launch (start us, length us, event | category | flops | bytes accessed | tf_op | source)
XLA Modules:
  0.0 968.5 jit_solution(11343909164099221890)
XLA Ops:
  37.1 11.8 %shard_map.383 = bf16[1024,768]{1,0:T(8,128)(2,1)} custom-call(s32[1024,1]{1,0:T(8,128)} %copy.202.wanted_ref, f32[4016,768]{1,0:T(8,128)} %table_ref.1), custom_call_target="tpu_custom_call" | custom-call | flops 6316621824 | bytes 12337152 | tf_op jit(solution)/shard_map/pallas_call | solution.py:976
  58.4 23.6 %all-to-all-done.6 = bf16[8,128,768]{2,1,0:T(8,128)(2,1)} async-done(((bf16[8,128,768]{2,1,0:T(8,128)(2,1)}), bf16[8,128,768]{2,1,0:T(8,128)(2,1)}, u32[]{:S(2)}, u32[]{:S(2)}) %all-to-all-start.6) | async-done | bytes 1572896 | tf_op jit(solution)/shard_map/all_to_all | solution.py:1324
  97.4 14.3 %shard_map.384 = (bf16[768,768]{1,0:T(8,128)(2,1)}, f32[12,1,768]{2,1,0:T(1,128)}) custom-call(f32[2,12]{1,0:T(2,128)} %fusion.103.refs_0_, f32[12,1,512]{2,1,0:T(1,128)} %broadcast_in_dim.105.refs_1_, bf16[768,2304]{1,0:T(8,128)(2,1)} %convolution_convert_fusion.refs_2_.refs_3_.refs_4_, bf16[768,2304]{1,0:T(8,128)(2,1)} %convolution_convert_fusion.refs_2_.refs_3_.refs_4_, ...), custom_call_target="tpu_custom_call" | custom-call | flops 1811939328 | bytes 9437184 | tf_op jit(solution)/shard_map/pallas_call | solution.py:291
  147.8 14.0 %all-to-all-done.7 = bf16[4,240,768]{2,1,0:T(8,128)(2,1)} async-done(((bf16[4,240,768]{2,1,0:T(8,128)(2,1)}), bf16[4,240,768]{2,1,0:T(8,128)(2,1)}, u32[]{:S(2)}, u32[]{:S(2)}) %all-to-all-start.7) | async-done | bytes 1474592 | tf_op jit(solution)/shard_map/all_to_all | solution.py:1230
  162.4 16.3 %shard_map.385 = (f32[4,960,768]{2,1,0:T(8,128)}, bf16[960,768]{1,0:T(8,128)(2,1)}) custom-call(bf16[960,768]{1,0:T(8,128)(2,1)} %bitcast.17.x_ref, bf16[8,2,768,384]{3,2,1,0:T(8,128)(2,1)} %bitcast.450, bf16[8,2,768,384]{3,2,1,0:T(8,128)(2,1)} %bitcast.451), custom_call_target="tpu_custom_call" | custom-call | flops 9059696640 | bytes 24182784 | tf_op jit(solution)/shard_map/pallas_call | solution.py:387
  201.3 16.2 %all-to-all-done.8 = bf16[4,240,768]{2,1,0:T(8,128)(2,1)} async-done(((bf16[4,240,768]{2,1,0:T(8,128)(2,1)}), bf16[4,240,768]{2,1,0:T(8,128)(2,1)}, u32[]{:S(2)}, u32[]{:S(2)}) %all-to-all-start.8) | async-done | bytes 1474592 | tf_op jit(solution)/shard_map/all_to_all | solution.py:1230
  233.1 9.6 shard_map.387
  249.6 13.3 %all-to-all-done.9 = bf16[4,80,768]{2,1,0:T(8,128)(2,1)S(1)} async-done(((bf16[4,80,768]{2,1,0:T(8,128)(2,1)}), bf16[4,80,768]{2,1,0:T(8,128)(2,1)S(1)}, u32[]{:S(2)}, u32[]{:S(2)}) %all-to-all-start.9) | async-done | bytes 491552 | tf_op jit(solution)/shard_map/all_to_all | solution.py:1230
  276.3 12.8 %all-to-all-done.10 = bf16[4,80,768]{2,1,0:T(8,128)(2,1)S(1)} async-done(((bf16[4,80,768]{2,1,0:T(8,128)(2,1)}), bf16[4,80,768]{2,1,0:T(8,128)(2,1)S(1)}, u32[]{:S(2)}, u32[]{:S(2)}) %all-to-all-start.10) | async-done | bytes 491552 | tf_op jit(solution)/shard_map/all_to_all | solution.py:1230
  290.8 13.3 %shard_map.389 = bf16[8,128,768]{2,1,0:T(8,128)(2,1)S(1)} custom-call(bf16[128,768]{1,0:T(8,128)(2,1)S(1)} %convolution_convert_fusion.21.x_ref), custom_call_target="tpu_custom_call" | custom-call | bytes 20000000 | tf_op jit(solution)/shard_map/pallas_call | solution.py:927
  304.2 9.7 %fusion.10 = (f32[1024]{0:T(1024)S(1)}, f32[1024,4032]{0,1:T(8,128)S(1)}) fusion(pred[4032]{0:T(1024)(128)(4,1)S(1)} %fusion.86, bf16[1024,768]{1,0:T(8,128)(2,1)S(1)} %bitcast.352, bf16[4032,768]{1,0:T(8,128)(2,1)} %bitcast.374), kind=kOutput, calls=%fused_computation.24 | convolution fusion | flops 6354172928 | bytes 24289216 | tf_op jit(solution)/shard_map/dot_general | solution.py:78
  336.4 13.8 %multiply_convert_fusion.2 = bf16[1024,768]{1,0:T(8,128)(2,1)} fusion(bf16[1024,4032]{0,1:T(8,128)(2,1)S(1)} %multiply_convert_fusion, bf16[4032,768]{1,0:T(8,128)(2,1)} %bitcast.375), kind=kOutput, calls=%fused_computation.52 | convolution fusion | flops 6343360512 | bytes 16023552 | tf_op jit(solution)/shard_map/dot_general | solution.py:72
  355.2 11.7 %multiply_convert_fusion.1 = bf16[4032,768]{1,0:T(8,128)(2,1)} fusion(bf16[1024,4032]{0,1:T(8,128)(2,1)} %copy-done.21, bf16[1024,768]{1,0:T(8,128)(2,1)S(1)} %bitcast.353), kind=kOutput, calls=%fused_computation.23 | convolution fusion | flops 6347980800 | bytes 16023552 | tf_op jit(solution)/shard_map/dot_general | solution.py:84
  378.7 28.4 %all_to_all.108 = bf16[4,80,768]{2,1,0:T(8,128)(2,1)} all-to-all(bf16[4,80,768]{2,1,0:T(8,128)(2,1)S(1)} %bitcast.407), channel_id=1, replica_groups=mesh['dp'=4,'mp'=8] {'dp'}, dimensions={0} | all-to-all | bytes 983040 | tf_op jit(solution)/shard_map/all_to_all | solution.py:1230
  407.1 14.4 %shard_map.391 = (bf16[8,2,768,384]{3,2,1,0:T(8,128)(2,1)}, bf16[320,768]{1,0:T(8,128)(2,1)}) custom-call(bf16[320,768]{1,0:T(8,128)(2,1)} %bitcast.397, bf16[320,768]{1,0:T(8,128)(2,1)} %bitcast.406, f32[4,320,768]{2,1,0:T(8,128)} %get-tuple-element.197.pre_ref, bf16[8,2,768,384]{3,2,1,0:T(8,128)(2,1)} %bitcast.356, bf16[8,2,768,384]{3,2,1,0:T(8,128)(2,1)} %bitcast.357), custom_call_target="tpu_custom_call" | custom-call | flops 6039797760 | bytes 24772608 | tf_op jit(solution)/shard_map/pallas_call | solution.py:449
  432.7 22.5 %all-to-all-done.13 = bf16[4,80,768]{2,1,0:T(8,128)(2,1)S(1)} async-done(((bf16[4,80,768]{2,1,0:T(8,128)(2,1)}), bf16[4,80,768]{2,1,0:T(8,128)(2,1)S(1)}, u32[]{:S(2)}, u32[]{:S(2)}) %all-to-all-start.13) | async-done | bytes 491552 | tf_op jit(solution)/shard_map/all_to_all | solution.py:1230
  460.7 11.1 %shard_map.392 = (bf16[256,768]{1,0:T(8,128)(2,1)}, bf16[768,768]{1,0:T(8,128)(2,1)}, bf16[768,768]{1,0:T(8,128)(2,1)}) custom-call(bf16[256,768]{1,0:T(8,128)(2,1)} %convolution_convert_fusion.20.refs_0_, bf16[768,1536]{1,0:T(8,128)(2,1)} %convolution_convert_fusion.2.refs_1_.refs_2_, bf16[768,1536]{1,0:T(8,128)(2,1)} %convolution_convert_fusion.2.refs_1_.refs_2_, ...), custom_call_target="tpu_custom_call" | custom-call | flops 1509949440 | bytes 6291456 | tf_op jit(solution)/shard_map/pallas_call | solution.py:317
  477.7 10.6 %shard_map.393 = (bf16[256,768]{1,0:T(8,128)(2,1)}, bf16[256,768]{1,0:T(8,128)(2,1)}, bf16[256,768]{1,0:T(8,128)(2,1)}, f32[12,1,768]{2,1,0:T(1,128)}) custom-call(f32[2,12]{1,0:T(2,128)} %fusion.102.refs_0_, f32[12,1,512]{2,1,0:T(1,128)} %broadcast_in_dim.106.refs_1_, bf16[256,2304]{1,0:T(8,128)(2,1)} %convolution_convert_fusion.1.refs_2_.refs_3_.refs_4_, ...), custom_call_target="tpu_custom_call" | custom-call | flops 503316480 | bytes 3145728 | tf_op jit(solution)/shard_map/pallas_call | solution.py:317
  528.8 17.6 %all-to-all-done.14 = bf16[4,240,768]{2,1,0:T(8,128)(2,1)} async-done(((bf16[4,240,768]{2,1,0:T(8,128)(2,1)}), bf16[4,240,768]{2,1,0:T(8,128)(2,1)}, u32[]{:S(2)}, u32[]{:S(2)}) %all-to-all-start.14) | async-done | bytes 1474592 | tf_op jit(solution)/shard_map/all_to_all | solution.py:1230
  549.4 27.2 %shard_map.394 = (bf16[8,2,768,384]{3,2,1,0:T(8,128)(2,1)}, bf16[960,768]{1,0:T(8,128)(2,1)}) custom-call(bf16[960,768]{1,0:T(8,128)(2,1)} %bitcast.17.x_ref, bf16[960,768]{1,0:T(8,128)(2,1)} %bitcast.55.g_ref, f32[4,960,768]{2,1,0:T(8,128)} %get-tuple-element.209.pre_ref, bf16[8,2,768,384]{3,2,1,0:T(8,128)(2,1)} %bitcast.452, bf16[8,2,768,384]{3,2,1,0:T(8,128)(2,1)} %bitcast.453), custom_call_target="tpu_custom_call" | custom-call | flops 18119393280 | bytes 36569088 | tf_op jit(solution)/shard_map/pallas_call | solution.py:449
  588.1 28.4 %all-to-all-done.15 = bf16[4,240,768]{2,1,0:T(8,128)(2,1)} async-done(((bf16[4,240,768]{2,1,0:T(8,128)(2,1)}), bf16[4,240,768]{2,1,0:T(8,128)(2,1)}, u32[]{:S(2)}, u32[]{:S(2)}) %all-to-all-start.15) | async-done | bytes 1474592 | tf_op jit(solution)/shard_map/all_to_all | solution.py:1230
  628.7 25.2 %shard_map.395 = (bf16[768,768]{1,0:T(8,128)(2,1)}, bf16[768,768]{1,0:T(8,128)(2,1)}, bf16[768,768]{1,0:T(8,128)(2,1)}, f32[12,1,768]{2,1,0:T(1,128)}) custom-call(f32[2,12]{1,0:T(2,128)} %fusion.103.refs_0_, f32[12,1,512]{2,1,0:T(1,128)} %broadcast_in_dim.105.refs_1_, bf16[768,2304]{1,0:T(8,128)(2,1)} %convolution_convert_fusion.refs_2_.refs_3_.refs_4_, ...), custom_call_target="tpu_custom_call" | custom-call | flops 4529848320 | bytes 9437184 | tf_op jit(solution)/shard_map/pallas_call | solution.py:317
  706.2 66.6 %shard_map.396 = (f32[3,96,768]{2,1,0:T(8,128)}, f32[104,128]{1,0:T(8,128)}) custom-call(bf16[2,4,4,96,768]{4,3,2,1,0:T(8,128)(2,1)} %pad_maximum_fusion.enc_ref, bf16[8,96,768]{2,1,0:T(8,128)(2,1)} %bitcast.413, f32[104,128]{1,0:T(8,128)} %pad_bitcast_fusion.small_ref), custom_call_target="tpu_custom_call" | custom-call | bytes 200000000 | tf_op jit(solution)/shard_map/pallas_call | solution.py:1166
  802.4 124.6 %shard_map.397 = (f32[8,128]{1,0:T(8,128)}, f32[4,768,384]{2,1,0:T(8,128)}, bf16[4,768,384]{2,1,0:T(8,128)(2,1)}, bf16[4,3,96,768]{3,2,1,0:T(8,128)(2,1)}, bf16[4,3,96,768]{3,2,1,0:T(8,128)(2,1)}) custom-call(f32[8,128]{1,0:T(8,128)} %add.822.squares_ref, f32[4,768,384]{2,1,0:T(8,128)} %bitcast.454, bf16[4,768,384]{2,1,0:T(8,128)(2,1)} %bitcast.401, ...), custom_call_target="tpu_custom_call" | custom-call | flops 40768634880 | bytes 94371840 | tf_op jit(solution)/shard_map/pallas_call | solution.py:823
  (573 shorter events, 384.9 us)
Async XLA Ops:
  7.2 74.8 %all-gather.7.cloned.1.call-start = ((), (), s32[]{:S(2)}) async-start(), calls=%async_computation.21 | async-start | bytes 5308416 | tf_op jit(solution)/shard_map/all_gather | solution.py:1462
  12.3 149.5 %all-gather.11.cloned.1.call-start = ((), (), s32[]{:S(2)}) async-start(), calls=%async_computation.27 | async-start | bytes 10616832 | tf_op jit(solution)/shard_map/all_gather | solution.py:1510
  26.1 7.5 all-to-all-start.5
  49.0 33.1 %all-to-all-start.6 = ((bf16[8,128,768]{2,1,0:T(8,128)(2,1)}), bf16[8,128,768]{2,1,0:T(8,128)(2,1)}, u32[]{:S(2)}, u32[]{:S(2)}) async-start(bf16[8,128,768]{2,1,0:T(8,128)(2,1)} %bitcast.408), calls=%async_computation.6 | async-start | bytes 3145728 | tf_op jit(solution)/shard_map/all_to_all | solution.py:1324
  54.8 132.8 %all-gather.9.cloned.1.call-start = ((), (), s32[]{:S(2)}) async-start(), calls=%async_computation.22 | async-start | bytes 10616832 | tf_op jit(solution)/shard_map/all_gather | solution.py:1526
  55.4 106.7 %copy-start.115 = (s32[512]{0:T(512)}, s32[512]{0:T(512)S(1)}, u32[]{:S(2)}) copy-start(s32[512]{0:T(512)S(1)} %get-tuple-element.521) | copy-start | bytes 6148
  89.4 109.1 %copy-start.2 = (f32[1024,768]{0,1:T(8,128)}, f32[1024,768]{0,1:T(8,128)S(1)}, u32[]{:S(2)}) copy-start(f32[1024,768]{0,1:T(8,128)S(1)} %add_convert_fusion.1) | copy-start | bytes 9437188
  118.0 387.8 %copy-start.95 = (s32[768]{0:T(1024)}, s32[768]{0:T(1024)S(1)}, u32[]{:S(2)}) copy-start(s32[768]{0:T(1024)S(1)} %add_reduce_fusion) | copy-start | bytes 9220
  123.4 38.4 %all-to-all-start.7 = ((bf16[4,240,768]{2,1,0:T(8,128)(2,1)}), bf16[4,240,768]{2,1,0:T(8,128)(2,1)}, u32[]{:S(2)}, u32[]{:S(2)}) async-start(bf16[4,240,768]{2,1,0:T(8,128)(2,1)} %bitcast.412), calls=%async_computation.7 | async-start | bytes 2949120 | tf_op jit(solution)/shard_map/all_to_all | solution.py:1230
  128.2 134.6 %all-gather.13.cloned.1.call-start = ((), (), s32[]{:S(2)}) async-start(), calls=%async_computation.28 | async-start | bytes 10616832 | tf_op jit(solution)/shard_map/all_gather | solution.py:1536
  178.7 38.7 %all-to-all-start.8 = ((bf16[4,240,768]{2,1,0:T(8,128)(2,1)}), bf16[4,240,768]{2,1,0:T(8,128)(2,1)}, u32[]{:S(2)}, u32[]{:S(2)}) async-start(bf16[4,240,768]{2,1,0:T(8,128)(2,1)} %bitcast.411), calls=%async_computation.8 | async-start | bytes 2949120 | tf_op jit(solution)/shard_map/all_to_all | solution.py:1230
  246.1 16.8 %all-to-all-start.9 = ((bf16[4,80,768]{2,1,0:T(8,128)(2,1)}), bf16[4,80,768]{2,1,0:T(8,128)(2,1)S(1)}, u32[]{:S(2)}, u32[]{:S(2)}) async-start(bf16[4,80,768]{2,1,0:T(8,128)(2,1)} %bitcast.34), calls=%async_computation.9 | async-start | bytes 983040 | tf_op jit(solution)/shard_map/all_to_all | solution.py:1230
  272.3 16.9 %all-to-all-start.10 = ((bf16[4,80,768]{2,1,0:T(8,128)(2,1)}), bf16[4,80,768]{2,1,0:T(8,128)(2,1)S(1)}, u32[]{:S(2)}, u32[]{:S(2)}) async-start(bf16[4,80,768]{2,1,0:T(8,128)(2,1)} %bitcast.421), calls=%async_computation.10 | async-start | bytes 983040 | tf_op jit(solution)/shard_map/all_to_all | solution.py:1230
  350.2 24.4 %all-to-all-start.11 = ((bf16[8,128,768]{2,1,0:T(8,128)(2,1)}), bf16[8,128,768]{2,1,0:T(8,128)(2,1)}, u32[]{:S(2)}, u32[]{:S(2)}) async-start(bf16[8,128,768]{2,1,0:T(8,128)(2,1)} %bitcast.409), calls=%async_computation.11 | async-start | bytes 3145728 | tf_op jit(solution)/shard_map/all_to_all | solution.py:1324
  355.0 191.4 %reduce-scatter.5.cloned.1.call-start = ((), (), s32[]{:S(2)}) async-start(), calls=%async_computation.23 | async-start | bytes 7741440 | tf_op jit(solution)/shard_map/reduce_scatter | solution.py:1598
  374.7 249.7 %reduce-scatter.7.cloned.1.call-start = ((), (), s32[]{:S(2)}) async-start(), calls=%async_computation.24 | async-start | bytes 10616832 | tf_op jit(solution)/shard_map/reduce_scatter | solution.py:1604
  421.5 33.7 %all-to-all-start.13 = ((bf16[4,80,768]{2,1,0:T(8,128)(2,1)}), bf16[4,80,768]{2,1,0:T(8,128)(2,1)S(1)}, u32[]{:S(2)}, u32[]{:S(2)}) async-start(bf16[4,80,768]{2,1,0:T(8,128)(2,1)} %bitcast.50), calls=%async_computation.13 | async-start | bytes 983040 | tf_op jit(solution)/shard_map/all_to_all | solution.py:1230
  427.4 278.8 %reduce-scatter.9.cloned.1.call-start = ((), (), s32[]{:S(2)}) async-start(), calls=%async_computation.25 | async-start | bytes 10616832 | tf_op jit(solution)/shard_map/reduce_scatter | solution.py:1423
  508.5 37.9 %all-to-all-start.14 = ((bf16[4,240,768]{2,1,0:T(8,128)(2,1)}), bf16[4,240,768]{2,1,0:T(8,128)(2,1)}, u32[]{:S(2)}, u32[]{:S(2)}) async-start(bf16[4,240,768]{2,1,0:T(8,128)(2,1)} %bitcast.54), calls=%async_computation.14 | async-start | bytes 2949120 | tf_op jit(solution)/shard_map/all_to_all | solution.py:1230
  546.4 30.2 %all-to-all-start.4 = ((s32[32,1,48]{2,1,0:T(1,128)}), s32[32,1,48]{2,1,0:T(1,128)S(1)}, u32[]{:S(2)}, u32[]{:S(2)}) async-start(s32[32,1,48]{2,1,0:T(1,128)} %all_to_all.65), calls=%async_computation.4 | async-start | bytes 32768 | tf_op jit(solution)/shard_map/all_to_all | solution.py:1324
  576.6 39.9 %all-to-all-start.15 = ((bf16[4,240,768]{2,1,0:T(8,128)(2,1)}), bf16[4,240,768]{2,1,0:T(8,128)(2,1)}, u32[]{:S(2)}, u32[]{:S(2)}) async-start(bf16[4,240,768]{2,1,0:T(8,128)(2,1)} %bitcast.410), calls=%async_computation.16 | async-start | bytes 2949120 | tf_op jit(solution)/shard_map/all_to_all | solution.py:1230
  581.2 216.9 %reduce-scatter.11.cloned.1.call-start = ((), (), s32[]{:S(2)}) async-start(), calls=%async_computation.26 | async-start | bytes 10616832 | tf_op jit(solution)/shard_map/reduce_scatter | solution.py:1628
  667.3 105.5 %all-to-all-start.16 = ((bf16[32,48,768]{2,1,0:T(8,128)(2,1)}), bf16[32,48,768]{2,1,0:T(8,128)(2,1)}, u32[]{:S(2)}, u32[]{:S(2)}) async-start(bf16[32,48,768]{2,1,0:T(8,128)(2,1)} %bitcast.400), calls=%async_computation.18 | async-start | bytes 4718592 | tf_op jit(solution)/shard_map/all_to_all | solution.py:1324
  706.2 81.6 %copy-start.85 = (s32[1536]{0:T(1024)S(1)}, s32[1536]{0:T(1024)}, u32[]{:S(2)}) copy-start(s32[1536]{0:T(1024)} %reshape.1056) | copy-start | bytes 18436
  (134 other events, 1086.9 us)
Sparse Core Ops, SparseCore 0:
  12.4 40.1 all-gather.6
  55.0 67.2 all-gather.10
  124.8 58.8 all-gather.8
  186.0 58.8 all-gather.12
  374.8 123.1 reduce-scatter.4
  501.8 80.8 reduce-scatter.6
  586.6 76.4 reduce-scatter.8
  667.0 115.3 reduce-scatter.10
